TPU v7x, 256 devices: a whole 4x4x8 slice. The times are simulated.
256 devices in a mesh: row: 32 (over y, z_lo, core), col: 8 (over x, z_hi).
Axes of the slice: x: 4, y: 4, z: 8 (z_hi: 2, z_lo: 4; z = z_hi * 4 + z_lo), core: 2. Of those that a mesh axis runs over, the one named last changes fastest.
Arguments:
- features: bfloat16 [131072, 128], P(('col', 'row')), may hold values from -6 to 6
- weight: bfloat16 [128, 172], replicated, may hold values from -0.5 to 0.5
- labels: int32 [131072], P(('row', 'col')), may hold values from -43 to 171
- tile_rows: int32 [32, 8, 256], P('row', 'col'), may hold values from 0 to 31, as said below
- tile_cols: int32 [32, 8, 256], P('row', 'col'), may hold values from 0 to 127
- tile_count: int32 [32, 8], P('row', 'col'), may hold values from 1 to 256, as said below
- tile_vals: bfloat16 [32, 8, 256, 128, 128], P('row', 'col'), may hold values from -0.07470703 to 0.07470703
Outputs:
- logits: float32 [131072, 172], P(('row', 'col'))
- weight_grad: float32 [128, 172], replicated
Inputs may be any that keep to these rules, and one draw needn't show every extreme that they name: `tile_rows`: within one device the used slots name distinct tiles; unused slots are ignored. `tile_count`: counts differ between devices; in every draw some device uses all 256 slots.
All inputs are finite; a program needn't handle non-finite values.
Results may differ from a plain program's by a relative error of at most 0.0029.
Values may be sent and summed in bfloat16 or wider, within the bound.
No kernel may reach another device: no remote copies, remote signals or barrier semaphores. Data moves between devices by JAX's collectives and lax.ppermute only.
A program may use at most 128 MiB of HBM per device.

v0:
```python
import jax
import jax.numpy as jnp
from jax import lax
from jax.sharding import PartitionSpec as P


def aggregate(table, gather_idx, scatter_idx, vals, count, out_tiles, transpose):
    blk = min(32, vals.shape[0])
    classes = table.shape[-1]
    nblk = (count + blk - 1) // blk

    def step(b, acc):
        start = (b * blk).astype(jnp.int32)
        piece = lax.dynamic_slice_in_dim(vals, start, blk, 0)
        gidx = lax.dynamic_slice_in_dim(gather_idx, start, blk, 0)
        sidx = lax.dynamic_slice_in_dim(scatter_idx, start, blk, 0)
        sel = table[gidx]
        if transpose:
            prod = jnp.einsum("tji,tjc->tic", piece, sel, preferred_element_type=jnp.float32)
        else:
            prod = jnp.einsum("tij,tjc->tic", piece, sel, preferred_element_type=jnp.float32)
        valid = (start + jnp.arange(blk, dtype=jnp.int32) < count).astype(jnp.float32)
        return acc.at[sidx].add(prod * valid[:, None, None])

    init = jnp.zeros((out_tiles, table.shape[1], classes), jnp.float32)
    return lax.fori_loop(0, nblk, step, init)


def split_product(inputs, grads):
    upper = lax.optimization_barrier(grads.astype(jnp.bfloat16))
    lower = (grads - upper.astype(jnp.float32)).astype(jnp.bfloat16)
    first = jnp.einsum("nf,nc->fc", inputs, upper, preferred_element_type=jnp.float32)
    second = jnp.einsum("nf,nc->fc", inputs, lower, preferred_element_type=jnp.float32)
    return first + second


def local(features, weight, labels, tile_rows, tile_cols, tile_count, tile_vals):
    classes = weight.shape[1]
    tile = tile_vals.shape[-1]
    slots = tile_vals.shape[2]
    vals = tile_vals.reshape(slots, tile, tile)
    rows_idx = tile_rows.reshape(slots)
    cols_idx = tile_cols.reshape(slots)
    count = tile_count.reshape(())
    row_tiles = lax.axis_size("col") * features.shape[0] // tile
    nodes = features.shape[0] * lax.axis_size("row") * lax.axis_size("col")
    local_xw = jnp.dot(features, weight, preferred_element_type=jnp.float32).astype(jnp.bfloat16)
    xw_full = lax.all_gather(local_xw, "row", axis=0, tiled=True)
    table = xw_full.reshape(-1, tile, classes)
    col_tiles = table.shape[0]
    partial_value = aggregate(table, cols_idx, rows_idx, vals, count, row_tiles, False)
    logits = lax.psum_scatter(
        partial_value.reshape(-1, classes), "col", scatter_dimension=0, tiled=True
    )
    onehot = (labels[:, None] == jnp.arange(classes, dtype=jnp.int32)[None, :]).astype(jnp.float32)
    residual_grad = jnp.where(labels[:, None] >= 0, logits - onehot, 0.0).astype(jnp.bfloat16)
    loss_full = lax.all_gather(residual_grad, "col", axis=0, tiled=True)
    back = aggregate(
        loss_full.reshape(-1, tile, classes), rows_idx, cols_idx, vals, count, col_tiles, True
    )
    projected_grad = lax.psum_scatter(
        back.reshape(-1, classes), "row", scatter_dimension=0, tiled=True
    )
    local_grad = split_product(features, projected_grad)
    total_grad = lax.psum(local_grad, ("row", "col"))
    weight_grad = total_grad / jnp.sqrt(jnp.float32(nodes))
    return (logits, weight_grad)


def solution(mesh):
    placed = (
        P(("col", "row"), None),
        P(),
        P(("row", "col")),
        P("row", "col", None),
        P("row", "col", None),
        P("row", "col"),
        P("row", "col", None, None, None),
    )
    return jax.shard_map(
        local, mesh=mesh, in_specs=placed, out_specs=(P(("row", "col"), None), P()), check_vma=False
    )
```

profile of v0, /device:TPU:1, one launch (start us, length us, event | category | flops | bytes accessed | tf_op | source)
XLA Modules:
  0.0 958.3 jit_solution(16695922642993902090)
XLA Ops:
  10.5 70.0 %all-gather.3.cloned.1.call-done = bf16[16384,172]{0,1:T(8,128)(2,1)} async-done(((bf16[512,172]{0,1:T(8,128)(2,1)}), bf16[16384,172]{0,1:T(8,128)(2,1)}) %all-gather.3.cloned.1.call-update) | async-done | bytes 5636112 | tf_op jit(solution)/shard_map/all_gather | solution.py:48
  80.5 9.9 %copy.22 = bf16[16384,172]{1,0:T(8,128)(2,1)} copy(bf16[16384,172]{0,1:T(8,128)(2,1)} %all-gather.3.cloned.1.call-done) | data formatting | bytes 11272192 | tf_op jit(solution)/shard_map/while | solution.py:26
  92.2 64.4 %while.20 = (s32[]{:T(128)}, f32[32,128,172]{1,2,0:T(8,128)}, s32[]{:T(128)}, s32[256]{0:T(256)S(1)}, bf16[256,128,128]{2,1,0:T(8,128)(2,1)}, /*index=5*/s32[256...) while((s32[]{:T(128)}, f32[32,128,172]{1,2,0:T(8,128)}, ...), condition=%wide.region_2.3_spmd, body=%wide.region_0.2_spmd.sunk | while | flops 181765408 | bytes 17241396 | solution.py:26
  93.0 5.5 gather_fusion
  101.2 7.1 scatter_fusion
  109.0 5.5 gather_fusion
  117.3 7.1 scatter_fusion
  125.1 5.5 gather_fusion
  133.4 7.1 scatter_fusion
  141.2 5.5 gather_fusion
  149.5 7.1 scatter_fusion
  159.6 4.0 copy.24
  164.3 162.4 %reduce-scatter.3.cloned.1.call-done = f32[512,172]{0,1:T(8,128)} async-done(((f32[4096,172]{0,1:T(8,128)}), f32[512,172]{0,1:T(8,128)}) %reduce-scatter.3.cloned.1.call-update) | async-done | bytes 352272 | tf_op jit(solution)/shard_map/reduce_scatter | solution.py:52
  328.5 63.9 %all-gather.5.cloned.1.call-done = bf16[4096,172]{0,1:T(8,128)(2,1)} async-done(((bf16[512,172]{0,1:T(8,128)(2,1)}), bf16[4096,172]{0,1:T(8,128)(2,1)}) %all-gather.5.cloned.1.call-update) | async-done | bytes 1409040 | tf_op jit(solution)/shard_map/all_gather | solution.py:57
  392.4 3.8 copy.23
  396.2 5.1 broadcast_in_dim.36
  401.3 57.3 %while.21 = (s32[]{:T(128)}, f32[128,128,172]{1,2,0:T(8,128)}, s32[]{:T(128)}, s32[256]{0:T(256)S(1)}, bf16[256,128,128]{2,1,0:T(8,128)(2,1)}, /*index=5*/s32[25...) while((s32[]{:T(128)}, f32[128,128,172]{1,2,0:T(8,128)}, ...), condition=%wide.region_6.7_spmd, body=%wide.region_4.6_spmd.sunk | while | flops 181765408 | bytes 17241396 | solution.py:26
  402.0 3.6 gather_fusion.1
  405.6 2.8 convolution_multiply_fusion.5
  408.4 7.1 scatter_fusion.1
  416.3 3.6 gather_fusion.1
  422.7 7.3 scatter_fusion.1
  430.7 3.6 gather_fusion.1
  434.3 2.8 convolution_multiply_fusion.5
  437.1 7.2 scatter_fusion.1
  445.0 3.6 gather_fusion.1
  451.4 7.2 scatter_fusion.1
  458.6 7.9 copy.28
  466.5 5.2 pad.3
  471.7 18.7 %copy.25 = f32[22,8,128,128]{3,1,2,0:T(8,128)} copy(f32[22,8,128,128]{3,2,1,0:T(8,128)} %bitcast.35) | data formatting | bytes 23068672
  490.4 212.4 %reduce-scatter.5.cloned.1.call-done = f32[512,172]{0,1:T(8,128)} async-done(((f32[16384,172]{0,1:T(8,128)}), f32[512,172]{0,1:T(8,128)}) %reduce-scatter.5.cloned.1.call-update) | async-done | bytes 352272 | tf_op jit(solution)/shard_map/reduce_scatter | solution.py:61
  705.9 244.3 %all-reduce.2.cloned.1.call-done = f32[128,172]{0,1:T(8,128)} async-done(((f32[128,172]{0,1:T(8,128)}), f32[128,172]{0,1:T(8,128)}) %all-reduce.2.cloned.1.call-update) | async-done | bytes 88080 | tf_op jit(solution)/shard_map/psum | solution.py:65
  (58 shorter events, 37.0 us)
Async XLA Ops:
  7.2 0.9 copy-start
  7.2 73.3 %all-gather.3.cloned.1.call-start = ((), (), s32[]{:S(2)}) async-start(), calls=%async_computation.2 | async-start | bytes 5947392 | tf_op jit(solution)/shard_map/all_gather | solution.py:48
  9.8 316.9 %reduce-scatter.3.cloned.1.call-start = ((), (), s32[]{:S(2)}) async-start(), calls=%async_computation.3 | async-start | bytes 3244032 | tf_op jit(solution)/shard_map/reduce_scatter | solution.py:52
  90.4 1.9 copy-start.1
  90.4 1.9 copy-start.2
  163.6 0.7 copy-start.3
  163.6 228.8 %all-gather.5.cloned.1.call-start = ((), (), s32[]{:S(2)}) async-start(), calls=%async_computation.4 | async-start | bytes 1622016 | tf_op jit(solution)/shard_map/all_gather | solution.py:57
  328.4 374.4 %reduce-scatter.5.cloned.1.call-start = ((), (), s32[]{:S(2)}) async-start(), calls=%async_computation.5 | async-start | bytes 11894784 | tf_op jit(solution)/shard_map/reduce_scatter | solution.py:61
  490.4 459.8 %all-reduce.2.cloned.1.call-start = ((), (), s32[]{:S(2)}) async-start(), calls=%async_computation.6 | async-start | bytes 180224 | tf_op jit(solution)/shard_map/psum | solution.py:65
Sparse Core Ops, SparseCore 0:
  10.5 69.9 all-gather.2
  163.7 162.9 reduce-scatter.2
  329.2 63.1 all-gather.4
  490.5 212.3 reduce-scatter.4
  708.8 241.3 all-reduce.1
where the time goes:
time: 962 us; the launch traced here: 958 us
  waiting for transfers between devices  753 us (78%)
  local copies, waits for them, and re-layouts  97.1 us (10%)
  other arithmetic  67.3 us (7%)
  matrix products  25.9 us (3%)
  between operations  14.5 us (2%)
    psum x1, waiting for transfers between devices, local(): total_grad = lax.psum(local_grad, ('row', 'col'))  244 us
    reduce_scatter x1, waiting for transfers between devices, local(): lax.psum_scatter(back.reshape(-1, classes), 'row', scatter_dimension=0, t...  212 us
    reduce_scatter x1, waiting for transfers between devices, local(): lax.psum_scatter(partial_value.reshape(-1, classes), 'col', scatter_dimen...  162 us
    all_gather x1, waiting for transfers between devices, local(): xw_full = lax.all_gather(local_xw, 'row', axis=0, tiled=True)  70 us
    all_gather x1, waiting for transfers between devices, local(): loss_full = lax.all_gather(residual_grad, 'col', axis=0, tiled=True)  63.9 us
    scatter-add x8, other arithmetic, step(): return acc.at[sidx].add(prod * valid[:, None, None])  57.2 us
    gather x8, local copies, waits for them, and re-layouts, step(): sel = table[gidx]  36.2 us
    unnamed x12, local copies, waits for them, and re-layouts  29.6 us
  transfers between devices with their start and end apart: 5, of which 5 were waited for; matrix products, arithmetic and copies ran while one was open for 0% of the time, Pallas kernels for 0%

commit v1 on v0

v1 whole, which is shorter than its diff:
```python
import math

import jax
import jax.numpy as jnp
from jax import lax
from jax.experimental import pallas as pl
from jax.experimental.pallas import tpu as pltpu
from jax.sharding import Mesh, PartitionSpec as P

AXES = ("y", "zl", "core", "x", "zh")
SIZES = (4, 4, 2, 4, 2)
ROW = AXES[:3]
COL = AXES[3:]
GROUP = 8
CHUNK = 32


def shift(value, axes, step):
    n = lax.axis_size(axes)
    return lax.ppermute(value, axes, [(i, (i + step) % n) for i in range(n)])


def aggregate_kernel(count_ref, rows_ref, places_ref, mine_ref, other_ref, vals_ref, out_ref,
                     table, vals, acc, prods, sem_table, sem_vals):
    tile = vals.shape[-1]
    half = mine_ref.shape[0]
    chunks = vals.shape[0] // CHUNK
    count = count_ref[0]

    def vals_copy(k):
        part = pl.ds(k * CHUNK, CHUNK)
        return pltpu.make_async_copy(vals_ref.at[part], vals.at[part], sem_vals.at[k])

    table_copies = [
        pltpu.make_async_copy(mine_ref, table.at[pl.ds(0, half)], sem_table.at[0]),
        pltpu.make_async_copy(other_ref, table.at[pl.ds(half, half)], sem_table.at[1]),
    ]
    vals_copy(0).start()
    for copy in table_copies:
        copy.start()
    for k in range(1, chunks):
        @pl.when(k * CHUNK < count)
        def _(k=k):
            vals_copy(k).start()
    acc[...] = jnp.zeros_like(acc)
    for copy in table_copies:
        copy.wait()

    def group(g, _):
        slots = [g * GROUP + i for i in range(GROUP)]
        for i, s in enumerate(slots):
            place = pl.multiple_of(places_ref[s], tile)
            prods[i] = jnp.dot(vals[s], table[pl.ds(place, tile), :], preferred_element_type=jnp.float32)
        for i, s in enumerate(slots):
            row = pl.multiple_of(rows_ref[s], tile)
            acc[pl.ds(row, tile), :] += prods[i]
        return 0

    for k in range(chunks):
        @pl.when(k * CHUNK < count)
        def _(k=k):
            vals_copy(k).wait()
            left = jnp.minimum(count - k * CHUNK, CHUNK)
            lax.fori_loop(k * (CHUNK // GROUP), k * (CHUNK // GROUP) + (left + GROUP - 1) // GROUP, group, 0)
    out_ref[...] = acc[pl.ds(0, out_ref.shape[0]), :].astype(out_ref.dtype)


def aggregate(count, rows, places, mine, other, vals, out_rows):
    slots, tile, _ = vals.shape
    feat = mine.shape[1]
    smem = pl.BlockSpec(memory_space=pltpu.SMEM)
    hbm = pl.BlockSpec(memory_space=pl.ANY)
    return pl.pallas_call(
        aggregate_kernel,
        out_shape=jax.ShapeDtypeStruct((out_rows, feat), jnp.bfloat16),
        in_specs=[smem, smem, smem, hbm, hbm, hbm],
        out_specs=pl.BlockSpec(memory_space=pltpu.VMEM),
        scratch_shapes=[
            pltpu.VMEM((2 * mine.shape[0], feat), jnp.bfloat16),
            pltpu.VMEM((slots, tile, tile), jnp.bfloat16),
            pltpu.VMEM((out_rows + tile, feat), jnp.float32),
            pltpu.VMEM((GROUP, tile, feat), jnp.float32),
            pltpu.SemaphoreType.DMA((2,)),
            pltpu.SemaphoreType.DMA((slots // CHUNK,)),
        ],
        compiler_params=pltpu.CompilerParams(vmem_limit_bytes=32 * 2**20),
        cost_estimate=pl.CostEstimate(flops=2 * slots * tile * tile * feat, bytes_accessed=14 * 2**20, transcendentals=0),
        name="aggregate",
    )(count, rows, places, mine, other, vals)


def head_kernel(scale, own_ref, far_ref, weight_ref, labels_ref, logits_ref, grad_ref):
    total = far_ref[...].astype(jnp.float32)
    for k in range(own_ref.shape[0]):
        total += own_ref[k].astype(jnp.float32)
    upper = total.astype(jnp.bfloat16)
    lower = (total - upper.astype(jnp.float32)).astype(jnp.bfloat16)
    weight = weight_ref[...]
    logits = jnp.dot(upper, weight, preferred_element_type=jnp.float32)
    logits += jnp.dot(lower, weight, preferred_element_type=jnp.float32)
    logits_ref[...] = logits
    labels = labels_ref[...]
    classes = lax.broadcasted_iota(jnp.int32, logits.shape, 1)
    residual = logits - (labels == classes).astype(jnp.float32)
    residual = jnp.where(labels >= 0, residual, 0.0).astype(jnp.bfloat16)
    over_nodes = (((0,), (0,)), ((), ()))
    grad = lax.dot_general(upper, residual, over_nodes, preferred_element_type=jnp.float32)
    grad += lax.dot_general(lower, residual, over_nodes, preferred_element_type=jnp.float32)
    grad_ref[...] = grad * scale


def head(own, far, weight, labels, scale):
    rows, feat = far.shape
    classes = weight.shape[1]
    vmem = pl.BlockSpec(memory_space=pltpu.VMEM)
    return pl.pallas_call(
        lambda *refs: head_kernel(scale, *refs),
        out_shape=(
            jax.ShapeDtypeStruct((rows, classes), jnp.float32),
            jax.ShapeDtypeStruct((feat, classes), jnp.float32),
        ),
        in_specs=[vmem] * 4,
        out_specs=(vmem, vmem),
        compiler_params=pltpu.CompilerParams(vmem_limit_bytes=32 * 2**20),
        name="head",
    )(own, far, weight, labels)


def gather_features(features):
    plane = ("y", "zl")
    pieces = [features] + [shift(features, plane, -k) for k in range(1, lax.axis_size(plane))]
    mine = jnp.concatenate(pieces, 0)
    return mine, shift(mine, "core", 1)


def places_of(tile_cols, per_device, tile):
    device, part = tile_cols // per_device, tile_cols % per_device
    chip, core = device // 2, device % 2
    away = (chip - lax.axis_index(("y", "zl"))) % 16
    other = (core != lax.axis_index("core")).astype(jnp.int32)
    return (((other * 16 + away) * per_device) + part) * tile


def sum_everywhere(grad):
    core = lax.axis_index("core")
    half = grad.shape[0] // 2
    keep = lax.dynamic_slice_in_dim(grad, core * half, half, 0)
    give = lax.dynamic_slice_in_dim(grad, (1 - core) * half, half, 0)
    total = keep + shift(give, "core", 1)
    for axis in ("y", "zl", "x"):
        total = total + shift(total, axis, 1) + shift(total, axis, 2) + shift(total, axis, 3)
    total = total + shift(total, "zh", 1)
    rest = shift(total, "core", 1)
    return jnp.where(core == 0, jnp.concatenate([total, rest], 0), jnp.concatenate([rest, total], 0))


def local(features, weight, labels, tile_rows, tile_cols, tile_count, tile_vals):
    tile = tile_vals.shape[-1]
    slots = tile_vals.shape[2]
    vals = tile_vals.reshape(slots, tile, tile)
    count = tile_count.reshape(1)
    rows_out = features.shape[0] * lax.axis_size(COL)
    nodes = features.shape[0] * lax.axis_size(AXES)
    used = jnp.arange(slots, dtype=jnp.int32) < count
    rows = jnp.where(used, tile_rows.reshape(slots) * tile, rows_out)
    places = places_of(tile_cols.reshape(slots), features.shape[0] // tile, tile)

    mine, other = gather_features(features)
    part = aggregate(count, rows, places, mine, other, vals, rows_out)

    n_x = lax.axis_size("x")
    block = lax.all_to_all(part, "x", 0, 0, tiled=True).reshape(n_x, rows_out // n_x, -1)
    zh = lax.axis_index("zh")
    half = rows_out // n_x // 2
    give = lax.dynamic_slice_in_dim(block, (1 - zh) * half, half, 1)
    own = lax.dynamic_slice_in_dim(block, zh * half, half, 1)
    give = jnp.sum(give.astype(jnp.float32), 0).astype(jnp.bfloat16)
    far = shift(give, "zh", 1)
    logits, grad = head(own, far, weight, labels[:, None], 1.0 / math.sqrt(nodes))
    return logits, sum_everywhere(grad)


def solution(mesh):
    fine = Mesh(mesh.devices.reshape(SIZES), AXES)
    placed = (
        P(COL + ROW, None),
        P(),
        P(AXES),
        P(ROW, COL, None),
        P(ROW, COL, None),
        P(ROW, COL),
        P(ROW, COL, None, None, None),
    )
    return jax.shard_map(
        local, mesh=fine, in_specs=placed, out_specs=(P(AXES, None), P()), check_vma=False
    )
```

time: 962 us -> 140 us (0.15)
  waiting for transfers between devices: 753 us -> 49.2 us
  local copies, waits for them, and re-layouts: 97.1 us -> 6.55 us
  starting transfers between devices: 0.2 us -> 75.1 us
  other arithmetic: 67.3 us -> 0.19 us
  matrix products: 25.9 us -> 0 us
  between operations: 14.5 us -> 1.63 us
    reduce_scatter x2 -> x0, waiting for transfers between devices: 375 us -> none  [the longest x1 212 us: local(): lax.psum_scatter(back.reshape(-1, classes), 'row', scatter_dimension=0, t...]
    psum x1 -> x0, waiting for transfers between devices: 244 us -> none  [local(): total_grad = lax.psum(local_grad, ('row', 'col'))]
    all_gather x2 -> x0, waiting for transfers between devices: 134 us -> none  [the longest x1 70 us: local(): xw_full = lax.all_gather(local_xw, 'row', axis=0, tiled=True)]
    ppermute x0 -> x29, starting transfers between devices: none -> 68.3 us  [shift(): return lax.ppermute(value, axes, [(i, (i + step) % n) for i in range(n)])]
    scatter-add x8 -> x0, other arithmetic: 57.2 us -> none  [step(): return acc.at[sidx].add(prod * valid[:, None, None])]
    ppermute x0 -> x29, waiting for transfers between devices: none -> 36.7 us  [shift(): return lax.ppermute(value, axes, [(i, (i + step) % n) for i in range(n)])]
    gather x8 -> x0, local copies, waits for them, and re-layouts: 36.2 us -> none  [step(): sel = table[gidx]]
    dot_general x11 -> x0, matrix products: 25.9 us -> none  [the longest x4 11.2 us: step(): jnp.einsum('tji,tjc->tic', piece, sel, preferred_element_type=jnp.float32)]
  transfers between devices with their start and end apart: 5 -> 30, of which waited for: 5 -> 14; matrix products, arithmetic and copies ran while one was open for 0% -> 2% of each run, Pallas kernels for 0% -> 0%
where the time goes in v1:
time: 140 us
  starting transfers between devices  75.1 us (54%)
  waiting for transfers between devices  49.2 us (35%)
  Pallas kernels  7.46 us (5%)
  local copies, waits for them, and re-layouts  6.55 us (5%)
  between operations  1.63 us (1%)
    ppermute x29, starting transfers between devices, shift(): return lax.ppermute(value, axes, [(i, (i + step) % n) for i in range(n)])  68.3 us
    ppermute x29, waiting for transfers between devices, shift(): return lax.ppermute(value, axes, [(i, (i + step) % n) for i in range(n)])  36.7 us
    all_to_all x1, waiting for transfers between devices, local(): lax.all_to_all(part, 'x', 0, 0, tiled=True)  12.5 us
    all_to_all x1, starting transfers between devices, local(): lax.all_to_all(part, 'x', 0, 0, tiled=True)  6.89 us
    pallas_call x1, Pallas kernels, aggregate(): pl.pallas_call(aggregate_kernel, out_shape=jax.ShapeDtypeStruct((out_rows...  6.89 us
    unnamed x30, local copies, waits for them, and re-layouts  6.38 us
  transfers between devices with their start and end apart: 30, of which 14 were waited for; matrix products, arithmetic and copies ran while one was open for 2% of the time, Pallas kernels for 0%

profile of v1, /device:TPU:1, one launch (start us, length us, event | category | flops | bytes accessed | tf_op | source)
XLA Modules:
  0.0 140.2 jit_solution(7216586093784441227)
XLA Ops:
  0.7 7.7 %collective-permute-start = (bf16[512,128]{1,0:T(8,128)(2,1)}, bf16[512,128]{1,0:T(8,128)(2,1)S(1)}, u32[]{:S(2)}, u32[]{:S(2)}) collective-permute-start(bf16[512,128]{1,0:T(8,128)(2,1)} %param.7), channel_id=1, source_target_pairs={{0,240},{16,0},{32,16},{48,32},{64,48},{80,64},{96,80},{112,96},{1... | collective-permute-start | bytes 393224 | tf_op jit(solution)/shard_map/ppermute | solution.py:20
  9.1 2.8 %collective-permute-start.4 = (bf16[512,128]{1,0:T(8,128)(2,1)}, bf16[512,128]{1,0:T(8,128)(2,1)S(1)}, u32[]{:S(2)}, u32[]{:S(2)}) collective-permute-start(bf16[512,128]{1,0:T(8,128)(2,1)} %param.7), channel_id=1, source_target_pairs={{0,176},{16,192},{32,208},{48,224},{64,240},{80,0},{96,16},{112,32... | collective-permute-start | bytes 393224 | tf_op jit(solution)/shard_map/ppermute | solution.py:20
  12.8 3.3 %collective-permute-start.5 = (bf16[512,128]{1,0:T(8,128)(2,1)}, bf16[512,128]{1,0:T(8,128)(2,1)S(1)}, u32[]{:S(2)}, u32[]{:S(2)}) collective-permute-start(bf16[512,128]{1,0:T(8,128)(2,1)} %param.7), channel_id=1, source_target_pairs={{0,160},{16,176},{32,192},{48,208},{64,224},{80,240},{96,0},{112,1... | collective-permute-start | bytes 393224 | tf_op jit(solution)/shard_map/ppermute | solution.py:20
  16.1 3.5 %collective-permute-done.1 = bf16[512,128]{1,0:T(8,128)(2,1)S(1)} collective-permute-done((bf16[512,128]{1,0:T(8,128)(2,1)}, bf16[512,128]{1,0:T(8,128)(2,1)S(1)}, u32[]{:S(2)}, u32[]{:S(2)}) %collective-permute-start.1) | collective-permute-done | bytes 131104 | tf_op jit(solution)/shard_map/ppermute | solution.py:20
  20.2 6.9 %collective-permute-start.8 = (bf16[512,128]{1,0:T(8,128)(2,1)}, bf16[512,128]{1,0:T(8,128)(2,1)S(1)}, u32[]{:S(2)}, u32[]{:S(2)}) collective-permute-start(bf16[512,128]{1,0:T(8,128)(2,1)} %param.7), channel_id=1, source_target_pairs={{0,112},{16,128},{32,144},{48,160},{64,176},{80,192},{96,208},{112... | collective-permute-start | bytes 393224 | tf_op jit(solution)/shard_map/ppermute | solution.py:20
  27.1 3.0 %collective-permute-start.9 = (bf16[512,128]{1,0:T(8,128)(2,1)}, bf16[512,128]{1,0:T(8,128)(2,1)S(1)}, u32[]{:S(2)}, u32[]{:S(2)}) collective-permute-start(bf16[512,128]{1,0:T(8,128)(2,1)} %param.7), channel_id=1, source_target_pairs={{0,96},{16,112},{32,128},{48,144},{64,160},{80,176},{96,192},{112,... | collective-permute-start | bytes 393224 | tf_op jit(solution)/shard_map/ppermute | solution.py:20
  30.1 2.0 %collective-permute-start.10 = (bf16[512,128]{1,0:T(8,128)(2,1)}, bf16[512,128]{1,0:T(8,128)(2,1)S(1)}, u32[]{:S(2)}, u32[]{:S(2)}) collective-permute-start(bf16[512,128]{1,0:T(8,128)(2,1)} %param.7), channel_id=1, source_target_pairs={{0,80},{16,96},{32,112},{48,128},{64,144},{80,160},{96,176},{112,1... | collective-permute-start | bytes 393224 | tf_op jit(solution)/shard_map/ppermute | solution.py:20
  32.2 5.8 %collective-permute-start.11 = (bf16[512,128]{1,0:T(8,128)(2,1)}, bf16[512,128]{1,0:T(8,128)(2,1)S(1)}, u32[]{:S(2)}, u32[]{:S(2)}) collective-permute-start(bf16[512,128]{1,0:T(8,128)(2,1)} %param.7), channel_id=1, source_target_pairs={{0,64},{16,80},{32,96},{48,112},{64,128},{80,144},{96,160},{112,17... | collective-permute-start | bytes 393224 | tf_op jit(solution)/shard_map/ppermute | solution.py:20
  38.0 3.4 %collective-permute-start.12 = (bf16[512,128]{1,0:T(8,128)(2,1)S(1)}, bf16[512,128]{1,0:T(8,128)(2,1)S(1)}, u32[]{:S(2)}, u32[]{:S(2)}) collective-permute-start(bf16[512,128]{1,0:T(8,128)(2,1)S(1)} %copy-done.1), channel_id=1, source_target_pairs={{0,48},{16,64},{32,80},{48,96},{64,112},{80,128},{96,144},{112,160... | collective-permute-start | bytes 393224 | tf_op jit(solution)/shard_map/ppermute | solution.py:20
  41.6 4.6 %collective-permute-start.14 = (bf16[512,128]{1,0:T(8,128)(2,1)S(1)}, bf16[512,128]{1,0:T(8,128)(2,1)S(1)}, u32[]{:S(2)}, u32[]{:S(2)}) collective-permute-start(bf16[512,128]{1,0:T(8,128)(2,1)S(1)} %copy-done.1), channel_id=1, source_target_pairs={{0,16},{16,32},{32,48},{48,64},{64,80},{80,96},{96,112},{112,128},... | collective-permute-start | bytes 393224 | tf_op jit(solution)/shard_map/ppermute | solution.py:20
  46.3 2.7 %collective-permute-done.12 = bf16[512,128]{1,0:T(8,128)(2,1)S(1)} collective-permute-done((bf16[512,128]{1,0:T(8,128)(2,1)S(1)}, bf16[512,128]{1,0:T(8,128)(2,1)S(1)}, u32[]{:S(2)}, u32[]{:S(2)}) %collective-permute-start.12) | collective-permute-done | bytes 131104 | tf_op jit(solution)/shard_map/ppermute | solution.py:20
  49.0 8.4 %collective-permute-done.13 = bf16[512,128]{1,0:T(8,128)(2,1)S(1)} collective-permute-done((bf16[512,128]{1,0:T(8,128)(2,1)S(1)}, bf16[512,128]{1,0:T(8,128)(2,1)S(1)}, u32[]{:S(2)}, u32[]{:S(2)}) %collective-permute-start.13) | collective-permute-done | bytes 131104 | tf_op jit(solution)/shard_map/ppermute | solution.py:20
  57.5 1.2 collective-permute-start.15
  59.4 3.2 %collective-permute-done.15.other_ref = bf16[8192,128]{1,0:T(8,128)(2,1)} collective-permute-done((bf16[8192,128]{1,0:T(8,128)(2,1)S(1)}, bf16[8192,128]{1,0:T(8,128)(2,1)}, u32[]{:S(2)}, u32[]{:S(2)}) %collective-permute-start.15) | collective-permute-done | bytes 2097184 | tf_op jit(solution)/shard_map/ppermute | solution.py:20
  62.6 3.4 %copy-done = bf16[1,1,256,128,128]{4,3,2,1,0:T(8,128)(2,1)S(1)} copy-done((bf16[1,1,256,128,128]{4,3,2,1,0:T(8,128)(2,1)S(1)}, bf16[1,1,256,128,128]{4,3,2,1,0:T(8,128)(2,1)}, u32[]{:S(2)}) %copy-start) | copy-done | bytes 8388632
  66.0 6.9 %aggregate.1 = bf16[4096,128]{1,0:T(8,128)(2,1)} custom-call(s32[1]{0:T(128)} %bitcast.7.count_ref, s32[256]{0:T(256)S(1)} %get-tuple-element.12.rows_ref, s32[256]{0:T(256)S(1)} %get-tuple-element.13.places_ref, bf16[8192,128]{1,0:T(8,128)(2,1)S(1)} %constant_dynamic-update-slice_fusion.mine_ref, bf16[8192,128]{1,0:T(8,128)(2,1)} %collective-permute-done.15.other_ref, ...), custom_call_target="tpu_custom_call" | custom-call | flops 1073741824 | bytes 14680064 | tf_op jit(solution)/shard_map/aggregate/pallas_call | solution.py:73
  72.9 6.9 %all-to-all-start = ((bf16[4,1024,128]{2,1,0:T(8,128)(2,1)}), bf16[4,1024,128]{2,1,0:T(8,128)(2,1)S(1)}, u32[]{:S(2)}, u32[]{:S(2)}) async-start(bf16[4,1024,128]{2,1,0:T(8,128)(2,1)} %bitcast.5), calls=%async_computation | async-start | bytes 2097152 | tf_op jit(solution)/shard_map/all_to_all | solution.py:172
  79.8 12.5 %all-to-all-done = bf16[4,1024,128]{2,1,0:T(8,128)(2,1)S(1)} async-done(((bf16[4,1024,128]{2,1,0:T(8,128)(2,1)}), bf16[4,1024,128]{2,1,0:T(8,128)(2,1)S(1)}, u32[]{:S(2)}, u32[]{:S(2)}) %all-to-all-start) | async-done | bytes 1048608 | tf_op jit(solution)/shard_map/all_to_all | solution.py:172
  92.4 2.8 %collective-permute-start.16 = (bf16[512,128]{1,0:T(8,128)(2,1)S(1)}, bf16[512,128]{1,0:T(8,128)(2,1)S(1)}, u32[]{:S(2)}, u32[]{:S(2)}) collective-permute-start(bf16[512,128]{1,0:T(8,128)(2,1)S(1)} %get-tuple-element.10), channel_id=1, source_target_pairs={{0,1},{1,0},{2,3},{3,2},{4,5},{5,4},{6,7},{7,6},{8,9},{9,8},{10,11... | collective-permute-start | bytes 393224 | tf_op jit(solution)/shard_map/ppermute | solution.py:20
  95.5 6.8 %collective-permute-done.16.refs_1_ = bf16[512,128]{1,0:T(8,128)(2,1)S(1)} collective-permute-done((bf16[512,128]{1,0:T(8,128)(2,1)S(1)}, bf16[512,128]{1,0:T(8,128)(2,1)S(1)}, u32[]{:S(2)}, u32[]{:S(2)}) %collective-permute-start.16) | collective-permute-done | bytes 131104 | tf_op jit(solution)/shard_map/ppermute | solution.py:20
  103.0 1.2 collective-permute-done.17
  104.3 3.7 %collective-permute-start.18 = (f32[64,172]{1,0:T(8,128)S(1)}, f32[64,172]{1,0:T(8,128)S(1)}, u32[]{:S(2)}, u32[]{:S(2)}) collective-permute-start(f32[64,172]{1,0:T(8,128)S(1)} %dynamic-slice_add_fusion), channel_id=1, source_target_pairs={{0,64},{64,128},{128,192},{192,0},{1,65},{65,129},{129,193},{193,1... | collective-permute-start | bytes 132104 | tf_op jit(solution)/shard_map/ppermute | solution.py:20
  108.0 1.1 collective-permute-start.19
  109.1 2.0 %collective-permute-start.20 = (f32[64,172]{1,0:T(8,128)S(1)}, f32[64,172]{1,0:T(8,128)S(1)}, u32[]{:S(2)}, u32[]{:S(2)}) collective-permute-start(f32[64,172]{1,0:T(8,128)S(1)} %dynamic-slice_add_fusion), channel_id=1, source_target_pairs={{0,192},{64,0},{128,64},{192,128},{1,193},{65,1},{129,65},{193,129... | collective-permute-start | bytes 132104 | tf_op jit(solution)/shard_map/ppermute | solution.py:20
  111.1 1.6 %collective-permute-done.19 = f32[64,172]{1,0:T(8,128)S(1)} collective-permute-done((f32[64,172]{1,0:T(8,128)S(1)}, f32[64,172]{1,0:T(8,128)S(1)}, u32[]{:S(2)}, u32[]{:S(2)}) %collective-permute-start.19) | collective-permute-done | bytes 44064 | tf_op jit(solution)/shard_map/ppermute | solution.py:20
  113.3 1.6 %collective-permute-start.22 = (f32[64,172]{1,0:T(8,128)S(1)}, f32[64,172]{1,0:T(8,128)S(1)}, u32[]{:S(2)}, u32[]{:S(2)}) collective-permute-start(f32[64,172]{1,0:T(8,128)S(1)} %add_add_fusion.2), channel_id=1, source_target_pairs={{0,32},{16,48},{32,0},{48,16},{1,33},{17,49},{33,1},{49,17},{2,34}... | collective-permute-start | bytes 132104 | tf_op jit(solution)/shard_map/ppermute | solution.py:20
  114.9 2.3 %collective-permute-start.23 = (f32[64,172]{1,0:T(8,128)S(1)}, f32[64,172]{1,0:T(8,128)S(1)}, u32[]{:S(2)}, u32[]{:S(2)}) collective-permute-start(f32[64,172]{1,0:T(8,128)S(1)} %add_add_fusion.2), channel_id=1, source_target_pairs={{0,48},{16,0},{32,16},{48,32},{1,49},{17,1},{33,17},{49,33},{2,50}... | collective-permute-start | bytes 132104 | tf_op jit(solution)/shard_map/ppermute | solution.py:20
  119.5 1.8 %collective-permute-start.25 = (f32[64,172]{1,0:T(8,128)S(1)}, f32[64,172]{1,0:T(8,128)S(1)}, u32[]{:S(2)}, u32[]{:S(2)}) collective-permute-start(f32[64,172]{1,0:T(8,128)S(1)} %add_add_fusion.1), channel_id=1, source_target_pairs={{0,4},{2,6},{4,0},{6,2},{1,5},{3,7},{5,1},{7,3},{8,12},{10,14},{12... | collective-permute-start | bytes 132104 | tf_op jit(solution)/shard_map/ppermute | solution.py:20
  122.0 2.2 %collective-permute-done.24 = f32[64,172]{1,0:T(8,128)S(1)} collective-permute-done((f32[64,172]{1,0:T(8,128)S(1)}, f32[64,172]{1,0:T(8,128)S(1)}, u32[]{:S(2)}, u32[]{:S(2)}) %collective-permute-start.24) | collective-permute-done | bytes 44064 | tf_op jit(solution)/shard_map/ppermute | solution.py:20
  124.8 2.5 %collective-permute-start.27 = (f32[64,172]{1,0:T(8,128)S(1)}, f32[64,172]{1,0:T(8,128)S(1)}, u32[]{:S(2)}, u32[]{:S(2)}) collective-permute-start(f32[64,172]{1,0:T(8,128)S(1)} %add_add_fusion), channel_id=1, source_target_pairs={{0,1},{1,0},{2,3},{3,2},{4,5},{5,4},{6,7},{7,6},{8,9},{9,8},{10,11... | collective-permute-start | bytes 132104 | tf_op jit(solution)/shard_map/ppermute | solution.py:20
  127.3 4.6 %collective-permute-done.27 = f32[64,172]{1,0:T(8,128)S(1)} collective-permute-done((f32[64,172]{1,0:T(8,128)S(1)}, f32[64,172]{1,0:T(8,128)S(1)}, u32[]{:S(2)}, u32[]{:S(2)}) %collective-permute-start.27) | collective-permute-done | bytes 44064 | tf_op jit(solution)/shard_map/ppermute | solution.py:20
  131.9 6.6 %collective-permute-start.28 = (f32[64,172]{1,0:T(8,128)S(1)}, f32[64,172]{1,0:T(8,128)S(1)}, u32[]{:S(2)}, u32[]{:S(2)}) collective-permute-start(f32[64,172]{1,0:T(8,128)S(1)} %add.90), channel_id=1, source_target_pairs={{0,8},{8,0},{1,9},{9,1},{2,10},{10,2},{3,11},{11,3},{4,12},{12,4},... | collective-permute-start | bytes 132104 | tf_op jit(solution)/shard_map/ppermute | solution.py:20
  (72 shorter events, 9.7 us)
Async XLA Ops:
  0.6 58.7 %copy-start.4 = (s32[1,1,256]{2,1,0:T(1,128)S(1)}, s32[1,1,256]{2,1,0:T(1,128)}, u32[]{:S(2)}) copy-start(s32[1,1,256]{2,1,0:T(1,128)} %param.10) | copy-start | bytes 3076
  0.7 58.7 %copy-start.5 = (s32[1,1,256]{2,1,0:T(1,128)S(1)}, s32[1,1,256]{2,1,0:T(1,128)}, u32[]{:S(2)}) copy-start(s32[1,1,256]{2,1,0:T(1,128)} %param.11) | copy-start | bytes 3076
  0.7 12.2 %collective-permute-start = (bf16[512,128]{1,0:T(8,128)(2,1)}, bf16[512,128]{1,0:T(8,128)(2,1)S(1)}, u32[]{:S(2)}, u32[]{:S(2)}) collective-permute-start(bf16[512,128]{1,0:T(8,128)(2,1)} %param.7), channel_id=1, source_target_pairs={{0,240},{16,0},{32,16},{48,32},{64,48},{80,64},{96,80},{112,96},{1... | collective-permute-start | bytes 393224 | tf_op jit(solution)/shard_map/ppermute | solution.py:20
  8.4 11.2 %collective-permute-start.1 = (bf16[512,128]{1,0:T(8,128)(2,1)}, bf16[512,128]{1,0:T(8,128)(2,1)S(1)}, u32[]{:S(2)}, u32[]{:S(2)}) collective-permute-start(bf16[512,128]{1,0:T(8,128)(2,1)} %param.7), channel_id=1, source_target_pairs={{0,224},{16,240},{32,0},{48,16},{64,32},{80,48},{96,64},{112,80},{... | collective-permute-start | bytes 393224 | tf_op jit(solution)/shard_map/ppermute | solution.py:20
  8.4 11.2 %collective-permute-start.2 = (bf16[512,128]{1,0:T(8,128)(2,1)}, bf16[512,128]{1,0:T(8,128)(2,1)S(1)}, u32[]{:S(2)}, u32[]{:S(2)}) collective-permute-start(bf16[512,128]{1,0:T(8,128)(2,1)} %param.7), channel_id=1, source_target_pairs={{0,208},{16,224},{32,240},{48,0},{64,16},{80,32},{96,48},{112,64},... | collective-permute-start | bytes 393224 | tf_op jit(solution)/shard_map/ppermute | solution.py:20
  8.9 11.3 %collective-permute-start.3 = (bf16[512,128]{1,0:T(8,128)(2,1)}, bf16[512,128]{1,0:T(8,128)(2,1)S(1)}, u32[]{:S(2)}, u32[]{:S(2)}) collective-permute-start(bf16[512,128]{1,0:T(8,128)(2,1)} %param.7), channel_id=1, source_target_pairs={{0,192},{16,208},{32,224},{48,240},{64,0},{80,16},{96,32},{112,48}... | collective-permute-start | bytes 393224 | tf_op jit(solution)/shard_map/ppermute | solution.py:20
  9.1 18.0 %collective-permute-start.4 = (bf16[512,128]{1,0:T(8,128)(2,1)}, bf16[512,128]{1,0:T(8,128)(2,1)S(1)}, u32[]{:S(2)}, u32[]{:S(2)}) collective-permute-start(bf16[512,128]{1,0:T(8,128)(2,1)} %param.7), channel_id=1, source_target_pairs={{0,176},{16,192},{32,208},{48,224},{64,240},{80,0},{96,16},{112,32... | collective-permute-start | bytes 393224 | tf_op jit(solution)/shard_map/ppermute | solution.py:20
  12.8 17.3 %collective-permute-start.5 = (bf16[512,128]{1,0:T(8,128)(2,1)}, bf16[512,128]{1,0:T(8,128)(2,1)S(1)}, u32[]{:S(2)}, u32[]{:S(2)}) collective-permute-start(bf16[512,128]{1,0:T(8,128)(2,1)} %param.7), channel_id=1, source_target_pairs={{0,160},{16,176},{32,192},{48,208},{64,224},{80,240},{96,0},{112,1... | collective-permute-start | bytes 393224 | tf_op jit(solution)/shard_map/ppermute | solution.py:20
  19.6 12.6 %collective-permute-start.6 = (bf16[512,128]{1,0:T(8,128)(2,1)}, bf16[512,128]{1,0:T(8,128)(2,1)S(1)}, u32[]{:S(2)}, u32[]{:S(2)}) collective-permute-start(bf16[512,128]{1,0:T(8,128)(2,1)} %param.7), channel_id=1, source_target_pairs={{0,144},{16,160},{32,176},{48,192},{64,208},{80,224},{96,240},{112... | collective-permute-start | bytes 393224 | tf_op jit(solution)/shard_map/ppermute | solution.py:20
  19.6 18.4 %collective-permute-start.7 = (bf16[512,128]{1,0:T(8,128)(2,1)}, bf16[512,128]{1,0:T(8,128)(2,1)S(1)}, u32[]{:S(2)}, u32[]{:S(2)}) collective-permute-start(bf16[512,128]{1,0:T(8,128)(2,1)} %param.7), channel_id=1, source_target_pairs={{0,128},{16,144},{32,160},{48,176},{64,192},{80,208},{96,224},{112... | collective-permute-start | bytes 393224 | tf_op jit(solution)/shard_map/ppermute | solution.py:20
  20.2 21.2 %collective-permute-start.8 = (bf16[512,128]{1,0:T(8,128)(2,1)}, bf16[512,128]{1,0:T(8,128)(2,1)S(1)}, u32[]{:S(2)}, u32[]{:S(2)}) collective-permute-start(bf16[512,128]{1,0:T(8,128)(2,1)} %param.7), channel_id=1, source_target_pairs={{0,112},{16,128},{32,144},{48,160},{64,176},{80,192},{96,208},{112... | collective-permute-start | bytes 393224 | tf_op jit(solution)/shard_map/ppermute | solution.py:20
  27.1 14.4 %collective-permute-start.9 = (bf16[512,128]{1,0:T(8,128)(2,1)}, bf16[512,128]{1,0:T(8,128)(2,1)S(1)}, u32[]{:S(2)}, u32[]{:S(2)}) collective-permute-start(bf16[512,128]{1,0:T(8,128)(2,1)} %param.7), channel_id=1, source_target_pairs={{0,96},{16,112},{32,128},{48,144},{64,160},{80,176},{96,192},{112,... | collective-permute-start | bytes 393224 | tf_op jit(solution)/shard_map/ppermute | solution.py:20
  30.1 16.1 %collective-permute-start.10 = (bf16[512,128]{1,0:T(8,128)(2,1)}, bf16[512,128]{1,0:T(8,128)(2,1)S(1)}, u32[]{:S(2)}, u32[]{:S(2)}) collective-permute-start(bf16[512,128]{1,0:T(8,128)(2,1)} %param.7), channel_id=1, source_target_pairs={{0,80},{16,96},{32,112},{48,128},{64,144},{80,160},{96,176},{112,1... | collective-permute-start | bytes 393224 | tf_op jit(solution)/shard_map/ppermute | solution.py:20
  32.2 14.1 %collective-permute-start.11 = (bf16[512,128]{1,0:T(8,128)(2,1)}, bf16[512,128]{1,0:T(8,128)(2,1)S(1)}, u32[]{:S(2)}, u32[]{:S(2)}) collective-permute-start(bf16[512,128]{1,0:T(8,128)(2,1)} %param.7), channel_id=1, source_target_pairs={{0,64},{16,80},{32,96},{48,112},{64,128},{80,144},{96,160},{112,17... | collective-permute-start | bytes 393224 | tf_op jit(solution)/shard_map/ppermute | solution.py:20
  38.0 11.0 %collective-permute-start.12 = (bf16[512,128]{1,0:T(8,128)(2,1)S(1)}, bf16[512,128]{1,0:T(8,128)(2,1)S(1)}, u32[]{:S(2)}, u32[]{:S(2)}) collective-permute-start(bf16[512,128]{1,0:T(8,128)(2,1)S(1)} %copy-done.1), channel_id=1, source_target_pairs={{0,48},{16,64},{32,80},{48,96},{64,112},{80,128},{96,144},{112,160... | collective-permute-start | bytes 393224 | tf_op jit(solution)/shard_map/ppermute | solution.py:20
  41.4 16.0 %collective-permute-start.13 = (bf16[512,128]{1,0:T(8,128)(2,1)S(1)}, bf16[512,128]{1,0:T(8,128)(2,1)S(1)}, u32[]{:S(2)}, u32[]{:S(2)}) collective-permute-start(bf16[512,128]{1,0:T(8,128)(2,1)S(1)} %copy-done.1), channel_id=1, source_target_pairs={{0,32},{16,48},{32,64},{48,80},{64,96},{80,112},{96,128},{112,144}... | collective-permute-start | bytes 393224 | tf_op jit(solution)/shard_map/ppermute | solution.py:20
  41.6 15.9 %collective-permute-start.14 = (bf16[512,128]{1,0:T(8,128)(2,1)S(1)}, bf16[512,128]{1,0:T(8,128)(2,1)S(1)}, u32[]{:S(2)}, u32[]{:S(2)}) collective-permute-start(bf16[512,128]{1,0:T(8,128)(2,1)S(1)} %copy-done.1), channel_id=1, source_target_pairs={{0,16},{16,32},{32,48},{48,64},{64,80},{80,96},{96,112},{112,128},... | collective-permute-start | bytes 393224 | tf_op jit(solution)/shard_map/ppermute | solution.py:20
  57.5 5.2 %collective-permute-start.15 = (bf16[8192,128]{1,0:T(8,128)(2,1)S(1)}, bf16[8192,128]{1,0:T(8,128)(2,1)}, u32[]{:S(2)}, u32[]{:S(2)}) collective-permute-start(bf16[8192,128]{1,0:T(8,128)(2,1)S(1)} %constant_dynamic-update-slice_fusion.mine_ref), channel_id=1, source_target_pairs={{0,8},{8,0},{1,9},{9,1},{2,10},{10,2},{3,11},{11,3},{4,12},{12,4},... | collective-permute-start | bytes 6291464 | tf_op jit(solution)/shard_map/ppermute | solution.py:20
  72.9 19.4 %all-to-all-start = ((bf16[4,1024,128]{2,1,0:T(8,128)(2,1)}), bf16[4,1024,128]{2,1,0:T(8,128)(2,1)S(1)}, u32[]{:S(2)}, u32[]{:S(2)}) async-start(bf16[4,1024,128]{2,1,0:T(8,128)(2,1)} %bitcast.5), calls=%async_computation | async-start | bytes 2097152 | tf_op jit(solution)/shard_map/all_to_all | solution.py:172
  92.4 9.9 %collective-permute-start.16 = (bf16[512,128]{1,0:T(8,128)(2,1)S(1)}, bf16[512,128]{1,0:T(8,128)(2,1)S(1)}, u32[]{:S(2)}, u32[]{:S(2)}) collective-permute-start(bf16[512,128]{1,0:T(8,128)(2,1)S(1)} %get-tuple-element.10), channel_id=1, source_target_pairs={{0,1},{1,0},{2,3},{3,2},{4,5},{5,4},{6,7},{7,6},{8,9},{9,8},{10,11... | collective-permute-start | bytes 393224 | tf_op jit(solution)/shard_map/ppermute | solution.py:20
  102.9 1.3 collective-permute-start.17
  104.3 6.8 %collective-permute-start.18 = (f32[64,172]{1,0:T(8,128)S(1)}, f32[64,172]{1,0:T(8,128)S(1)}, u32[]{:S(2)}, u32[]{:S(2)}) collective-permute-start(f32[64,172]{1,0:T(8,128)S(1)} %dynamic-slice_add_fusion), channel_id=1, source_target_pairs={{0,64},{64,128},{128,192},{192,0},{1,65},{65,129},{129,193},{193,1... | collective-permute-start | bytes 132104 | tf_op jit(solution)/shard_map/ppermute | solution.py:20
  108.0 4.6 %collective-permute-start.19 = (f32[64,172]{1,0:T(8,128)S(1)}, f32[64,172]{1,0:T(8,128)S(1)}, u32[]{:S(2)}, u32[]{:S(2)}) collective-permute-start(f32[64,172]{1,0:T(8,128)S(1)} %dynamic-slice_add_fusion), channel_id=1, source_target_pairs={{0,128},{64,192},{128,0},{192,64},{1,129},{65,193},{129,1},{193,65... | collective-permute-start | bytes 132104 | tf_op jit(solution)/shard_map/ppermute | solution.py:20
  109.1 3.5 %collective-permute-start.20 = (f32[64,172]{1,0:T(8,128)S(1)}, f32[64,172]{1,0:T(8,128)S(1)}, u32[]{:S(2)}, u32[]{:S(2)}) collective-permute-start(f32[64,172]{1,0:T(8,128)S(1)} %dynamic-slice_add_fusion), channel_id=1, source_target_pairs={{0,192},{64,0},{128,64},{192,128},{1,193},{65,1},{129,65},{193,129... | collective-permute-start | bytes 132104 | tf_op jit(solution)/shard_map/ppermute | solution.py:20
  112.7 5.1 %collective-permute-start.21 = (f32[64,172]{1,0:T(8,128)S(1)}, f32[64,172]{1,0:T(8,128)S(1)}, u32[]{:S(2)}, u32[]{:S(2)}) collective-permute-start(f32[64,172]{1,0:T(8,128)S(1)} %add_add_fusion.2), channel_id=1, source_target_pairs={{0,16},{16,32},{32,48},{48,0},{1,17},{17,33},{33,49},{49,1},{2,18}... | collective-permute-start | bytes 132104 | tf_op jit(solution)/shard_map/ppermute | solution.py:20
  113.3 4.8 %collective-permute-start.22 = (f32[64,172]{1,0:T(8,128)S(1)}, f32[64,172]{1,0:T(8,128)S(1)}, u32[]{:S(2)}, u32[]{:S(2)}) collective-permute-start(f32[64,172]{1,0:T(8,128)S(1)} %add_add_fusion.2), channel_id=1, source_target_pairs={{0,32},{16,48},{32,0},{48,16},{1,33},{17,49},{33,1},{49,17},{2,34}... | collective-permute-start | bytes 132104 | tf_op jit(solution)/shard_map/ppermute | solution.py:20
  114.9 4.2 %collective-permute-start.23 = (f32[64,172]{1,0:T(8,128)S(1)}, f32[64,172]{1,0:T(8,128)S(1)}, u32[]{:S(2)}, u32[]{:S(2)}) collective-permute-start(f32[64,172]{1,0:T(8,128)S(1)} %add_add_fusion.2), channel_id=1, source_target_pairs={{0,48},{16,0},{32,16},{48,32},{1,49},{17,1},{33,17},{49,33},{2,50}... | collective-permute-start | bytes 132104 | tf_op jit(solution)/shard_map/ppermute | solution.py:20
  119.1 5.1 %collective-permute-start.24 = (f32[64,172]{1,0:T(8,128)S(1)}, f32[64,172]{1,0:T(8,128)S(1)}, u32[]{:S(2)}, u32[]{:S(2)}) collective-permute-start(f32[64,172]{1,0:T(8,128)S(1)} %add_add_fusion.1), channel_id=1, source_target_pairs={{0,2},{2,4},{4,6},{6,0},{1,3},{3,5},{5,7},{7,1},{8,10},{10,12},{12... | collective-permute-start | bytes 132104 | tf_op jit(solution)/shard_map/ppermute | solution.py:20
  119.5 4.7 %collective-permute-start.25 = (f32[64,172]{1,0:T(8,128)S(1)}, f32[64,172]{1,0:T(8,128)S(1)}, u32[]{:S(2)}, u32[]{:S(2)}) collective-permute-start(f32[64,172]{1,0:T(8,128)S(1)} %add_add_fusion.1), channel_id=1, source_target_pairs={{0,4},{2,6},{4,0},{6,2},{1,5},{3,7},{5,1},{7,3},{8,12},{10,14},{12... | collective-permute-start | bytes 132104 | tf_op jit(solution)/shard_map/ppermute | solution.py:20
  121.2 3.5 %collective-permute-start.26 = (f32[64,172]{1,0:T(8,128)S(1)}, f32[64,172]{1,0:T(8,128)S(1)}, u32[]{:S(2)}, u32[]{:S(2)}) collective-permute-start(f32[64,172]{1,0:T(8,128)S(1)} %add_add_fusion.1), channel_id=1, source_target_pairs={{0,6},{2,0},{4,2},{6,4},{1,7},{3,1},{5,3},{7,5},{8,14},{10,8},{12,... | collective-permute-start | bytes 132104 | tf_op jit(solution)/shard_map/ppermute | solution.py:20
  124.8 7.1 %collective-permute-start.27 = (f32[64,172]{1,0:T(8,128)S(1)}, f32[64,172]{1,0:T(8,128)S(1)}, u32[]{:S(2)}, u32[]{:S(2)}) collective-permute-start(f32[64,172]{1,0:T(8,128)S(1)} %add_add_fusion), channel_id=1, source_target_pairs={{0,1},{1,0},{2,3},{3,2},{4,5},{5,4},{6,7},{7,6},{8,9},{9,8},{10,11... | collective-permute-start | bytes 132104 | tf_op jit(solution)/shard_map/ppermute | solution.py:20
  131.9 7.5 %collective-permute-start.28 = (f32[64,172]{1,0:T(8,128)S(1)}, f32[64,172]{1,0:T(8,128)S(1)}, u32[]{:S(2)}, u32[]{:S(2)}) collective-permute-start(f32[64,172]{1,0:T(8,128)S(1)} %add.90), channel_id=1, source_target_pairs={{0,8},{8,0},{1,9},{9,1},{2,10},{10,2},{3,11},{11,3},{4,12},{12,4},... | collective-permute-start | bytes 132104 | tf_op jit(solution)/shard_map/ppermute | solution.py:20
  (4 other events, 85.5 us)

commit v2 on v1

v2 whole, which is shorter than its diff:
```python
import math

import jax
import jax.numpy as jnp
from jax import lax
from jax.experimental import pallas as pl
from jax.experimental.pallas import tpu as pltpu
from jax.sharding import Mesh, PartitionSpec as P

AXES = ("y", "zl", "core", "x", "zh")
SIZES = (4, 4, 2, 4, 2)
ROW = AXES[:3]
COL = AXES[3:]
GROUP = 8
CHUNK = 32


def shift(value, axes, step):
    n = lax.axis_size(axes)
    return lax.ppermute(value, axes, [(i, (i + step) % n) for i in range(n)])


def shift_z(value, step):
    n_lo, n_hi = lax.axis_size("zl"), lax.axis_size("zh")
    n = n_lo * n_hi
    at = lambda z: (z % n_lo) * n_hi + z // n_lo
    return lax.ppermute(value, ("zl", "zh"), [(at(z), at((z + step) % n)) for z in range(n)])


def fetch_kernel(count_ref, vals_ref, out_ref, sems):
    count = count_ref[0]

    def each(act):
        for k in range(vals_ref.shape[0] // CHUNK):
            @pl.when(k * CHUNK < count)
            def _(k=k):
                part = pl.ds(k * CHUNK, CHUNK)
                act(pltpu.make_async_copy(vals_ref.at[part], out_ref.at[part], sems.at[k]))

    each(lambda copy: copy.start())
    each(lambda copy: copy.wait())


def fetch(count, vals):
    return pl.pallas_call(
        fetch_kernel,
        out_shape=jax.ShapeDtypeStruct(vals.shape, vals.dtype),
        in_specs=[pl.BlockSpec(memory_space=pltpu.SMEM), pl.BlockSpec(memory_space=pltpu.HBM)],
        out_specs=pl.BlockSpec(memory_space=pltpu.VMEM),
        scratch_shapes=[pltpu.SemaphoreType.DMA((vals.shape[0] // CHUNK,))],
        compiler_params=pltpu.CompilerParams(vmem_limit_bytes=12 * 2**20),
        cost_estimate=pl.CostEstimate(flops=0, bytes_accessed=16 * 2**20, transcendentals=0),
        name="fetch",
    )(count, vals)


def aggregate_kernel(n_pieces, count_ref, rows_ref, places_ref, vals_ref, *refs):
    pieces, refs = refs[:n_pieces], refs[n_pieces:]
    own_ref, *away_refs = refs[:4]
    table, acc, prods, sem_table = refs[4:]
    tile = vals_ref.shape[-1]
    count = count_ref[0]

    table_copies, start = [], 0
    for i, piece in enumerate(pieces):
        rows = piece.shape[0]
        table_copies.append(pltpu.make_async_copy(piece, table.at[pl.ds(start, rows)], sem_table.at[i]))
        start += rows
    for copy in table_copies:
        copy.start()
    acc[...] = jnp.zeros_like(acc)
    for copy in table_copies:
        copy.wait()

    def group(g, _):
        slots = [g * GROUP + i for i in range(GROUP)]
        for i, s in enumerate(slots):
            place = pl.multiple_of(places_ref[s], tile)
            prods[i] = jnp.dot(vals_ref[s], table[pl.ds(place, tile), :], preferred_element_type=jnp.float32)
        for i, s in enumerate(slots):
            row = pl.multiple_of(rows_ref[s], tile)
            acc[pl.ds(row, tile), :] += prods[i]
        return 0

    lax.fori_loop(0, (count + GROUP - 1) // GROUP, group, 0)
    size = own_ref.shape[0]
    own_ref[...] = acc[pl.ds(0, size), :]
    for k, ref in enumerate(away_refs):
        ref[...] = acc[pl.ds((k + 1) * size, size), :].astype(ref.dtype)


def aggregate(count, rows, places, vals, pieces, out_rows):
    slots, tile, _ = vals.shape
    feat = pieces[0].shape[1]
    table_rows = sum(piece.shape[0] for piece in pieces)
    n_x = lax.axis_size("x")
    smem = pl.BlockSpec(memory_space=pltpu.SMEM)
    vmem = pl.BlockSpec(memory_space=pltpu.VMEM)
    shape = (out_rows // n_x, feat)
    return pl.pallas_call(
        lambda *refs: aggregate_kernel(len(pieces), *refs),
        out_shape=[jax.ShapeDtypeStruct(shape, jnp.float32)] + [jax.ShapeDtypeStruct(shape, jnp.bfloat16)] * (n_x - 1),
        in_specs=[smem, smem, smem, vmem] + [pl.BlockSpec(memory_space=pl.ANY)] * len(pieces),
        out_specs=[vmem] * n_x,
        scratch_shapes=[
            pltpu.VMEM((table_rows, feat), jnp.bfloat16),
            pltpu.VMEM((out_rows + tile, feat), jnp.float32),
            pltpu.VMEM((GROUP, tile, feat), jnp.float32),
            pltpu.SemaphoreType.DMA((len(pieces),)),
        ],
        compiler_params=pltpu.CompilerParams(vmem_limit_bytes=24 * 2**20),
        cost_estimate=pl.CostEstimate(flops=2 * slots * tile * tile * feat, bytes_accessed=14 * 2**20, transcendentals=0),
        name="aggregate",
    )(count, rows, places, vals, *pieces)


def head_kernel(scale, core_ref, own_ref, far_ref, *refs):
    *more_refs, weight_ref, labels_ref, logits_ref, keep_ref, give_ref = refs
    rows = far_ref.shape[0]
    total = own_ref[pl.ds(0, rows), :]
    for ref in more_refs:
        total += ref[pl.ds(0, rows), :].astype(jnp.float32)
    total += far_ref[...].astype(jnp.float32)
    upper = total.astype(jnp.bfloat16)
    lower = (total - upper.astype(jnp.float32)).astype(jnp.bfloat16)
    weight = weight_ref[...]
    by_feature = (((1,), (1,)), ((), ()))
    logits = lax.dot_general(weight, upper, by_feature, preferred_element_type=jnp.float32)
    logits += lax.dot_general(weight, lower, by_feature, preferred_element_type=jnp.float32)
    logits_ref[...] = logits
    labels = labels_ref[...]
    classes = lax.broadcasted_iota(jnp.int32, logits.shape, 0)
    residual = logits - (labels == classes).astype(jnp.float32)
    residual = jnp.where(labels >= 0, residual, 0.0).astype(jnp.bfloat16)
    grad = jnp.dot(residual, upper, preferred_element_type=jnp.float32)
    grad += jnp.dot(residual, lower, preferred_element_type=jnp.float32)
    grad = grad * scale
    half = keep_ref.shape[0]
    first, second = grad[:half], grad[half:]
    second = jnp.concatenate([second, jnp.zeros((2 * half - grad.shape[0], grad.shape[1]), grad.dtype)], 0)
    swap = core_ref[0] == 1
    keep_ref[...] = jnp.where(swap, second, first)
    give_ref[...] = jnp.where(swap, first, second)


def head(core, own, far, more, weight, labels, scale):
    rows, feat = far.shape
    classes = weight.shape[0]
    half = (classes + 15) // 16 * 8
    vmem = pl.BlockSpec(memory_space=pltpu.VMEM)
    return pl.pallas_call(
        lambda *refs: head_kernel(scale, *refs),
        out_shape=(
            jax.ShapeDtypeStruct((classes, rows), jnp.float32),
            jax.ShapeDtypeStruct((half, feat), jnp.float32),
            jax.ShapeDtypeStruct((half, feat), jnp.float32),
        ),
        in_specs=[pl.BlockSpec(memory_space=pltpu.SMEM)] + [vmem] * (4 + len(more)),
        out_specs=(vmem, vmem, vmem),
        compiler_params=pltpu.CompilerParams(vmem_limit_bytes=32 * 2**20),
        name="head",
    )(core, own, far, *more, weight, labels)


def gather_features(features):
    by_z = jnp.concatenate([features] + [shift(features, "zl", -k) for k in (1, 2, 3)], 0)
    opposite = shift(features, "y", 2)
    opposite = jnp.concatenate([opposite] + [shift(opposite, "zl", -k) for k in (1, 2, 3)], 0)
    mine = [by_z, shift(by_z, "y", -1), opposite, shift(by_z, "y", 1)]
    return mine + [shift(piece, "core", 1) for piece in mine]


def places_of(tile_cols, per_device, tile):
    device, part = tile_cols // per_device, tile_cols % per_device
    y, z, core = device // 8, device // 2 % 4, device % 2
    y = (y - lax.axis_index("y")) % 4
    z = (z - lax.axis_index("zl")) % 4
    core = (core - lax.axis_index("core")) % 2
    return (((core * 4 + y) * 4 + z) * per_device + part) * tile


def rows_of(tile_rows, per_device, tile):
    device, part = tile_rows // per_device, tile_rows % per_device
    x, zh = device // 2, device % 2
    x = (x - lax.axis_index("x")) % 4
    zh = (zh - lax.axis_index("zh")) % 2
    return ((x * 2 + zh) * per_device + part) * tile


def sum_everywhere(keep, give, core, classes):
    total = keep + shift(give, "core", 1)
    for axis in ("y", "x"):
        total = total + shift(total, axis, 1) + shift(total, axis, 2) + shift(total, axis, 3)
    total = total + shift(total, "zh", 1)
    total = total + shift_z(total, 1) + shift_z(total, 2) + shift_z(total, -1)
    rest = shift(total, "core", 1)
    swap = core == 1
    return jnp.concatenate([jnp.where(swap, rest, total), jnp.where(swap, total, rest)], 0)[:classes]


def local(features, weight, labels, tile_rows, tile_cols, tile_count, tile_vals):
    tile = tile_vals.shape[-1]
    slots = tile_vals.shape[2]
    classes = weight.shape[1]
    nodes, feat = features.shape
    vals = tile_vals.reshape(slots, tile, tile)
    count = tile_count.reshape(1)
    out_rows = nodes * lax.axis_size(COL)
    used = jnp.arange(slots, dtype=jnp.int32) < count
    rows = jnp.where(used, rows_of(tile_rows.reshape(slots), nodes // tile, tile), out_rows)
    places = places_of(tile_cols.reshape(slots), nodes // tile, tile)
    core = lax.axis_index("core").astype(jnp.int32)

    pieces = gather_features(features)
    own, *away = aggregate(count, rows, places, fetch(count, vals), pieces, out_rows)
    more = [shift(part, "x", k + 1) for k, part in enumerate(away)]
    give = own[nodes:] + sum(part[nodes:].astype(jnp.float32) for part in more)
    far = shift(give.astype(jnp.bfloat16), "zh", 1)
    scale = 1.0 / math.sqrt(nodes * lax.axis_size(AXES))
    logits, keep, give = head(core.reshape(1), own, far, more, weight.T, labels.reshape(1, nodes), scale)
    return logits.T, sum_everywhere(keep, give, core, classes).T


def solution(mesh):
    fine = Mesh(mesh.devices.reshape(SIZES), AXES)
    placed = (
        P(COL + ROW, None),
        P(),
        P(AXES),
        P(ROW, COL, None),
        P(ROW, COL, None),
        P(ROW, COL),
        P(ROW, COL, None, None, None),
    )
    return jax.shard_map(
        local, mesh=fine, in_specs=placed, out_specs=(P(AXES, None), P()), check_vma=False
    )
```

time: 140 us -> 112 us (0.80)
  starting transfers between devices: 75.1 us -> 51.5 us
  Pallas kernels: 7.46 us -> 4.89 us
  local copies, waits for them, and re-layouts: 6.55 us -> 4.87 us
    ppermute x29 -> x26, starting transfers between devices: 68.3 us -> 48.2 us  [shift(): return lax.ppermute(value, axes, [(i, (i + step) % n) for i in range(n)])]
    all_to_all x1 -> x0, waiting for transfers between devices: 12.5 us -> none  [local(): lax.all_to_all(part, 'x', 0, 0, tiled=True)]
    ppermute x29 -> x26, waiting for transfers between devices: 36.7 us -> 46.6 us  [shift(): return lax.ppermute(value, axes, [(i, (i + step) % n) for i in range(n)])]
    all_to_all x1 -> x0, starting transfers between devices: 6.89 us -> none  [local(): lax.all_to_all(part, 'x', 0, 0, tiled=True)]
    ppermute x0 -> x3, starting transfers between devices: none -> 3.31 us  [shift_z(): lax.ppermute(value, ('zl', 'zh'), [(at(z), at((z + step) % n)) for z in r...]
    pallas_call x1 -> x2, Pallas kernels: 6.89 us -> 3.8 us  [the longest x1 3.55 us: aggregate(): pl.pallas_call(lambda *refs: aggregate_kernel(len(pieces), *refs), out_sh...]
    ppermute x0 -> x3, waiting for transfers between devices: none -> 1.86 us  [shift_z(): lax.ppermute(value, ('zl', 'zh'), [(at(z), at((z + step) % n)) for z in r...]
    unnamed x30 -> x16, local copies, waits for them, and re-layouts: 6.38 us -> 4.83 us
  transfers between devices with their start and end apart: 30 -> 29, of which waited for: 14 -> 17; matrix products, arithmetic and copies ran while one was open for 2% -> 1% of each run, Pallas kernels for 0% -> 0%
where the time goes in v2:
time: 112 us
  starting transfers between devices  51.5 us (46%)
  waiting for transfers between devices  48.5 us (43%)
  Pallas kernels  4.89 us (4%)
  local copies, waits for them, and re-layouts  4.87 us (4%)
  between operations  1.46 us (1%)
    ppermute x26, starting transfers between devices, shift(): return lax.ppermute(value, axes, [(i, (i + step) % n) for i in range(n)])  48.2 us
    ppermute x26, waiting for transfers between devices, shift(): return lax.ppermute(value, axes, [(i, (i + step) % n) for i in range(n)])  46.6 us
    unnamed x16, local copies, waits for them, and re-layouts  4.83 us
    pallas_call x1, Pallas kernels, aggregate(): pl.pallas_call(lambda *refs: aggregate_kernel(len(pieces), *refs), out_sh...  3.55 us
    ppermute x3, starting transfers between devices, shift_z(): lax.ppermute(value, ('zl', 'zh'), [(at(z), at((z + step) % n)) for z in r...  3.31 us
  transfers between devices with their start and end apart: 29, of which 17 were waited for; matrix products, arithmetic and copies ran while one was open for 1% of the time, Pallas kernels for 0%

profile of v2, /device:TPU:1, one launch (start us, length us, event | category | flops | bytes accessed | tf_op | source)
XLA Modules:
  0.0 112.0 jit_solution(7519200491916643327)
XLA Ops:
  0.6 5.3 %collective-permute-start = (bf16[512,128]{1,0:T(8,128)(2,1)}, bf16[512,128]{1,0:T(8,128)(2,1)S(1)}, u32[]{:S(2)}, u32[]{:S(2)}) collective-permute-start(bf16[512,128]{1,0:T(8,128)(2,1)} %param.7), channel_id=1, source_target_pairs={{0,48},{16,0},{32,16},{48,32},{1,49},{17,1},{33,17},{49,33},{2,50}... | collective-permute-start | bytes 393224 | tf_op jit(solution)/shard_map/ppermute | solution.py:20
  5.9 2.9 %collective-permute-start.4 = (bf16[512,128]{1,0:T(8,128)(2,1)}, bf16[512,128]{1,0:T(8,128)(2,1)S(1)}, u32[]{:S(2)}, u32[]{:S(2)}) collective-permute-start(bf16[512,128]{1,0:T(8,128)(2,1)} %param.7), channel_id=1, source_target_pairs={{0,128},{64,192},{128,0},{192,64},{1,129},{65,193},{129,1},{193,65... | collective-permute-start | bytes 393224 | tf_op jit(solution)/shard_map/ppermute | solution.py:20
  9.2 0.9 constant_dynamic-update-slice_fusion.3
  10.2 8.3 %collective-permute-done.1 = bf16[512,128]{1,0:T(8,128)(2,1)S(1)} collective-permute-done((bf16[512,128]{1,0:T(8,128)(2,1)}, bf16[512,128]{1,0:T(8,128)(2,1)S(1)}, u32[]{:S(2)}, u32[]{:S(2)}) %collective-permute-start.1) | collective-permute-done | bytes 131104 | tf_op jit(solution)/shard_map/ppermute | solution.py:20
  18.5 2.4 %collective-permute-start.3 = (bf16[2048,128]{1,0:T(8,128)(2,1)S(1)}, bf16[2048,128]{1,0:T(8,128)(2,1)S(1)}, u32[]{:S(2)}, u32[]{:S(2)}) collective-permute-start(bf16[2048,128]{1,0:T(8,128)(2,1)S(1)} %constant_dynamic-update-slice_fusion.refs_4_), channel_id=1, source_target_pairs={{0,192},{64,0},{128,64},{192,128},{1,193},{65,1},{129,65},{193,129... | collective-permute-start | bytes 1572872 | tf_op jit(solution)/shard_map/ppermute | solution.py:20
  20.9 0.9 collective-permute-start.5
  21.8 1.1 %collective-permute-start.9 = (bf16[2048,128]{1,0:T(8,128)(2,1)S(1)}, bf16[2048,128]{1,0:T(8,128)(2,1)S(1)}, u32[]{:S(2)}, u32[]{:S(2)}) collective-permute-start(bf16[2048,128]{1,0:T(8,128)(2,1)S(1)} %constant_dynamic-update-slice_fusion.refs_4_), channel_id=1, source_target_pairs={{0,8},{8,0},{1,9},{9,1},{2,10},{10,2},{3,11},{11,3},{4,12},{12,4},... | collective-permute-start | bytes 1572872 | tf_op jit(solution)/shard_map/ppermute | solution.py:20
  22.9 1.6 %collective-permute-start.6 = (bf16[512,128]{1,0:T(8,128)(2,1)S(1)}, bf16[512,128]{1,0:T(8,128)(2,1)S(1)}, u32[]{:S(2)}, u32[]{:S(2)}) collective-permute-start(bf16[512,128]{1,0:T(8,128)(2,1)S(1)} %collective-permute-done.4), channel_id=1, source_target_pairs={{0,32},{16,48},{32,0},{48,16},{1,33},{17,49},{33,1},{49,17},{2,34}... | collective-permute-start | bytes 393224 | tf_op jit(solution)/shard_map/ppermute | solution.py:20
  25.0 2.1 %collective-permute-start.7 = (bf16[512,128]{1,0:T(8,128)(2,1)S(1)}, bf16[512,128]{1,0:T(8,128)(2,1)S(1)}, u32[]{:S(2)}, u32[]{:S(2)}) collective-permute-start(bf16[512,128]{1,0:T(8,128)(2,1)S(1)} %collective-permute-done.4), channel_id=1, source_target_pairs={{0,16},{16,32},{32,48},{48,0},{1,17},{17,33},{33,49},{49,1},{2,18}... | collective-permute-start | bytes 393224 | tf_op jit(solution)/shard_map/ppermute | solution.py:20
  27.1 8.1 %collective-permute-done.6 = bf16[512,128]{1,0:T(8,128)(2,1)S(1)} collective-permute-done((bf16[512,128]{1,0:T(8,128)(2,1)S(1)}, bf16[512,128]{1,0:T(8,128)(2,1)S(1)}, u32[]{:S(2)}, u32[]{:S(2)}) %collective-permute-start.6) | collective-permute-done | bytes 131104 | tf_op jit(solution)/shard_map/ppermute | solution.py:20
  35.3 1.4 %collective-permute-start.11 = (bf16[2048,128]{1,0:T(8,128)(2,1)S(1)}, bf16[2048,128]{1,0:T(8,128)(2,1)S(1)}, u32[]{:S(2)}, u32[]{:S(2)}) collective-permute-start(bf16[2048,128]{1,0:T(8,128)(2,1)S(1)} %constant_dynamic-update-slice_fusion.4.refs_6_), channel_id=1, source_target_pairs={{0,8},{8,0},{1,9},{9,1},{2,10},{10,2},{3,11},{11,3},{4,12},{12,4},... | collective-permute-start | bytes 1572872 | tf_op jit(solution)/shard_map/ppermute | solution.py:20
  37.9 3.4 %copy-done = bf16[1,1,256,128,128]{4,3,2,1,0:T(8,128)(2,1)S(1)} copy-done((bf16[1,1,256,128,128]{4,3,2,1,0:T(8,128)(2,1)S(1)}, bf16[1,1,256,128,128]{4,3,2,1,0:T(8,128)(2,1)}, u32[]{:S(2)}) %copy-start) | copy-done | bytes 8388632
  42.0 3.5 %aggregate.1 = (f32[1024,128]{1,0:T(8,128)S(1)}, bf16[1024,128]{1,0:T(8,128)(2,1)S(1)}, bf16[1024,128]{1,0:T(8,128)(2,1)S(1)}, bf16[1024,128]{1,0:T(8,128)(2,1)S(1)}) custom-call(s32[1]{0:T(128)} %bitcast.12.refs_0_, s32[256]{0:T(256)S(1)} %get-tuple-element.18.refs_1_, s32[256]{0:T(256)S(1)} %get-tuple-element.19.refs_2_, ...), custom_call_target="tpu_custom_call" | custom-call | flops 1073741824 | bytes 14680064 | tf_op jit(solution)/shard_map/aggregate/pallas_call | solution.py:100
  45.6 1.3 %collective-permute-start.13 = (bf16[1024,128]{1,0:T(8,128)(2,1)S(1)}, bf16[1024,128]{1,0:T(8,128)(2,1)S(1)}, u32[]{:S(2)}, u32[]{:S(2)}) collective-permute-start(bf16[1024,128]{1,0:T(8,128)(2,1)S(1)} %get-tuple-element.10), channel_id=1, source_target_pairs={{0,2},{2,4},{4,6},{6,0},{1,3},{3,5},{5,7},{7,1},{8,10},{10,12},{12... | collective-permute-start | bytes 786440 | tf_op jit(solution)/shard_map/ppermute | solution.py:20
  46.9 4.8 %collective-permute-start.14 = (bf16[1024,128]{1,0:T(8,128)(2,1)S(1)}, bf16[1024,128]{1,0:T(8,128)(2,1)S(1)}, u32[]{:S(2)}, u32[]{:S(2)}) collective-permute-start(bf16[1024,128]{1,0:T(8,128)(2,1)S(1)} %get-tuple-element.11), channel_id=1, source_target_pairs={{0,4},{2,6},{4,0},{6,2},{1,5},{3,7},{5,1},{7,3},{8,12},{10,14},{12... | collective-permute-start | bytes 786440 | tf_op jit(solution)/shard_map/ppermute | solution.py:20
  51.9 5.1 %collective-permute-done.13.refs_3_ = bf16[1024,128]{1,0:T(8,128)(2,1)S(1)} collective-permute-done((bf16[1024,128]{1,0:T(8,128)(2,1)S(1)}, bf16[1024,128]{1,0:T(8,128)(2,1)S(1)}, u32[]{:S(2)}, u32[]{:S(2)}) %collective-permute-start.13) | collective-permute-done | bytes 262176 | tf_op jit(solution)/shard_map/ppermute | solution.py:20
  57.0 6.3 %collective-permute-done.14.refs_4_ = bf16[1024,128]{1,0:T(8,128)(2,1)S(1)} collective-permute-done((bf16[1024,128]{1,0:T(8,128)(2,1)S(1)}, bf16[1024,128]{1,0:T(8,128)(2,1)S(1)}, u32[]{:S(2)}, u32[]{:S(2)}) %collective-permute-start.14) | collective-permute-done | bytes 262176 | tf_op jit(solution)/shard_map/ppermute | solution.py:20
  63.8 2.7 %collective-permute-start.16 = (bf16[512,128]{1,0:T(8,128)(2,1)S(1)}, bf16[512,128]{1,0:T(8,128)(2,1)S(1)}, u32[]{:S(2)}, u32[]{:S(2)}) collective-permute-start(bf16[512,128]{1,0:T(8,128)(2,1)S(1)} %add_convert_fusion), channel_id=1, source_target_pairs={{0,1},{1,0},{2,3},{3,2},{4,5},{5,4},{6,7},{7,6},{8,9},{9,8},{10,11... | collective-permute-start | bytes 393224 | tf_op jit(solution)/shard_map/ppermute | solution.py:20
  66.5 6.1 %collective-permute-done.16.refs_2_ = bf16[512,128]{1,0:T(8,128)(2,1)S(1)} collective-permute-done((bf16[512,128]{1,0:T(8,128)(2,1)S(1)}, bf16[512,128]{1,0:T(8,128)(2,1)S(1)}, u32[]{:S(2)}, u32[]{:S(2)}) %collective-permute-start.16) | collective-permute-done | bytes 131104 | tf_op jit(solution)/shard_map/ppermute | solution.py:20
  72.6 1.1 head.1
  73.7 1.3 %collective-permute-start.17 = (f32[88,128]{1,0:T(8,128)S(1)}, f32[88,128]{1,0:T(8,128)S(1)}, u32[]{:S(2)}, u32[]{:S(2)}) collective-permute-start(f32[88,128]{1,0:T(8,128)S(1)} %get-tuple-element.15), channel_id=1, source_target_pairs={{0,8},{8,0},{1,9},{9,1},{2,10},{10,2},{3,11},{11,3},{4,12},{12,4},... | collective-permute-start | bytes 135176 | tf_op jit(solution)/shard_map/ppermute | solution.py:20
  75.9 6.0 %collective-permute-start.19 = (f32[88,128]{1,0:T(8,128)S(1)}, f32[88,128]{1,0:T(8,128)S(1)}, u32[]{:S(2)}, u32[]{:S(2)}) collective-permute-start(f32[88,128]{1,0:T(8,128)S(1)} %add.122), channel_id=1, source_target_pairs={{0,128},{64,192},{128,0},{192,64},{1,129},{65,193},{129,1},{193,65... | collective-permute-start | bytes 135176 | tf_op jit(solution)/shard_map/ppermute | solution.py:20
  82.2 1.8 %collective-permute-done.19 = f32[88,128]{1,0:T(8,128)S(1)} collective-permute-done((f32[88,128]{1,0:T(8,128)S(1)}, f32[88,128]{1,0:T(8,128)S(1)}, u32[]{:S(2)}, u32[]{:S(2)}) %collective-permute-start.19) | collective-permute-done | bytes 45088 | tf_op jit(solution)/shard_map/ppermute | solution.py:20
  84.0 1.2 %collective-permute-done.20 = f32[88,128]{1,0:T(8,128)S(1)} collective-permute-done((f32[88,128]{1,0:T(8,128)S(1)}, f32[88,128]{1,0:T(8,128)S(1)}, u32[]{:S(2)}, u32[]{:S(2)}) %collective-permute-start.20) | collective-permute-done | bytes 45088 | tf_op jit(solution)/shard_map/ppermute | solution.py:20
  85.1 1.7 %collective-permute-start.21 = (f32[88,128]{1,0:T(8,128)S(1)}, f32[88,128]{1,0:T(8,128)S(1)}, u32[]{:S(2)}, u32[]{:S(2)}) collective-permute-start(f32[88,128]{1,0:T(8,128)S(1)} %add_add_fusion.2), channel_id=1, source_target_pairs={{0,2},{2,4},{4,6},{6,0},{1,3},{3,5},{5,7},{7,1},{8,10},{10,12},{12... | collective-permute-start | bytes 135176 | tf_op jit(solution)/shard_map/ppermute | solution.py:20
  86.8 2.1 %collective-permute-start.22 = (f32[88,128]{1,0:T(8,128)S(1)}, f32[88,128]{1,0:T(8,128)S(1)}, u32[]{:S(2)}, u32[]{:S(2)}) collective-permute-start(f32[88,128]{1,0:T(8,128)S(1)} %add_add_fusion.2), channel_id=1, source_target_pairs={{0,4},{2,6},{4,0},{6,2},{1,5},{3,7},{5,1},{7,3},{8,12},{10,14},{12... | collective-permute-start | bytes 135176 | tf_op jit(solution)/shard_map/ppermute | solution.py:20
  89.3 1.9 %collective-permute-done.22 = f32[88,128]{1,0:T(8,128)S(1)} collective-permute-done((f32[88,128]{1,0:T(8,128)S(1)}, f32[88,128]{1,0:T(8,128)S(1)}, u32[]{:S(2)}, u32[]{:S(2)}) %collective-permute-start.22) | collective-permute-done | bytes 45088 | tf_op jit(solution)/shard_map/ppermute | solution.py:20
  92.0 2.7 %collective-permute-start.24 = (f32[88,128]{1,0:T(8,128)S(1)}, f32[88,128]{1,0:T(8,128)S(1)}, u32[]{:S(2)}, u32[]{:S(2)}) collective-permute-start(f32[88,128]{1,0:T(8,128)S(1)} %add_add_fusion.1), channel_id=1, source_target_pairs={{0,1},{1,0},{2,3},{3,2},{4,5},{5,4},{6,7},{7,6},{8,9},{9,8},{10,11... | collective-permute-start | bytes 135176 | tf_op jit(solution)/shard_map/ppermute | solution.py:20
  94.7 4.2 %collective-permute-done.24 = f32[88,128]{1,0:T(8,128)S(1)} collective-permute-done((f32[88,128]{1,0:T(8,128)S(1)}, f32[88,128]{1,0:T(8,128)S(1)}, u32[]{:S(2)}, u32[]{:S(2)}) %collective-permute-start.24) | collective-permute-done | bytes 45088 | tf_op jit(solution)/shard_map/ppermute | solution.py:20
  99.7 2.6 %collective-permute-start.27 = (f32[88,128]{1,0:T(8,128)S(1)}, f32[88,128]{1,0:T(8,128)S(1)}, u32[]{:S(2)}, u32[]{:S(2)}) collective-permute-start(f32[88,128]{1,0:T(8,128)S(1)} %add.129), channel_id=1, source_target_pairs={{0,49},{16,0},{32,16},{48,32},{1,48},{17,1},{33,17},{49,33},{2,51}... | collective-permute-start | bytes 135176 | tf_op jit(solution)/shard_map/ppermute | solution.py:27
  102.2 1.1 collective-permute-done.25
  104.1 6.4 %collective-permute-start.28 = (f32[88,128]{1,0:T(8,128)S(1)}, f32[88,128]{1,0:T(8,128)S(1)}, u32[]{:S(2)}, u32[]{:S(2)}) collective-permute-start(f32[88,128]{1,0:T(8,128)S(1)} %add_add_fusion), channel_id=1, source_target_pairs={{0,8},{8,0},{1,9},{9,1},{2,10},{10,2},{3,11},{11,3},{4,12},{12,4},... | collective-permute-start | bytes 135176 | tf_op jit(solution)/shard_map/ppermute | solution.py:20
  (56 shorter events, 8.3 us)
Async XLA Ops:
  0.6 9.5 %collective-permute-start = (bf16[512,128]{1,0:T(8,128)(2,1)}, bf16[512,128]{1,0:T(8,128)(2,1)S(1)}, u32[]{:S(2)}, u32[]{:S(2)}) collective-permute-start(bf16[512,128]{1,0:T(8,128)(2,1)} %param.7), channel_id=1, source_target_pairs={{0,48},{16,0},{32,16},{48,32},{1,49},{17,1},{33,17},{49,33},{2,50}... | collective-permute-start | bytes 393224 | tf_op jit(solution)/shard_map/ppermute | solution.py:20
  5.9 15.0 %collective-permute-start.4 = (bf16[512,128]{1,0:T(8,128)(2,1)}, bf16[512,128]{1,0:T(8,128)(2,1)S(1)}, u32[]{:S(2)}, u32[]{:S(2)}) collective-permute-start(bf16[512,128]{1,0:T(8,128)(2,1)} %param.7), channel_id=1, source_target_pairs={{0,128},{64,192},{128,0},{192,64},{1,129},{65,193},{129,1},{193,65... | collective-permute-start | bytes 393224 | tf_op jit(solution)/shard_map/ppermute | solution.py:20
  8.8 9.7 %collective-permute-start.1 = (bf16[512,128]{1,0:T(8,128)(2,1)}, bf16[512,128]{1,0:T(8,128)(2,1)S(1)}, u32[]{:S(2)}, u32[]{:S(2)}) collective-permute-start(bf16[512,128]{1,0:T(8,128)(2,1)} %param.7), channel_id=1, source_target_pairs={{0,32},{16,48},{32,0},{48,16},{1,33},{17,49},{33,1},{49,17},{2,34}... | collective-permute-start | bytes 393224 | tf_op jit(solution)/shard_map/ppermute | solution.py:20
  8.8 9.7 %collective-permute-start.2 = (bf16[512,128]{1,0:T(8,128)(2,1)}, bf16[512,128]{1,0:T(8,128)(2,1)S(1)}, u32[]{:S(2)}, u32[]{:S(2)}) collective-permute-start(bf16[512,128]{1,0:T(8,128)(2,1)} %param.7), channel_id=1, source_target_pairs={{0,16},{16,32},{32,48},{48,0},{1,17},{17,33},{33,49},{49,1},{2,18}... | collective-permute-start | bytes 393224 | tf_op jit(solution)/shard_map/ppermute | solution.py:20
  18.5 18.2 %collective-permute-start.3 = (bf16[2048,128]{1,0:T(8,128)(2,1)S(1)}, bf16[2048,128]{1,0:T(8,128)(2,1)S(1)}, u32[]{:S(2)}, u32[]{:S(2)}) collective-permute-start(bf16[2048,128]{1,0:T(8,128)(2,1)S(1)} %constant_dynamic-update-slice_fusion.refs_4_), channel_id=1, source_target_pairs={{0,192},{64,0},{128,64},{192,128},{1,193},{65,1},{129,65},{193,129... | collective-permute-start | bytes 1572872 | tf_op jit(solution)/shard_map/ppermute | solution.py:20
  20.9 15.9 %collective-permute-start.8 = (bf16[2048,128]{1,0:T(8,128)(2,1)S(1)}, bf16[2048,128]{1,0:T(8,128)(2,1)S(1)}, u32[]{:S(2)}, u32[]{:S(2)}) collective-permute-start(bf16[2048,128]{1,0:T(8,128)(2,1)S(1)} %constant_dynamic-update-slice_fusion.refs_4_), channel_id=1, source_target_pairs={{0,64},{64,128},{128,192},{192,0},{1,65},{65,129},{129,193},{193,1... | collective-permute-start | bytes 1572872 | tf_op jit(solution)/shard_map/ppermute | solution.py:20
  20.9 4.1 %collective-permute-start.5 = (bf16[512,128]{1,0:T(8,128)(2,1)S(1)}, bf16[512,128]{1,0:T(8,128)(2,1)S(1)}, u32[]{:S(2)}, u32[]{:S(2)}) collective-permute-start(bf16[512,128]{1,0:T(8,128)(2,1)S(1)} %collective-permute-done.4), channel_id=1, source_target_pairs={{0,48},{16,0},{32,16},{48,32},{1,49},{17,1},{33,17},{49,33},{2,50}... | collective-permute-start | bytes 393224 | tf_op jit(solution)/shard_map/ppermute | solution.py:20
  21.8 20.2 %collective-permute-start.9 = (bf16[2048,128]{1,0:T(8,128)(2,1)S(1)}, bf16[2048,128]{1,0:T(8,128)(2,1)S(1)}, u32[]{:S(2)}, u32[]{:S(2)}) collective-permute-start(bf16[2048,128]{1,0:T(8,128)(2,1)S(1)} %constant_dynamic-update-slice_fusion.refs_4_), channel_id=1, source_target_pairs={{0,8},{8,0},{1,9},{9,1},{2,10},{10,2},{3,11},{11,3},{4,12},{12,4},... | collective-permute-start | bytes 1572872 | tf_op jit(solution)/shard_map/ppermute | solution.py:20
  22.9 12.3 %collective-permute-start.6 = (bf16[512,128]{1,0:T(8,128)(2,1)S(1)}, bf16[512,128]{1,0:T(8,128)(2,1)S(1)}, u32[]{:S(2)}, u32[]{:S(2)}) collective-permute-start(bf16[512,128]{1,0:T(8,128)(2,1)S(1)} %collective-permute-done.4), channel_id=1, source_target_pairs={{0,32},{16,48},{32,0},{48,16},{1,33},{17,49},{33,1},{49,17},{2,34}... | collective-permute-start | bytes 393224 | tf_op jit(solution)/shard_map/ppermute | solution.py:20
  25.0 10.2 %collective-permute-start.7 = (bf16[512,128]{1,0:T(8,128)(2,1)S(1)}, bf16[512,128]{1,0:T(8,128)(2,1)S(1)}, u32[]{:S(2)}, u32[]{:S(2)}) collective-permute-start(bf16[512,128]{1,0:T(8,128)(2,1)S(1)} %collective-permute-done.4), channel_id=1, source_target_pairs={{0,16},{16,32},{32,48},{48,0},{1,17},{17,33},{33,49},{49,1},{2,18}... | collective-permute-start | bytes 393224 | tf_op jit(solution)/shard_map/ppermute | solution.py:20
  35.3 6.7 %collective-permute-start.11 = (bf16[2048,128]{1,0:T(8,128)(2,1)S(1)}, bf16[2048,128]{1,0:T(8,128)(2,1)S(1)}, u32[]{:S(2)}, u32[]{:S(2)}) collective-permute-start(bf16[2048,128]{1,0:T(8,128)(2,1)S(1)} %constant_dynamic-update-slice_fusion.4.refs_6_), channel_id=1, source_target_pairs={{0,8},{8,0},{1,9},{9,1},{2,10},{10,2},{3,11},{11,3},{4,12},{12,4},... | collective-permute-start | bytes 1572872 | tf_op jit(solution)/shard_map/ppermute | solution.py:20
  36.7 5.3 %collective-permute-start.10 = (bf16[2048,128]{1,0:T(8,128)(2,1)S(1)}, bf16[2048,128]{1,0:T(8,128)(2,1)}, u32[]{:S(2)}, u32[]{:S(2)}) collective-permute-start(bf16[2048,128]{1,0:T(8,128)(2,1)S(1)} %collective-permute-done.3.refs_5_), channel_id=1, source_target_pairs={{0,8},{8,0},{1,9},{9,1},{2,10},{10,2},{3,11},{11,3},{4,12},{12,4},... | collective-permute-start | bytes 1572872 | tf_op jit(solution)/shard_map/ppermute | solution.py:20
  36.8 5.2 %collective-permute-start.12 = (bf16[2048,128]{1,0:T(8,128)(2,1)S(1)}, bf16[2048,128]{1,0:T(8,128)(2,1)}, u32[]{:S(2)}, u32[]{:S(2)}) collective-permute-start(bf16[2048,128]{1,0:T(8,128)(2,1)S(1)} %collective-permute-done.8.refs_7_), channel_id=1, source_target_pairs={{0,8},{8,0},{1,9},{9,1},{2,10},{10,2},{3,11},{11,3},{4,12},{12,4},... | collective-permute-start | bytes 1572872 | tf_op jit(solution)/shard_map/ppermute | solution.py:20
  37.9 3.4 %copy-start = (bf16[1,1,256,128,128]{4,3,2,1,0:T(8,128)(2,1)S(1)}, bf16[1,1,256,128,128]{4,3,2,1,0:T(8,128)(2,1)}, u32[]{:S(2)}) copy-start(bf16[1,1,256,128,128]{4,3,2,1,0:T(8,128)(2,1)} %param.13) | copy-start | bytes 25165828
  41.5 31.1 %copy-start.1 = (bf16[128,172]{0,1:T(8,128)(2,1)S(1)}, bf16[128,172]{0,1:T(8,128)(2,1)}, u32[]{:S(2)}) copy-start(bf16[128,172]{0,1:T(8,128)(2,1)} %param.8) | copy-start | bytes 132100
  41.5 31.1 %copy-start.2 = (s32[512]{0:T(512)S(1)}, s32[512]{0:T(512)}, u32[]{:S(2)}) copy-start(s32[512]{0:T(512)} %param.9) | copy-start | bytes 6148
  45.6 11.4 %collective-permute-start.13 = (bf16[1024,128]{1,0:T(8,128)(2,1)S(1)}, bf16[1024,128]{1,0:T(8,128)(2,1)S(1)}, u32[]{:S(2)}, u32[]{:S(2)}) collective-permute-start(bf16[1024,128]{1,0:T(8,128)(2,1)S(1)} %get-tuple-element.10), channel_id=1, source_target_pairs={{0,2},{2,4},{4,6},{6,0},{1,3},{3,5},{5,7},{7,1},{8,10},{10,12},{12... | collective-permute-start | bytes 786440 | tf_op jit(solution)/shard_map/ppermute | solution.py:20
  46.9 16.4 %collective-permute-start.14 = (bf16[1024,128]{1,0:T(8,128)(2,1)S(1)}, bf16[1024,128]{1,0:T(8,128)(2,1)S(1)}, u32[]{:S(2)}, u32[]{:S(2)}) collective-permute-start(bf16[1024,128]{1,0:T(8,128)(2,1)S(1)} %get-tuple-element.11), channel_id=1, source_target_pairs={{0,4},{2,6},{4,0},{6,2},{1,5},{3,7},{5,1},{7,3},{8,12},{10,14},{12... | collective-permute-start | bytes 786440 | tf_op jit(solution)/shard_map/ppermute | solution.py:20
  51.7 12.0 %collective-permute-start.15 = (bf16[1024,128]{1,0:T(8,128)(2,1)S(1)}, bf16[1024,128]{1,0:T(8,128)(2,1)S(1)}, u32[]{:S(2)}, u32[]{:S(2)}) collective-permute-start(bf16[1024,128]{1,0:T(8,128)(2,1)S(1)} %get-tuple-element.12), channel_id=1, source_target_pairs={{0,6},{2,0},{4,2},{6,4},{1,7},{3,1},{5,3},{7,5},{8,14},{10,8},{12,... | collective-permute-start | bytes 786440 | tf_op jit(solution)/shard_map/ppermute | solution.py:20
  63.8 8.9 %collective-permute-start.16 = (bf16[512,128]{1,0:T(8,128)(2,1)S(1)}, bf16[512,128]{1,0:T(8,128)(2,1)S(1)}, u32[]{:S(2)}, u32[]{:S(2)}) collective-permute-start(bf16[512,128]{1,0:T(8,128)(2,1)S(1)} %add_convert_fusion), channel_id=1, source_target_pairs={{0,1},{1,0},{2,3},{3,2},{4,5},{5,4},{6,7},{7,6},{8,9},{9,8},{10,11... | collective-permute-start | bytes 393224 | tf_op jit(solution)/shard_map/ppermute | solution.py:20
  73.7 2.2 %collective-permute-start.17 = (f32[88,128]{1,0:T(8,128)S(1)}, f32[88,128]{1,0:T(8,128)S(1)}, u32[]{:S(2)}, u32[]{:S(2)}) collective-permute-start(f32[88,128]{1,0:T(8,128)S(1)} %get-tuple-element.15), channel_id=1, source_target_pairs={{0,8},{8,0},{1,9},{9,1},{2,10},{10,2},{3,11},{11,3},{4,12},{12,4},... | collective-permute-start | bytes 135176 | tf_op jit(solution)/shard_map/ppermute | solution.py:20
  75.9 6.3 %collective-permute-start.18 = (f32[88,128]{1,0:T(8,128)S(1)}, f32[88,128]{1,0:T(8,128)S(1)}, u32[]{:S(2)}, u32[]{:S(2)}) collective-permute-start(f32[88,128]{1,0:T(8,128)S(1)} %add.122), channel_id=1, source_target_pairs={{0,64},{64,128},{128,192},{192,0},{1,65},{65,129},{129,193},{193,1... | collective-permute-start | bytes 135176 | tf_op jit(solution)/shard_map/ppermute | solution.py:20
  75.9 8.0 %collective-permute-start.19 = (f32[88,128]{1,0:T(8,128)S(1)}, f32[88,128]{1,0:T(8,128)S(1)}, u32[]{:S(2)}, u32[]{:S(2)}) collective-permute-start(f32[88,128]{1,0:T(8,128)S(1)} %add.122), channel_id=1, source_target_pairs={{0,128},{64,192},{128,0},{192,64},{1,129},{65,193},{129,1},{193,65... | collective-permute-start | bytes 135176 | tf_op jit(solution)/shard_map/ppermute | solution.py:20
  81.9 3.2 %collective-permute-start.20 = (f32[88,128]{1,0:T(8,128)S(1)}, f32[88,128]{1,0:T(8,128)S(1)}, u32[]{:S(2)}, u32[]{:S(2)}) collective-permute-start(f32[88,128]{1,0:T(8,128)S(1)} %add.122), channel_id=1, source_target_pairs={{0,192},{64,0},{128,64},{192,128},{1,193},{65,1},{129,65},{193,129... | collective-permute-start | bytes 135176 | tf_op jit(solution)/shard_map/ppermute | solution.py:20
  85.1 4.2 %collective-permute-start.21 = (f32[88,128]{1,0:T(8,128)S(1)}, f32[88,128]{1,0:T(8,128)S(1)}, u32[]{:S(2)}, u32[]{:S(2)}) collective-permute-start(f32[88,128]{1,0:T(8,128)S(1)} %add_add_fusion.2), channel_id=1, source_target_pairs={{0,2},{2,4},{4,6},{6,0},{1,3},{3,5},{5,7},{7,1},{8,10},{10,12},{12... | collective-permute-start | bytes 135176 | tf_op jit(solution)/shard_map/ppermute | solution.py:20
  86.8 4.4 %collective-permute-start.22 = (f32[88,128]{1,0:T(8,128)S(1)}, f32[88,128]{1,0:T(8,128)S(1)}, u32[]{:S(2)}, u32[]{:S(2)}) collective-permute-start(f32[88,128]{1,0:T(8,128)S(1)} %add_add_fusion.2), channel_id=1, source_target_pairs={{0,4},{2,6},{4,0},{6,2},{1,5},{3,7},{5,1},{7,3},{8,12},{10,14},{12... | collective-permute-start | bytes 135176 | tf_op jit(solution)/shard_map/ppermute | solution.py:20
  88.9 3.1 %collective-permute-start.23 = (f32[88,128]{1,0:T(8,128)S(1)}, f32[88,128]{1,0:T(8,128)S(1)}, u32[]{:S(2)}, u32[]{:S(2)}) collective-permute-start(f32[88,128]{1,0:T(8,128)S(1)} %add_add_fusion.2), channel_id=1, source_target_pairs={{0,6},{2,0},{4,2},{6,4},{1,7},{3,1},{5,3},{7,5},{8,14},{10,8},{12,... | collective-permute-start | bytes 135176 | tf_op jit(solution)/shard_map/ppermute | solution.py:20
  92.0 6.9 %collective-permute-start.24 = (f32[88,128]{1,0:T(8,128)S(1)}, f32[88,128]{1,0:T(8,128)S(1)}, u32[]{:S(2)}, u32[]{:S(2)}) collective-permute-start(f32[88,128]{1,0:T(8,128)S(1)} %add_add_fusion.1), channel_id=1, source_target_pairs={{0,1},{1,0},{2,3},{3,2},{4,5},{5,4},{6,7},{7,6},{8,9},{9,8},{10,11... | collective-permute-start | bytes 135176 | tf_op jit(solution)/shard_map/ppermute | solution.py:20
  98.9 4.4 %collective-permute-start.25 = (f32[88,128]{1,0:T(8,128)S(1)}, f32[88,128]{1,0:T(8,128)S(1)}, u32[]{:S(2)}, u32[]{:S(2)}) collective-permute-start(f32[88,128]{1,0:T(8,128)S(1)} %add.129), channel_id=1, source_target_pairs={{0,16},{16,32},{32,48},{48,1},{1,17},{17,33},{33,49},{49,0},{2,18}... | collective-permute-start | bytes 135176 | tf_op jit(solution)/shard_map/ppermute | solution.py:27
  99.0 5.1 %collective-permute-start.26 = (f32[88,128]{1,0:T(8,128)S(1)}, f32[88,128]{1,0:T(8,128)S(1)}, u32[]{:S(2)}, u32[]{:S(2)}) collective-permute-start(f32[88,128]{1,0:T(8,128)S(1)} %add.129), channel_id=1, source_target_pairs={{0,32},{16,48},{32,1},{48,17},{1,33},{17,49},{33,0},{49,16},{2,34}... | collective-permute-start | bytes 135176 | tf_op jit(solution)/shard_map/ppermute | solution.py:27
  99.7 4.4 %collective-permute-start.27 = (f32[88,128]{1,0:T(8,128)S(1)}, f32[88,128]{1,0:T(8,128)S(1)}, u32[]{:S(2)}, u32[]{:S(2)}) collective-permute-start(f32[88,128]{1,0:T(8,128)S(1)} %add.129), channel_id=1, source_target_pairs={{0,49},{16,0},{32,16},{48,32},{1,48},{17,1},{33,17},{49,33},{2,51}... | collective-permute-start | bytes 135176 | tf_op jit(solution)/shard_map/ppermute | solution.py:27
  104.1 7.2 %collective-permute-start.28 = (f32[88,128]{1,0:T(8,128)S(1)}, f32[88,128]{1,0:T(8,128)S(1)}, u32[]{:S(2)}, u32[]{:S(2)}) collective-permute-start(f32[88,128]{1,0:T(8,128)S(1)} %add_add_fusion), channel_id=1, source_target_pairs={{0,8},{8,0},{1,9},{9,1},{2,10},{10,2},{3,11},{11,3},{4,12},{12,4},... | collective-permute-start | bytes 135176 | tf_op jit(solution)/shard_map/ppermute | solution.py:20
  (2 other events, 1.4 us)

commit v3 on v2

v3 whole, which is shorter than its diff:
```python
import functools
import math

import jax
import jax.numpy as jnp
from jax import lax
from jax.experimental import pallas as pl
from jax.experimental.pallas import tpu as pltpu
from jax.sharding import Mesh, PartitionSpec as P

AXES = ("y", "zl", "core", "x", "zh")
SIZES = (4, 4, 2, 4, 2)
ROW = AXES[:3]
COL = AXES[3:]
GROUP = 8


def shift(value, axes, step):
    n = lax.axis_size(axes)
    return lax.ppermute(value, axes, [(i, (i + step) % n) for i in range(n)])


def shift_z(value, step):
    n_lo, n_hi = lax.axis_size("zl"), lax.axis_size("zh")
    n = n_lo * n_hi
    at = lambda z: (z % n_lo) * n_hi + z // n_lo
    return lax.ppermute(value, ("zl", "zh"), [(at(z), at((z + step) % n)) for z in range(n)])


def plan_kernel(per_device, tile, place_ref, rows_ref, cols_ref, plan_ref):
    y0, z0, core0, x0, zh0, count = (place_ref[i] for i in range(6))
    slots = rows_ref.shape[1]
    slot = lax.broadcasted_iota(jnp.int32, (1, slots), 1)
    device, part = rows_ref[...] // per_device, rows_ref[...] % per_device
    row = (device // 2 - x0) % 4 * per_device + part
    far = (device % 2 - zh0) % 2 == 1
    device, part = cols_ref[...] // per_device, cols_ref[...] % per_device
    place = (device % 2 - core0) % 2 * 4 + (device // 8 - y0) % 4
    place = (place * 4 + (device // 2 % 4 - z0) % 4) * per_device + part
    used = slot < count
    before = lax.broadcasted_iota(jnp.int32, (slots, slots), 0) <= lax.broadcasted_iota(jnp.int32, (slots, slots), 1)
    before = before.astype(jnp.bfloat16)
    listed = lax.broadcasted_iota(jnp.int32, (slots, slots), 0)
    blank = jnp.zeros((5, slots), jnp.float32)
    values = jnp.concatenate([v.astype(jnp.float32) for v in (slot, row, place)] + [blank], 0).astype(jnp.bfloat16)
    by_slot = (((1,), (1,)), ((), ()))
    for k, member in enumerate((used & far, used & jnp.logical_not(far))):
        marks = jnp.broadcast_to(member.astype(jnp.float32), (8, slots)).astype(jnp.bfloat16)
        rank = jnp.dot(marks, before, preferred_element_type=jnp.float32)[:1].astype(jnp.int32)
        size = jnp.max(rank, axis=1, keepdims=True)
        rank = jnp.where(member, rank - 1, -1)
        picks = (listed == rank).astype(jnp.float32).astype(jnp.bfloat16)
        chosen = lax.dot_general(values, picks, by_slot, preferred_element_type=jnp.float32).astype(jnp.int32)
        filled = slot < size
        plan_ref[pl.ds(4 * k, 1), :] = chosen[0:1]
        plan_ref[pl.ds(4 * k + 1, 1), :] = jnp.where(filled, chosen[1:2], 4 * per_device) * tile
        plan_ref[pl.ds(4 * k + 2, 1), :] = chosen[2:3] * tile
        plan_ref[pl.ds(4 * k + 3, 1), :] = jnp.broadcast_to(size, (1, slots))


def plan(tile_rows, tile_cols, count, per_device, tile):
    slots = tile_rows.shape[1]
    vmem = pl.BlockSpec(memory_space=pltpu.VMEM)
    place = jnp.stack([lax.axis_index(axis) for axis in AXES] + [count]).astype(jnp.int32)
    return pl.pallas_call(
        lambda *refs: plan_kernel(per_device, tile, *refs),
        out_shape=jax.ShapeDtypeStruct((8, slots), jnp.int32),
        in_specs=[pl.BlockSpec(memory_space=pltpu.SMEM), vmem, vmem],
        out_specs=vmem,
        name="plan",
    )(place, tile_rows, tile_cols)


def sum_tiles(part, plan_ref, vals_ref, table_ref, own_ref, away_refs, vals, acc, prods, sems, beside=None):
    tile = vals.shape[-1]
    groups = (plan_ref[4 * part + 3, 0] + GROUP - 1) // GROUP

    def fetch(g, _):
        for i in range(GROUP):
            s = g * GROUP + i
            pltpu.make_async_copy(vals_ref.at[plan_ref[4 * part, s]], vals.at[s], sems.at[g]).start()
        return 0

    lax.fori_loop(0, groups, fetch, 0)
    acc[...] = jnp.zeros_like(acc)
    if beside is not None:
        beside()

    def group(g, _):
        here = pl.ds(g * GROUP, GROUP)
        pltpu.make_async_copy(vals_ref.at[pl.ds(0, GROUP)], vals.at[here], sems.at[g]).wait()
        slots = [g * GROUP + i for i in range(GROUP)]
        for i, s in enumerate(slots):
            place = pl.multiple_of(plan_ref[4 * part + 2, s], tile)
            prods[i] = jnp.dot(vals[s], table_ref[pl.ds(place, tile), :], preferred_element_type=jnp.float32)
        for i, s in enumerate(slots):
            row = pl.multiple_of(plan_ref[4 * part + 1, s], tile)
            acc[pl.ds(row, tile), :] += prods[i]
        return 0

    lax.fori_loop(0, groups, group, 0)
    size = own_ref.shape[0]
    own_ref[...] = acc[pl.ds(0, size), :]
    for k, ref in enumerate(away_refs):
        ref[...] = acc[pl.ds((k + 1) * size, size), :].astype(ref.dtype)


def far_kernel(n_pieces, plan_ref, vals_ref, *refs):
    pieces, refs = refs[:n_pieces], refs[n_pieces:]
    table_ref, own_ref, *away_refs = refs[:5]
    vals, acc, prods, sems, sem_table = refs[5:]
    copies, start = [], 0
    for i, piece in enumerate(pieces):
        rows = piece.shape[0]
        copies.append(pltpu.make_async_copy(piece, table_ref.at[pl.ds(start, rows)], sem_table.at[i]))
        copies[-1].start()
        start += rows
    sum_tiles(0, plan_ref, vals_ref, table_ref, own_ref, away_refs, vals, acc, prods, sems,
              lambda: [copy.wait() for copy in copies])


def near_kernel(plan_ref, vals_ref, table_ref, own_ref, *refs):
    sum_tiles(1, plan_ref, vals_ref, table_ref, own_ref, refs[:3], *refs[3:])


def aggregate(kernel, plan, vals, pieces, out_rows, with_table):
    slots, tile, _ = vals.shape
    feat = pieces[0].shape[1]
    table_rows = sum(piece.shape[0] for piece in pieces)
    n_x = lax.axis_size("x")
    vmem = pl.BlockSpec(memory_space=pltpu.VMEM)
    shape = (out_rows // n_x, feat)
    out = [jax.ShapeDtypeStruct(shape, jnp.float32)] + [jax.ShapeDtypeStruct(shape, jnp.bfloat16)] * (n_x - 1)
    scratch = [
        pltpu.VMEM((slots, tile, tile), jnp.bfloat16),
        pltpu.VMEM((out_rows + tile, feat), jnp.float32),
        pltpu.VMEM((GROUP, tile, feat), jnp.float32),
        pltpu.SemaphoreType.DMA((slots // GROUP,)),
    ]
    if with_table:
        out = [jax.ShapeDtypeStruct((table_rows, feat), jnp.bfloat16)] + out
        scratch.append(pltpu.SemaphoreType.DMA((len(pieces),)))
    near = pl.BlockSpec(memory_space=pl.ANY) if with_table else vmem
    return pl.pallas_call(
        kernel,
        out_shape=out,
        in_specs=[pl.BlockSpec(memory_space=pltpu.SMEM), pl.BlockSpec(memory_space=pltpu.HBM)] + [near] * len(pieces),
        out_specs=[vmem] * len(out),
        scratch_shapes=scratch,
        compiler_params=pltpu.CompilerParams(vmem_limit_bytes=24 * 2**20),
        cost_estimate=pl.CostEstimate(flops=slots * tile * tile * feat, bytes_accessed=8 * 2**20, transcendentals=0),
        name="far_rows" if with_table else "near_rows",
    )(plan, vals, *pieces)


def head_kernel(scale, core_ref, own_ref, far_ref, *refs):
    *more_refs, weight_ref, labels_ref, logits_ref, keep_ref, give_ref = refs
    total = own_ref[...]
    for ref in more_refs:
        total += ref[...].astype(jnp.float32)
    total += far_ref[...].astype(jnp.float32)
    upper = total.astype(jnp.bfloat16)
    lower = (total - upper.astype(jnp.float32)).astype(jnp.bfloat16)
    weight = weight_ref[...]
    by_feature = (((1,), (1,)), ((), ()))
    logits = lax.dot_general(weight, upper, by_feature, preferred_element_type=jnp.float32)
    logits += lax.dot_general(weight, lower, by_feature, preferred_element_type=jnp.float32)
    logits_ref[...] = logits
    labels = labels_ref[...]
    classes = lax.broadcasted_iota(jnp.int32, logits.shape, 0)
    residual = logits - (labels == classes).astype(jnp.float32)
    residual = jnp.where(labels >= 0, residual, 0.0).astype(jnp.bfloat16)
    grad = jnp.dot(residual, upper, preferred_element_type=jnp.float32)
    grad += jnp.dot(residual, lower, preferred_element_type=jnp.float32)
    grad = grad * scale
    half = keep_ref.shape[0]
    first, second = grad[:half], grad[half:]
    second = jnp.concatenate([second, jnp.zeros((2 * half - grad.shape[0], grad.shape[1]), grad.dtype)], 0)
    swap = core_ref[0] == 1
    keep_ref[...] = jnp.where(swap, second, first)
    give_ref[...] = jnp.where(swap, first, second)


def head(core, own, far, more, weight, labels, scale):
    rows, feat = far.shape
    classes = weight.shape[0]
    half = (classes + 15) // 16 * 8
    vmem = pl.BlockSpec(memory_space=pltpu.VMEM)
    return pl.pallas_call(
        lambda *refs: head_kernel(scale, *refs),
        out_shape=(
            jax.ShapeDtypeStruct((classes, rows), jnp.float32),
            jax.ShapeDtypeStruct((half, feat), jnp.float32),
            jax.ShapeDtypeStruct((half, feat), jnp.float32),
        ),
        in_specs=[pl.BlockSpec(memory_space=pltpu.SMEM)] + [vmem] * (4 + len(more)),
        out_specs=(vmem, vmem, vmem),
        compiler_params=pltpu.CompilerParams(vmem_limit_bytes=32 * 2**20),
        name="head",
    )(core, own, far, *more, weight, labels)


def gather_features(features):
    by_z = jnp.concatenate([features] + [shift(features, "zl", -k) for k in (1, 2, 3)], 0)
    opposite = shift(features, "y", 2)
    opposite = jnp.concatenate([opposite] + [shift(opposite, "zl", -k) for k in (1, 2, 3)], 0)
    mine = [by_z, shift(by_z, "y", -1), opposite, shift(by_z, "y", 1)]
    return mine + [shift(piece, "core", 1) for piece in mine]


def sum_everywhere(keep, give, core, classes):
    total = keep + shift(give, "core", 1)
    for axis in ("y", "x"):
        total = total + shift(total, axis, 1) + shift(total, axis, 2) + shift(total, axis, 3)
    total = total + shift(total, "zh", 1)
    total = total + shift_z(total, 1) + shift_z(total, 2) + shift_z(total, -1)
    rest = shift(total, "core", 1)
    swap = core == 1
    return jnp.concatenate([jnp.where(swap, rest, total), jnp.where(swap, total, rest)], 0)[:classes]


def local(features, weight, labels, tile_rows, tile_cols, tile_count, tile_vals):
    tile = tile_vals.shape[-1]
    slots = tile_vals.shape[2]
    classes = weight.shape[1]
    nodes = features.shape[0]
    vals = pltpu.with_memory_space_constraint(tile_vals.reshape(slots, tile, tile), pltpu.HBM)
    out_rows = nodes * lax.axis_size("x")
    core = lax.axis_index("core").astype(jnp.int32)
    lists = plan(
        tile_rows.reshape(1, slots), tile_cols.reshape(1, slots), tile_count.reshape(()), nodes // tile, tile
    )

    pieces = gather_features(features)
    table, own, *away = aggregate(functools.partial(far_kernel, len(pieces)), lists, vals, pieces, out_rows, True)
    give = own + sum(shift(away[k], "x", k + 1).astype(jnp.float32) for k in (1, 0, 2))
    own, *away = aggregate(near_kernel, lists, vals, [table], out_rows, False)
    more = [shift(away[k], "x", k + 1) for k in (1, 0, 2)]
    far = shift(give.astype(jnp.bfloat16), "zh", 1)
    scale = 1.0 / math.sqrt(nodes * lax.axis_size(AXES))
    logits, keep, give = head(core.reshape(1), own, far, more, weight.T, labels.reshape(1, nodes), scale)
    return logits.T, sum_everywhere(keep, give, core, classes).T


def solution(mesh):
    fine = Mesh(mesh.devices.reshape(SIZES), AXES)
    placed = (
        P(COL + ROW, None),
        P(),
        P(AXES),
        P(ROW, COL, None),
        P(ROW, COL, None),
        P(ROW, COL),
        P(ROW, COL, None, None, None),
    )
    return jax.shard_map(
        local, mesh=fine, in_specs=placed, out_specs=(P(AXES, None), P()), check_vma=False
    )
```

time: 112 us -> 105 us (0.938)
  waiting for transfers between devices: 48.5 us -> 32.7 us
  Pallas kernels: 4.89 us -> 10.9 us
  starting transfers between devices: 51.5 us -> 56.3 us
  local copies, waits for them, and re-layouts: 4.87 us -> 2.35 us
    ppermute x26 -> x29, waiting for transfers between devices: 46.6 us -> 30.2 us  [shift(): return lax.ppermute(value, axes, [(i, (i + step) % n) for i in range(n)])]
    pallas_call x2 -> x3, Pallas kernels: 3.8 us -> 9.79 us  [the longest x2 8.14 us: aggregate(): pl.pallas_call(kernel, out_shape=out, in_specs=[pl.BlockSpec(memory_space...]
    ppermute x26 -> x29, starting transfers between devices: 48.2 us -> 51.9 us  [shift(): return lax.ppermute(value, axes, [(i, (i + step) % n) for i in range(n)])]
    unnamed x16 -> x12, local copies, waits for them, and re-layouts: 4.83 us -> 1.74 us
    ppermute x3, starting transfers between devices: 3.31 us -> 4.43 us  [shift_z(): lax.ppermute(value, ('zl', 'zh'), [(at(z), at((z + step) % n)) for z in r...]
  transfers between devices with their start and end apart: 29 -> 32, of which waited for: 17 -> 15; matrix products, arithmetic and copies ran while one was open for 1% -> 2% of each run, Pallas kernels for 0% -> 5%
where the time goes in v3:
time: 105 us; the launch traced here: 104 us
  starting transfers between devices  56.3 us (54%)
  waiting for transfers between devices  32.7 us (31%)
  Pallas kernels  10.9 us (10%)
  local copies, waits for them, and re-layouts  2.35 us (2%)
  between operations  1.46 us (1%)
    ppermute x29, starting transfers between devices, shift(): return lax.ppermute(value, axes, [(i, (i + step) % n) for i in range(n)])  51.9 us
    ppermute x29, waiting for transfers between devices, shift(): return lax.ppermute(value, axes, [(i, (i + step) % n) for i in range(n)])  30.2 us
    pallas_call x2, Pallas kernels, aggregate(): pl.pallas_call(kernel, out_shape=out, in_specs=[pl.BlockSpec(memory_space...  8.14 us
    ppermute x3, starting transfers between devices, shift_z(): lax.ppermute(value, ('zl', 'zh'), [(at(z), at((z + step) % n)) for z in r...  4.43 us
    ppermute x3, waiting for transfers between devices, shift_z(): lax.ppermute(value, ('zl', 'zh'), [(at(z), at((z + step) % n)) for z in r...  2.45 us
  transfers between devices with their start and end apart: 32, of which 15 were waited for; matrix products, arithmetic and copies ran while one was open for 2% of the time, Pallas kernels for 5%

profile of v3, /device:TPU:1, one launch (start us, length us, event | category | flops | bytes accessed | tf_op | source)
XLA Modules:
  0.0 104.5 jit_solution(16417047768011179701)
XLA Ops:
  0.6 5.3 %collective-permute-start = (bf16[512,128]{1,0:T(8,128)(2,1)}, bf16[512,128]{1,0:T(8,128)(2,1)S(1)}, u32[]{:S(2)}, u32[]{:S(2)}) collective-permute-start(bf16[512,128]{1,0:T(8,128)(2,1)} %param.7), channel_id=1, source_target_pairs={{0,48},{16,0},{32,16},{48,32},{1,49},{17,1},{33,17},{49,33},{2,50}... | collective-permute-start | bytes 393224 | tf_op jit(solution)/shard_map/ppermute | solution.py:20
  5.9 2.9 %collective-permute-start.4 = (bf16[512,128]{1,0:T(8,128)(2,1)}, bf16[512,128]{1,0:T(8,128)(2,1)S(1)}, u32[]{:S(2)}, u32[]{:S(2)}) collective-permute-start(bf16[512,128]{1,0:T(8,128)(2,1)} %param.7), channel_id=1, source_target_pairs={{0,128},{64,192},{128,0},{192,64},{1,129},{65,193},{129,1},{193,65... | collective-permute-start | bytes 393224 | tf_op jit(solution)/shard_map/ppermute | solution.py:20
  10.2 8.3 %collective-permute-done.1 = bf16[512,128]{1,0:T(8,128)(2,1)S(1)} collective-permute-done((bf16[512,128]{1,0:T(8,128)(2,1)}, bf16[512,128]{1,0:T(8,128)(2,1)S(1)}, u32[]{:S(2)}, u32[]{:S(2)}) %collective-permute-start.1) | collective-permute-done | bytes 131104 | tf_op jit(solution)/shard_map/ppermute | solution.py:20
  18.5 2.4 %collective-permute-start.3 = (bf16[2048,128]{1,0:T(8,128)(2,1)S(1)}, bf16[2048,128]{1,0:T(8,128)(2,1)S(1)}, u32[]{:S(2)}, u32[]{:S(2)}) collective-permute-start(bf16[2048,128]{1,0:T(8,128)(2,1)S(1)} %constant_dynamic-update-slice_fusion.refs_0_), channel_id=1, source_target_pairs={{0,192},{64,0},{128,64},{192,128},{1,193},{65,1},{129,65},{193,129... | collective-permute-start | bytes 1572872 | tf_op jit(solution)/shard_map/ppermute | solution.py:20
  21.8 1.1 %collective-permute-start.9 = (bf16[2048,128]{1,0:T(8,128)(2,1)S(1)}, bf16[2048,128]{1,0:T(8,128)(2,1)S(1)}, u32[]{:S(2)}, u32[]{:S(2)}) collective-permute-start(bf16[2048,128]{1,0:T(8,128)(2,1)S(1)} %constant_dynamic-update-slice_fusion.refs_0_), channel_id=1, source_target_pairs={{0,8},{8,0},{1,9},{9,1},{2,10},{10,2},{3,11},{11,3},{4,12},{12,4},... | collective-permute-start | bytes 1572872 | tf_op jit(solution)/shard_map/ppermute | solution.py:20
  22.9 1.6 %collective-permute-start.6 = (bf16[512,128]{1,0:T(8,128)(2,1)S(1)}, bf16[512,128]{1,0:T(8,128)(2,1)S(1)}, u32[]{:S(2)}, u32[]{:S(2)}) collective-permute-start(bf16[512,128]{1,0:T(8,128)(2,1)S(1)} %collective-permute-done.4), channel_id=1, source_target_pairs={{0,32},{16,48},{32,0},{48,16},{1,33},{17,49},{33,1},{49,17},{2,34}... | collective-permute-start | bytes 393224 | tf_op jit(solution)/shard_map/ppermute | solution.py:20
  25.0 2.1 %collective-permute-start.7 = (bf16[512,128]{1,0:T(8,128)(2,1)S(1)}, bf16[512,128]{1,0:T(8,128)(2,1)S(1)}, u32[]{:S(2)}, u32[]{:S(2)}) collective-permute-start(bf16[512,128]{1,0:T(8,128)(2,1)S(1)} %collective-permute-done.4), channel_id=1, source_target_pairs={{0,16},{16,32},{32,48},{48,0},{1,17},{17,33},{33,49},{49,1},{2,18}... | collective-permute-start | bytes 393224 | tf_op jit(solution)/shard_map/ppermute | solution.py:20
  27.1 8.1 %collective-permute-done.6 = bf16[512,128]{1,0:T(8,128)(2,1)S(1)} collective-permute-done((bf16[512,128]{1,0:T(8,128)(2,1)S(1)}, bf16[512,128]{1,0:T(8,128)(2,1)S(1)}, u32[]{:S(2)}, u32[]{:S(2)}) %collective-permute-start.6) | collective-permute-done | bytes 131104 | tf_op jit(solution)/shard_map/ppermute | solution.py:20
  35.3 1.4 %collective-permute-start.11 = (bf16[2048,128]{1,0:T(8,128)(2,1)S(1)}, bf16[2048,128]{1,0:T(8,128)(2,1)S(1)}, u32[]{:S(2)}, u32[]{:S(2)}) collective-permute-start(bf16[2048,128]{1,0:T(8,128)(2,1)S(1)} %constant_dynamic-update-slice_fusion.4.refs_2_), channel_id=1, source_target_pairs={{0,8},{8,0},{1,9},{9,1},{2,10},{10,2},{3,11},{11,3},{4,12},{12,4},... | collective-permute-start | bytes 1572872 | tf_op jit(solution)/shard_map/ppermute | solution.py:20
  38.4 1.6 %plan.1.plan_ref = s32[8,256]{1,0:T(8,128)} custom-call(s32[6]{0:T(128)} %stack.20.refs_0_, s32[1,256]{1,0:T(1,128)} %bitcast.19, s32[1,256]{1,0:T(1,128)} %bitcast.20), custom_call_target="tpu_custom_call" | custom-call | tf_op jit(solution)/shard_map/plan/pallas_call | solution.py:65
  40.8 4.4 %far_rows.1 = (bf16[16384,128]{1,0:T(8,128)(2,1)S(1)}, f32[512,128]{1,0:T(8,128)S(1)}, bf16[512,128]{1,0:T(8,128)(2,1)S(1)}, bf16[512,128]{1,0:T(8,128)(2,1)S(1)}, bf16[512,128]{1,0:T(8,128)(2,1)S(1)}) custom-call(s32[8,256]{1,0:T(8,128)S(1)} %copy-done, bf16[256,128,128]{2,1,0:T(8,128)(2,1)} %bitcast.17, ...), custom_call_target="tpu_custom_call" | custom-call | flops 536870912 | bytes 8388608 | tf_op jit(solution)/shard_map/far_rows/pallas_call | solution.py:144
  45.2 2.6 %collective-permute-start.13 = (bf16[512,128]{1,0:T(8,128)(2,1)S(1)}, bf16[512,128]{1,0:T(8,128)(2,1)S(1)}, u32[]{:S(2)}, u32[]{:S(2)}) collective-permute-start(bf16[512,128]{1,0:T(8,128)(2,1)S(1)} %get-tuple-element.17), channel_id=1, source_target_pairs={{0,4},{2,6},{4,0},{6,2},{1,5},{3,7},{5,1},{7,3},{8,12},{10,14},{12... | collective-permute-start | bytes 393224 | tf_op jit(solution)/shard_map/ppermute | solution.py:20
  48.1 2.4 %collective-permute-start.15 = (bf16[512,128]{1,0:T(8,128)(2,1)S(1)}, bf16[512,128]{1,0:T(8,128)(2,1)S(1)}, u32[]{:S(2)}, u32[]{:S(2)}) collective-permute-start(bf16[512,128]{1,0:T(8,128)(2,1)S(1)} %get-tuple-element.19), channel_id=1, source_target_pairs={{0,6},{2,0},{4,2},{6,4},{1,7},{3,1},{5,3},{7,5},{8,14},{10,8},{12,... | collective-permute-start | bytes 393224 | tf_op jit(solution)/shard_map/ppermute | solution.py:20
  50.5 3.8 %near_rows.1 = (f32[512,128]{1,0:T(8,128)S(1)}, bf16[512,128]{1,0:T(8,128)(2,1)S(1)}, bf16[512,128]{1,0:T(8,128)(2,1)S(1)}, bf16[512,128]{1,0:T(8,128)(2,1)S(1)}) custom-call(s32[8,256]{1,0:T(8,128)S(1)} %copy-done, bf16[256,128,128]{2,1,0:T(8,128)(2,1)} %bitcast.18, bf16[16384,128]{1,0:T(8,128)(2,1)S(1)} %get-tuple-element.14.table_ref), custom_call_target="tpu_custom_call" | custom-call | flops 536870912 | bytes 8388608 | tf_op jit(solution)/shard_map/near_rows/pallas_call | solution.py:144
  55.1 2.2 %collective-permute-start.19 = (bf16[512,128]{1,0:T(8,128)(2,1)S(1)}, bf16[512,128]{1,0:T(8,128)(2,1)S(1)}, u32[]{:S(2)}, u32[]{:S(2)}) collective-permute-start(bf16[512,128]{1,0:T(8,128)(2,1)S(1)} %get-tuple-element.22), channel_id=1, source_target_pairs={{0,6},{2,0},{4,2},{6,4},{1,7},{3,1},{5,3},{7,5},{8,14},{10,8},{12,... | collective-permute-start | bytes 393224 | tf_op jit(solution)/shard_map/ppermute | solution.py:20
  57.4 4.3 %collective-permute-start.16 = (bf16[512,128]{1,0:T(8,128)(2,1)S(1)}, bf16[512,128]{1,0:T(8,128)(2,1)S(1)}, u32[]{:S(2)}, u32[]{:S(2)}) collective-permute-start(bf16[512,128]{1,0:T(8,128)(2,1)S(1)} %add_convert_fusion), channel_id=1, source_target_pairs={{0,1},{1,0},{2,3},{3,2},{4,5},{5,4},{6,7},{7,6},{8,9},{9,8},{10,11... | collective-permute-start | bytes 393224 | tf_op jit(solution)/shard_map/ppermute | solution.py:20
  61.7 2.5 %collective-permute-done.18.refs_4_ = bf16[512,128]{1,0:T(8,128)(2,1)S(1)} collective-permute-done((bf16[512,128]{1,0:T(8,128)(2,1)S(1)}, bf16[512,128]{1,0:T(8,128)(2,1)S(1)}, u32[]{:S(2)}, u32[]{:S(2)}) %collective-permute-start.18) | collective-permute-done | bytes 131104 | tf_op jit(solution)/shard_map/ppermute | solution.py:20
  64.2 2.3 %collective-permute-done.16.refs_2_ = bf16[512,128]{1,0:T(8,128)(2,1)S(1)} collective-permute-done((bf16[512,128]{1,0:T(8,128)(2,1)S(1)}, bf16[512,128]{1,0:T(8,128)(2,1)S(1)}, u32[]{:S(2)}, u32[]{:S(2)}) %collective-permute-start.16) | collective-permute-done | bytes 131104 | tf_op jit(solution)/shard_map/ppermute | solution.py:20
  66.5 1.1 %head.1 = (f32[172,512]{1,0:T(8,128)}, f32[88,128]{1,0:T(8,128)S(1)}, f32[88,128]{1,0:T(8,128)S(1)}) custom-call(s32[1]{0:T(128)} %bitcast.refs_0_, f32[512,128]{1,0:T(8,128)S(1)} %get-tuple-element.15.refs_1_, bf16[512,128]{1,0:T(8,128)(2,1)S(1)} %collective-permute-done.16.refs_2_, bf16[512,128]{1,0:T(8,128)(2,1)S(1)} %collective-permute-done.17.refs_3_, ...), custom_call_target="tpu_custom_call" | custom-call | tf_op jit(solution)/shard_map/head/pallas_call | solution.py:189
  67.6 1.0 collective-permute-start.20
  70.0 4.2 %collective-permute-start.22 = (f32[88,128]{1,0:T(8,128)S(1)}, f32[88,128]{1,0:T(8,128)S(1)}, u32[]{:S(2)}, u32[]{:S(2)}) collective-permute-start(f32[88,128]{1,0:T(8,128)S(1)} %add.45), channel_id=1, source_target_pairs={{0,128},{64,192},{128,0},{192,64},{1,129},{65,193},{129,1},{193,65... | collective-permute-start | bytes 135176 | tf_op jit(solution)/shard_map/ppermute | solution.py:20
  74.5 1.8 %collective-permute-done.22 = f32[88,128]{1,0:T(8,128)S(1)} collective-permute-done((f32[88,128]{1,0:T(8,128)S(1)}, f32[88,128]{1,0:T(8,128)S(1)}, u32[]{:S(2)}, u32[]{:S(2)}) %collective-permute-start.22) | collective-permute-done | bytes 45088 | tf_op jit(solution)/shard_map/ppermute | solution.py:20
  76.3 1.2 %collective-permute-done.23 = f32[88,128]{1,0:T(8,128)S(1)} collective-permute-done((f32[88,128]{1,0:T(8,128)S(1)}, f32[88,128]{1,0:T(8,128)S(1)}, u32[]{:S(2)}, u32[]{:S(2)}) %collective-permute-start.23) | collective-permute-done | bytes 45088 | tf_op jit(solution)/shard_map/ppermute | solution.py:20
  77.5 2.3 %collective-permute-start.25 = (f32[88,128]{1,0:T(8,128)S(1)}, f32[88,128]{1,0:T(8,128)S(1)}, u32[]{:S(2)}, u32[]{:S(2)}) collective-permute-start(f32[88,128]{1,0:T(8,128)S(1)} %add_add_fusion.2), channel_id=1, source_target_pairs={{0,4},{2,6},{4,0},{6,2},{1,5},{3,7},{5,1},{7,3},{8,12},{10,14},{12... | collective-permute-start | bytes 135176 | tf_op jit(solution)/shard_map/ppermute | solution.py:20
  79.9 1.8 %collective-permute-start.26 = (f32[88,128]{1,0:T(8,128)S(1)}, f32[88,128]{1,0:T(8,128)S(1)}, u32[]{:S(2)}, u32[]{:S(2)}) collective-permute-start(f32[88,128]{1,0:T(8,128)S(1)} %add_add_fusion.2), channel_id=1, source_target_pairs={{0,6},{2,0},{4,2},{6,4},{1,7},{3,1},{5,3},{7,5},{8,14},{10,8},{12,... | collective-permute-start | bytes 135176 | tf_op jit(solution)/shard_map/ppermute | solution.py:20
  82.8 4.4 %collective-permute-start.27 = (f32[88,128]{1,0:T(8,128)S(1)}, f32[88,128]{1,0:T(8,128)S(1)}, u32[]{:S(2)}, u32[]{:S(2)}) collective-permute-start(f32[88,128]{1,0:T(8,128)S(1)} %add_add_fusion.1), channel_id=1, source_target_pairs={{0,1},{1,0},{2,3},{3,2},{4,5},{5,4},{6,7},{7,6},{8,9},{9,8},{10,11... | collective-permute-start | bytes 135176 | tf_op jit(solution)/shard_map/ppermute | solution.py:20
  87.2 2.5 %collective-permute-done.27 = f32[88,128]{1,0:T(8,128)S(1)} collective-permute-done((f32[88,128]{1,0:T(8,128)S(1)}, f32[88,128]{1,0:T(8,128)S(1)}, u32[]{:S(2)}, u32[]{:S(2)}) %collective-permute-start.27) | collective-permute-done | bytes 45088 | tf_op jit(solution)/shard_map/ppermute | solution.py:20
  89.8 1.8 %collective-permute-start.29 = (f32[88,128]{1,0:T(8,128)S(1)}, f32[88,128]{1,0:T(8,128)S(1)}, u32[]{:S(2)}, u32[]{:S(2)}) collective-permute-start(f32[88,128]{1,0:T(8,128)S(1)} %add.52), channel_id=1, source_target_pairs={{0,32},{16,48},{32,1},{48,17},{1,33},{17,49},{33,0},{49,16},{2,34}... | collective-permute-start | bytes 135176 | tf_op jit(solution)/shard_map/ppermute | solution.py:27
  91.5 2.6 %collective-permute-start.30 = (f32[88,128]{1,0:T(8,128)S(1)}, f32[88,128]{1,0:T(8,128)S(1)}, u32[]{:S(2)}, u32[]{:S(2)}) collective-permute-start(f32[88,128]{1,0:T(8,128)S(1)} %add.52), channel_id=1, source_target_pairs={{0,49},{16,0},{32,16},{48,32},{1,48},{17,1},{33,17},{49,33},{2,51}... | collective-permute-start | bytes 135176 | tf_op jit(solution)/shard_map/ppermute | solution.py:27
  94.2 1.2 %collective-permute-done.29 = f32[88,128]{1,0:T(8,128)S(1)} collective-permute-done((f32[88,128]{1,0:T(8,128)S(1)}, f32[88,128]{1,0:T(8,128)S(1)}, u32[]{:S(2)}, u32[]{:S(2)}) %collective-permute-start.29) | collective-permute-done | bytes 45088 | tf_op jit(solution)/shard_map/ppermute | solution.py:27
  95.4 1.2 %collective-permute-done.30 = f32[88,128]{1,0:T(8,128)S(1)} collective-permute-done((f32[88,128]{1,0:T(8,128)S(1)}, f32[88,128]{1,0:T(8,128)S(1)}, u32[]{:S(2)}, u32[]{:S(2)}) %collective-permute-start.30) | collective-permute-done | bytes 45088 | tf_op jit(solution)/shard_map/ppermute | solution.py:27
  96.6 6.4 %collective-permute-start.31 = (f32[88,128]{1,0:T(8,128)S(1)}, f32[88,128]{1,0:T(8,128)S(1)}, u32[]{:S(2)}, u32[]{:S(2)}) collective-permute-start(f32[88,128]{1,0:T(8,128)S(1)} %add_add_fusion), channel_id=1, source_target_pairs={{0,8},{8,0},{1,9},{9,1},{2,10},{10,2},{3,11},{11,3},{4,12},{12,4},... | collective-permute-start | bytes 135176 | tf_op jit(solution)/shard_map/ppermute | solution.py:20
  (59 shorter events, 10.5 us)
Async XLA Ops:
  0.6 9.5 %collective-permute-start = (bf16[512,128]{1,0:T(8,128)(2,1)}, bf16[512,128]{1,0:T(8,128)(2,1)S(1)}, u32[]{:S(2)}, u32[]{:S(2)}) collective-permute-start(bf16[512,128]{1,0:T(8,128)(2,1)} %param.7), channel_id=1, source_target_pairs={{0,48},{16,0},{32,16},{48,32},{1,49},{17,1},{33,17},{49,33},{2,50}... | collective-permute-start | bytes 393224 | tf_op jit(solution)/shard_map/ppermute | solution.py:20
  5.9 15.0 %collective-permute-start.4 = (bf16[512,128]{1,0:T(8,128)(2,1)}, bf16[512,128]{1,0:T(8,128)(2,1)S(1)}, u32[]{:S(2)}, u32[]{:S(2)}) collective-permute-start(bf16[512,128]{1,0:T(8,128)(2,1)} %param.7), channel_id=1, source_target_pairs={{0,128},{64,192},{128,0},{192,64},{1,129},{65,193},{129,1},{193,65... | collective-permute-start | bytes 393224 | tf_op jit(solution)/shard_map/ppermute | solution.py:20
  8.8 9.7 %collective-permute-start.1 = (bf16[512,128]{1,0:T(8,128)(2,1)}, bf16[512,128]{1,0:T(8,128)(2,1)S(1)}, u32[]{:S(2)}, u32[]{:S(2)}) collective-permute-start(bf16[512,128]{1,0:T(8,128)(2,1)} %param.7), channel_id=1, source_target_pairs={{0,32},{16,48},{32,0},{48,16},{1,33},{17,49},{33,1},{49,17},{2,34}... | collective-permute-start | bytes 393224 | tf_op jit(solution)/shard_map/ppermute | solution.py:20
  8.8 9.7 %collective-permute-start.2 = (bf16[512,128]{1,0:T(8,128)(2,1)}, bf16[512,128]{1,0:T(8,128)(2,1)S(1)}, u32[]{:S(2)}, u32[]{:S(2)}) collective-permute-start(bf16[512,128]{1,0:T(8,128)(2,1)} %param.7), channel_id=1, source_target_pairs={{0,16},{16,32},{32,48},{48,0},{1,17},{17,33},{33,49},{49,1},{2,18}... | collective-permute-start | bytes 393224 | tf_op jit(solution)/shard_map/ppermute | solution.py:20
  18.5 18.2 %collective-permute-start.3 = (bf16[2048,128]{1,0:T(8,128)(2,1)S(1)}, bf16[2048,128]{1,0:T(8,128)(2,1)S(1)}, u32[]{:S(2)}, u32[]{:S(2)}) collective-permute-start(bf16[2048,128]{1,0:T(8,128)(2,1)S(1)} %constant_dynamic-update-slice_fusion.refs_0_), channel_id=1, source_target_pairs={{0,192},{64,0},{128,64},{192,128},{1,193},{65,1},{129,65},{193,129... | collective-permute-start | bytes 1572872 | tf_op jit(solution)/shard_map/ppermute | solution.py:20
  20.9 15.9 %collective-permute-start.8 = (bf16[2048,128]{1,0:T(8,128)(2,1)S(1)}, bf16[2048,128]{1,0:T(8,128)(2,1)S(1)}, u32[]{:S(2)}, u32[]{:S(2)}) collective-permute-start(bf16[2048,128]{1,0:T(8,128)(2,1)S(1)} %constant_dynamic-update-slice_fusion.refs_0_), channel_id=1, source_target_pairs={{0,64},{64,128},{128,192},{192,0},{1,65},{65,129},{129,193},{193,1... | collective-permute-start | bytes 1572872 | tf_op jit(solution)/shard_map/ppermute | solution.py:20
  20.9 4.1 %collective-permute-start.5 = (bf16[512,128]{1,0:T(8,128)(2,1)S(1)}, bf16[512,128]{1,0:T(8,128)(2,1)S(1)}, u32[]{:S(2)}, u32[]{:S(2)}) collective-permute-start(bf16[512,128]{1,0:T(8,128)(2,1)S(1)} %collective-permute-done.4), channel_id=1, source_target_pairs={{0,48},{16,0},{32,16},{48,32},{1,49},{17,1},{33,17},{49,33},{2,50}... | collective-permute-start | bytes 393224 | tf_op jit(solution)/shard_map/ppermute | solution.py:20
  21.8 18.3 %collective-permute-start.9 = (bf16[2048,128]{1,0:T(8,128)(2,1)S(1)}, bf16[2048,128]{1,0:T(8,128)(2,1)S(1)}, u32[]{:S(2)}, u32[]{:S(2)}) collective-permute-start(bf16[2048,128]{1,0:T(8,128)(2,1)S(1)} %constant_dynamic-update-slice_fusion.refs_0_), channel_id=1, source_target_pairs={{0,8},{8,0},{1,9},{9,1},{2,10},{10,2},{3,11},{11,3},{4,12},{12,4},... | collective-permute-start | bytes 1572872 | tf_op jit(solution)/shard_map/ppermute | solution.py:20
  22.9 12.3 %collective-permute-start.6 = (bf16[512,128]{1,0:T(8,128)(2,1)S(1)}, bf16[512,128]{1,0:T(8,128)(2,1)S(1)}, u32[]{:S(2)}, u32[]{:S(2)}) collective-permute-start(bf16[512,128]{1,0:T(8,128)(2,1)S(1)} %collective-permute-done.4), channel_id=1, source_target_pairs={{0,32},{16,48},{32,0},{48,16},{1,33},{17,49},{33,1},{49,17},{2,34}... | collective-permute-start | bytes 393224 | tf_op jit(solution)/shard_map/ppermute | solution.py:20
  25.0 10.2 %collective-permute-start.7 = (bf16[512,128]{1,0:T(8,128)(2,1)S(1)}, bf16[512,128]{1,0:T(8,128)(2,1)S(1)}, u32[]{:S(2)}, u32[]{:S(2)}) collective-permute-start(bf16[512,128]{1,0:T(8,128)(2,1)S(1)} %collective-permute-done.4), channel_id=1, source_target_pairs={{0,16},{16,32},{32,48},{48,0},{1,17},{17,33},{33,49},{49,1},{2,18}... | collective-permute-start | bytes 393224 | tf_op jit(solution)/shard_map/ppermute | solution.py:20
  35.3 4.8 %collective-permute-start.11 = (bf16[2048,128]{1,0:T(8,128)(2,1)S(1)}, bf16[2048,128]{1,0:T(8,128)(2,1)S(1)}, u32[]{:S(2)}, u32[]{:S(2)}) collective-permute-start(bf16[2048,128]{1,0:T(8,128)(2,1)S(1)} %constant_dynamic-update-slice_fusion.4.refs_2_), channel_id=1, source_target_pairs={{0,8},{8,0},{1,9},{9,1},{2,10},{10,2},{3,11},{11,3},{4,12},{12,4},... | collective-permute-start | bytes 1572872 | tf_op jit(solution)/shard_map/ppermute | solution.py:20
  36.7 3.4 %collective-permute-start.10 = (bf16[2048,128]{1,0:T(8,128)(2,1)S(1)}, bf16[2048,128]{1,0:T(8,128)(2,1)}, u32[]{:S(2)}, u32[]{:S(2)}) collective-permute-start(bf16[2048,128]{1,0:T(8,128)(2,1)S(1)} %collective-permute-done.3.refs_1_), channel_id=1, source_target_pairs={{0,8},{8,0},{1,9},{9,1},{2,10},{10,2},{3,11},{11,3},{4,12},{12,4},... | collective-permute-start | bytes 1572872 | tf_op jit(solution)/shard_map/ppermute | solution.py:20
  36.8 3.3 %collective-permute-start.12 = (bf16[2048,128]{1,0:T(8,128)(2,1)S(1)}, bf16[2048,128]{1,0:T(8,128)(2,1)}, u32[]{:S(2)}, u32[]{:S(2)}) collective-permute-start(bf16[2048,128]{1,0:T(8,128)(2,1)S(1)} %collective-permute-done.8.refs_3_), channel_id=1, source_target_pairs={{0,8},{8,0},{1,9},{9,1},{2,10},{10,2},{3,11},{11,3},{4,12},{12,4},... | collective-permute-start | bytes 1572872 | tf_op jit(solution)/shard_map/ppermute | solution.py:20
  45.2 9.9 %collective-permute-start.13 = (bf16[512,128]{1,0:T(8,128)(2,1)S(1)}, bf16[512,128]{1,0:T(8,128)(2,1)S(1)}, u32[]{:S(2)}, u32[]{:S(2)}) collective-permute-start(bf16[512,128]{1,0:T(8,128)(2,1)S(1)} %get-tuple-element.17), channel_id=1, source_target_pairs={{0,4},{2,6},{4,0},{6,2},{1,5},{3,7},{5,1},{7,3},{8,12},{10,14},{12... | collective-permute-start | bytes 393224 | tf_op jit(solution)/shard_map/ppermute | solution.py:20
  47.8 9.5 %collective-permute-start.14 = (bf16[512,128]{1,0:T(8,128)(2,1)S(1)}, bf16[512,128]{1,0:T(8,128)(2,1)S(1)}, u32[]{:S(2)}, u32[]{:S(2)}) collective-permute-start(bf16[512,128]{1,0:T(8,128)(2,1)S(1)} %get-tuple-element.18), channel_id=1, source_target_pairs={{0,2},{2,4},{4,6},{6,0},{1,3},{3,5},{5,7},{7,1},{8,10},{10,12},{12... | collective-permute-start | bytes 393224 | tf_op jit(solution)/shard_map/ppermute | solution.py:20
  48.1 9.2 %collective-permute-start.15 = (bf16[512,128]{1,0:T(8,128)(2,1)S(1)}, bf16[512,128]{1,0:T(8,128)(2,1)S(1)}, u32[]{:S(2)}, u32[]{:S(2)}) collective-permute-start(bf16[512,128]{1,0:T(8,128)(2,1)S(1)} %get-tuple-element.19), channel_id=1, source_target_pairs={{0,6},{2,0},{4,2},{6,4},{1,7},{3,1},{5,3},{7,5},{8,14},{10,8},{12,... | collective-permute-start | bytes 393224 | tf_op jit(solution)/shard_map/ppermute | solution.py:20
  54.3 7.4 %collective-permute-start.17 = (bf16[512,128]{1,0:T(8,128)(2,1)S(1)}, bf16[512,128]{1,0:T(8,128)(2,1)S(1)}, u32[]{:S(2)}, u32[]{:S(2)}) collective-permute-start(bf16[512,128]{1,0:T(8,128)(2,1)S(1)} %get-tuple-element.20), channel_id=1, source_target_pairs={{0,4},{2,6},{4,0},{6,2},{1,5},{3,7},{5,1},{7,3},{8,12},{10,14},{12... | collective-permute-start | bytes 393224 | tf_op jit(solution)/shard_map/ppermute | solution.py:20
  54.6 9.6 %collective-permute-start.18 = (bf16[512,128]{1,0:T(8,128)(2,1)S(1)}, bf16[512,128]{1,0:T(8,128)(2,1)S(1)}, u32[]{:S(2)}, u32[]{:S(2)}) collective-permute-start(bf16[512,128]{1,0:T(8,128)(2,1)S(1)} %get-tuple-element.21), channel_id=1, source_target_pairs={{0,2},{2,4},{4,6},{6,0},{1,3},{3,5},{5,7},{7,1},{8,10},{10,12},{12... | collective-permute-start | bytes 393224 | tf_op jit(solution)/shard_map/ppermute | solution.py:20
  55.1 9.0 %collective-permute-start.19 = (bf16[512,128]{1,0:T(8,128)(2,1)S(1)}, bf16[512,128]{1,0:T(8,128)(2,1)S(1)}, u32[]{:S(2)}, u32[]{:S(2)}) collective-permute-start(bf16[512,128]{1,0:T(8,128)(2,1)S(1)} %get-tuple-element.22), channel_id=1, source_target_pairs={{0,6},{2,0},{4,2},{6,4},{1,7},{3,1},{5,3},{7,5},{8,14},{10,8},{12,... | collective-permute-start | bytes 393224 | tf_op jit(solution)/shard_map/ppermute | solution.py:20
  57.4 9.1 %collective-permute-start.16 = (bf16[512,128]{1,0:T(8,128)(2,1)S(1)}, bf16[512,128]{1,0:T(8,128)(2,1)S(1)}, u32[]{:S(2)}, u32[]{:S(2)}) collective-permute-start(bf16[512,128]{1,0:T(8,128)(2,1)S(1)} %add_convert_fusion), channel_id=1, source_target_pairs={{0,1},{1,0},{2,3},{3,2},{4,5},{5,4},{6,7},{7,6},{8,9},{9,8},{10,11... | collective-permute-start | bytes 393224 | tf_op jit(solution)/shard_map/ppermute | solution.py:20
  67.6 1.8 %collective-permute-start.20 = (f32[88,128]{1,0:T(8,128)S(1)}, f32[88,128]{1,0:T(8,128)S(1)}, u32[]{:S(2)}, u32[]{:S(2)}) collective-permute-start(f32[88,128]{1,0:T(8,128)S(1)} %get-tuple-element.25), channel_id=1, source_target_pairs={{0,8},{8,0},{1,9},{9,1},{2,10},{10,2},{3,11},{11,3},{4,12},{12,4},... | collective-permute-start | bytes 135176 | tf_op jit(solution)/shard_map/ppermute | solution.py:20
  69.4 5.1 %collective-permute-start.21 = (f32[88,128]{1,0:T(8,128)S(1)}, f32[88,128]{1,0:T(8,128)S(1)}, u32[]{:S(2)}, u32[]{:S(2)}) collective-permute-start(f32[88,128]{1,0:T(8,128)S(1)} %add.45), channel_id=1, source_target_pairs={{0,64},{64,128},{128,192},{192,0},{1,65},{65,129},{129,193},{193,1... | collective-permute-start | bytes 135176 | tf_op jit(solution)/shard_map/ppermute | solution.py:20
  70.0 6.3 %collective-permute-start.22 = (f32[88,128]{1,0:T(8,128)S(1)}, f32[88,128]{1,0:T(8,128)S(1)}, u32[]{:S(2)}, u32[]{:S(2)}) collective-permute-start(f32[88,128]{1,0:T(8,128)S(1)} %add.45), channel_id=1, source_target_pairs={{0,128},{64,192},{128,0},{192,64},{1,129},{65,193},{129,1},{193,65... | collective-permute-start | bytes 135176 | tf_op jit(solution)/shard_map/ppermute | solution.py:20
  74.3 3.2 %collective-permute-start.23 = (f32[88,128]{1,0:T(8,128)S(1)}, f32[88,128]{1,0:T(8,128)S(1)}, u32[]{:S(2)}, u32[]{:S(2)}) collective-permute-start(f32[88,128]{1,0:T(8,128)S(1)} %add.45), channel_id=1, source_target_pairs={{0,192},{64,0},{128,64},{192,128},{1,193},{65,1},{129,65},{193,129... | collective-permute-start | bytes 135176 | tf_op jit(solution)/shard_map/ppermute | solution.py:20
  77.4 4.2 %collective-permute-start.24 = (f32[88,128]{1,0:T(8,128)S(1)}, f32[88,128]{1,0:T(8,128)S(1)}, u32[]{:S(2)}, u32[]{:S(2)}) collective-permute-start(f32[88,128]{1,0:T(8,128)S(1)} %add_add_fusion.2), channel_id=1, source_target_pairs={{0,2},{2,4},{4,6},{6,0},{1,3},{3,5},{5,7},{7,1},{8,10},{10,12},{12... | collective-permute-start | bytes 135176 | tf_op jit(solution)/shard_map/ppermute | solution.py:20
  77.5 4.6 %collective-permute-start.25 = (f32[88,128]{1,0:T(8,128)S(1)}, f32[88,128]{1,0:T(8,128)S(1)}, u32[]{:S(2)}, u32[]{:S(2)}) collective-permute-start(f32[88,128]{1,0:T(8,128)S(1)} %add_add_fusion.2), channel_id=1, source_target_pairs={{0,4},{2,6},{4,0},{6,2},{1,5},{3,7},{5,1},{7,3},{8,12},{10,14},{12... | collective-permute-start | bytes 135176 | tf_op jit(solution)/shard_map/ppermute | solution.py:20
  79.9 2.9 %collective-permute-start.26 = (f32[88,128]{1,0:T(8,128)S(1)}, f32[88,128]{1,0:T(8,128)S(1)}, u32[]{:S(2)}, u32[]{:S(2)}) collective-permute-start(f32[88,128]{1,0:T(8,128)S(1)} %add_add_fusion.2), channel_id=1, source_target_pairs={{0,6},{2,0},{4,2},{6,4},{1,7},{3,1},{5,3},{7,5},{8,14},{10,8},{12,... | collective-permute-start | bytes 135176 | tf_op jit(solution)/shard_map/ppermute | solution.py:20
  82.8 6.9 %collective-permute-start.27 = (f32[88,128]{1,0:T(8,128)S(1)}, f32[88,128]{1,0:T(8,128)S(1)}, u32[]{:S(2)}, u32[]{:S(2)}) collective-permute-start(f32[88,128]{1,0:T(8,128)S(1)} %add_add_fusion.1), channel_id=1, source_target_pairs={{0,1},{1,0},{2,3},{3,2},{4,5},{5,4},{6,7},{7,6},{8,9},{9,8},{10,11... | collective-permute-start | bytes 135176 | tf_op jit(solution)/shard_map/ppermute | solution.py:20
  89.7 4.5 %collective-permute-start.28 = (f32[88,128]{1,0:T(8,128)S(1)}, f32[88,128]{1,0:T(8,128)S(1)}, u32[]{:S(2)}, u32[]{:S(2)}) collective-permute-start(f32[88,128]{1,0:T(8,128)S(1)} %add.52), channel_id=1, source_target_pairs={{0,16},{16,32},{32,48},{48,1},{1,17},{17,33},{33,49},{49,0},{2,18}... | collective-permute-start | bytes 135176 | tf_op jit(solution)/shard_map/ppermute | solution.py:27
  89.8 5.6 %collective-permute-start.29 = (f32[88,128]{1,0:T(8,128)S(1)}, f32[88,128]{1,0:T(8,128)S(1)}, u32[]{:S(2)}, u32[]{:S(2)}) collective-permute-start(f32[88,128]{1,0:T(8,128)S(1)} %add.52), channel_id=1, source_target_pairs={{0,32},{16,48},{32,1},{48,17},{1,33},{17,49},{33,0},{49,16},{2,34}... | collective-permute-start | bytes 135176 | tf_op jit(solution)/shard_map/ppermute | solution.py:27
  91.5 5.0 %collective-permute-start.30 = (f32[88,128]{1,0:T(8,128)S(1)}, f32[88,128]{1,0:T(8,128)S(1)}, u32[]{:S(2)}, u32[]{:S(2)}) collective-permute-start(f32[88,128]{1,0:T(8,128)S(1)} %add.52), channel_id=1, source_target_pairs={{0,49},{16,0},{32,16},{48,32},{1,48},{17,1},{33,17},{49,33},{2,51}... | collective-permute-start | bytes 135176 | tf_op jit(solution)/shard_map/ppermute | solution.py:27
  96.6 7.2 %collective-permute-start.31 = (f32[88,128]{1,0:T(8,128)S(1)}, f32[88,128]{1,0:T(8,128)S(1)}, u32[]{:S(2)}, u32[]{:S(2)}) collective-permute-start(f32[88,128]{1,0:T(8,128)S(1)} %add_add_fusion), channel_id=1, source_target_pairs={{0,8},{8,0},{1,9},{9,1},{2,10},{10,2},{3,11},{11,3},{4,12},{12,4},... | collective-permute-start | bytes 135176 | tf_op jit(solution)/shard_map/ppermute | solution.py:20
  (3 other events, 43.2 us)

commit v4 on v3

--- a/solution.py
+++ b/solution.py
@@ -12,7 +12,8 @@
 SIZES = (4, 4, 2, 4, 2)
 ROW = AXES[:3]
 COL = AXES[3:]
-GROUP = 8
+GROUP = 32
+CHUNK = 32
 
 
 def shift(value, axes, step):
@@ -71,34 +72,51 @@
     )(place, tile_rows, tile_cols)
 
 
-def sum_tiles(part, plan_ref, vals_ref, table_ref, own_ref, away_refs, vals, acc, prods, sems, beside=None):
-    tile = vals.shape[-1]
-    groups = (plan_ref[4 * part + 3, 0] + GROUP - 1) // GROUP
-
-    def fetch(g, _):
-        for i in range(GROUP):
-            s = g * GROUP + i
-            pltpu.make_async_copy(vals_ref.at[plan_ref[4 * part, s]], vals.at[s], sems.at[g]).start()
-        return 0
-
-    lax.fori_loop(0, groups, fetch, 0)
-    acc[...] = jnp.zeros_like(acc)
-    if beside is not None:
-        beside()
+def fetch_kernel(plan_ref, vals_ref, out_ref, token_ref, sems):
+    count = plan_ref[3, 0] + plan_ref[7, 0]
+
+    def each(act):
+        for k in range(vals_ref.shape[0] // CHUNK):
+            @pl.when(k * CHUNK < count)
+            def _(k=k):
+                part = pl.ds(k * CHUNK, CHUNK)
+                act(pltpu.make_async_copy(vals_ref.at[part], out_ref.at[part], sems.at[k]))
+
+    each(lambda copy: copy.start())
+    each(lambda copy: copy.wait())
+    token_ref[0] = count
+
+
+def fetch(plan, vals):
+    smem = pl.BlockSpec(memory_space=pltpu.SMEM)
+    return pl.pallas_call(
+        fetch_kernel,
+        out_shape=(jax.ShapeDtypeStruct(vals.shape, vals.dtype), jax.ShapeDtypeStruct((1,), jnp.int32)),
+        in_specs=[smem, pl.BlockSpec(memory_space=pltpu.HBM)],
+        out_specs=(pl.BlockSpec(memory_space=pltpu.VMEM), smem),
+        scratch_shapes=[pltpu.SemaphoreType.DMA((vals.shape[0] // CHUNK,))],
+        compiler_params=pltpu.CompilerParams(vmem_limit_bytes=12 * 2**20),
+        cost_estimate=pl.CostEstimate(flops=0, bytes_accessed=16 * 2**20, transcendentals=0),
+        name="fetch",
+    )(plan, vals)
+
+
+def sum_tiles(part, plan_ref, vals_ref, table_ref, own_ref, away_refs, acc, prods):
+    tile = vals_ref.shape[-1]
 
     def group(g, _):
-        here = pl.ds(g * GROUP, GROUP)
-        pltpu.make_async_copy(vals_ref.at[pl.ds(0, GROUP)], vals.at[here], sems.at[g]).wait()
-        slots = [g * GROUP + i for i in range(GROUP)]
-        for i, s in enumerate(slots):
+        entries = [g * GROUP + i for i in range(GROUP)]
+        for i, s in enumerate(entries):
             place = pl.multiple_of(plan_ref[4 * part + 2, s], tile)
-            prods[i] = jnp.dot(vals[s], table_ref[pl.ds(place, tile), :], preferred_element_type=jnp.float32)
-        for i, s in enumerate(slots):
+            prods[i] = jnp.dot(
+                vals_ref[plan_ref[4 * part, s]], table_ref[pl.ds(place, tile), :], preferred_element_type=jnp.float32
+            )
+        for i, s in enumerate(entries):
             row = pl.multiple_of(plan_ref[4 * part + 1, s], tile)
             acc[pl.ds(row, tile), :] += prods[i]
         return 0
 
-    lax.fori_loop(0, groups, group, 0)
+    lax.fori_loop(0, (plan_ref[4 * part + 3, 0] + GROUP - 1) // GROUP, group, 0)
     size = own_ref.shape[0]
     own_ref[...] = acc[pl.ds(0, size), :]
     for k, ref in enumerate(away_refs):
@@ -108,19 +126,23 @@
 def far_kernel(n_pieces, plan_ref, vals_ref, *refs):
     pieces, refs = refs[:n_pieces], refs[n_pieces:]
     table_ref, own_ref, *away_refs = refs[:5]
-    vals, acc, prods, sems, sem_table = refs[5:]
+    acc, prods, sem_table = refs[5:]
     copies, start = [], 0
     for i, piece in enumerate(pieces):
         rows = piece.shape[0]
         copies.append(pltpu.make_async_copy(piece, table_ref.at[pl.ds(start, rows)], sem_table.at[i]))
         copies[-1].start()
         start += rows
-    sum_tiles(0, plan_ref, vals_ref, table_ref, own_ref, away_refs, vals, acc, prods, sems,
-              lambda: [copy.wait() for copy in copies])
+    acc[...] = jnp.zeros_like(acc)
+    for copy in copies:
+        copy.wait()
+    sum_tiles(0, plan_ref, vals_ref, table_ref, own_ref, away_refs, acc, prods)
 
 
 def near_kernel(plan_ref, vals_ref, table_ref, own_ref, *refs):
-    sum_tiles(1, plan_ref, vals_ref, table_ref, own_ref, refs[:3], *refs[3:])
+    acc, prods = refs[3:]
+    acc[...] = jnp.zeros_like(acc)
+    sum_tiles(1, plan_ref, vals_ref, table_ref, own_ref, refs[:3], acc, prods)
 
 
 def aggregate(kernel, plan, vals, pieces, out_rows, with_table):
@@ -132,10 +154,8 @@
     shape = (out_rows // n_x, feat)
     out = [jax.ShapeDtypeStruct(shape, jnp.float32)] + [jax.ShapeDtypeStruct(shape, jnp.bfloat16)] * (n_x - 1)
     scratch = [
-        pltpu.VMEM((slots, tile, tile), jnp.bfloat16),
         pltpu.VMEM((out_rows + tile, feat), jnp.float32),
         pltpu.VMEM((GROUP, tile, feat), jnp.float32),
-        pltpu.SemaphoreType.DMA((slots // GROUP,)),
     ]
     if with_table:
         out = [jax.ShapeDtypeStruct((table_rows, feat), jnp.bfloat16)] + out
@@ -144,10 +164,10 @@
     return pl.pallas_call(
         kernel,
         out_shape=out,
-        in_specs=[pl.BlockSpec(memory_space=pltpu.SMEM), pl.BlockSpec(memory_space=pltpu.HBM)] + [near] * len(pieces),
+        in_specs=[pl.BlockSpec(memory_space=pltpu.SMEM), vmem] + [near] * len(pieces),
         out_specs=[vmem] * len(out),
         scratch_shapes=scratch,
-        compiler_params=pltpu.CompilerParams(vmem_limit_bytes=24 * 2**20),
+        compiler_params=pltpu.CompilerParams(vmem_limit_bytes=20 * 2**20),
         cost_estimate=pl.CostEstimate(flops=slots * tile * tile * feat, bytes_accessed=8 * 2**20, transcendentals=0),
         name="far_rows" if with_table else "near_rows",
     )(plan, vals, *pieces)
@@ -200,9 +220,13 @@
     )(core, own, far, *more, weight, labels)
 
 
-def gather_features(features):
+def after(value, token):
+    return jnp.where(token[0] < 0, jnp.zeros_like(value), value)
+
+
+def gather_features(features, token):
     by_z = jnp.concatenate([features] + [shift(features, "zl", -k) for k in (1, 2, 3)], 0)
-    opposite = shift(features, "y", 2)
+    opposite = after(shift(features, "y", 2), token)
     opposite = jnp.concatenate([opposite] + [shift(opposite, "zl", -k) for k in (1, 2, 3)], 0)
     mine = [by_z, shift(by_z, "y", -1), opposite, shift(by_z, "y", 1)]
     return mine + [shift(piece, "core", 1) for piece in mine]
@@ -211,9 +235,9 @@
 def sum_everywhere(keep, give, core, classes):
     total = keep + shift(give, "core", 1)
     for axis in ("y", "x"):
-        total = total + shift(total, axis, 1) + shift(total, axis, 2) + shift(total, axis, 3)
+        total = (total + shift(total, axis, 2)) + (shift(total, axis, 1) + shift(total, axis, 3))
     total = total + shift(total, "zh", 1)
-    total = total + shift_z(total, 1) + shift_z(total, 2) + shift_z(total, -1)
+    total = (total + shift_z(total, 2)) + (shift_z(total, 1) + shift_z(total, -1))
     rest = shift(total, "core", 1)
     swap = core == 1
     return jnp.concatenate([jnp.where(swap, rest, total), jnp.where(swap, total, rest)], 0)[:classes]
@@ -231,7 +255,8 @@
         tile_rows.reshape(1, slots), tile_cols.reshape(1, slots), tile_count.reshape(()), nodes // tile, tile
     )
 
-    pieces = gather_features(features)
+    vals, token = fetch(lists, vals)
+    pieces = gather_features(features, token)
     table, own, *away = aggregate(functools.partial(far_kernel, len(pieces)), lists, vals, pieces, out_rows, True)
     give = own + sum(shift(away[k], "x", k + 1).astype(jnp.float32) for k in (1, 0, 2))
     own, *away = aggregate(near_kernel, lists, vals, [table], out_rows, False)

time: 105 us -> 102 us (0.971)
  waiting for transfers between devices: 32.7 us -> 23 us
  starting transfers between devices: 56.3 us -> 63 us
    ppermute x29, waiting for transfers between devices: 30.2 us -> 20.2 us  [shift(): return lax.ppermute(value, axes, [(i, (i + step) % n) for i in range(n)])]
    ppermute x29, starting transfers between devices: 51.9 us -> 59.5 us  [shift(): return lax.ppermute(value, axes, [(i, (i + step) % n) for i in range(n)])]
    pallas_call x2, Pallas kernels: 8.14 us -> 4.09 us  [aggregate(): pl.pallas_call(kernel, out_shape=out, in_specs=[pl.BlockSpec(memory_space...]
    pallas_call x0 -> x1, Pallas kernels: none -> 3.43 us  [fetch(): pl.pallas_call(fetch_kernel, out_shape=(jax.ShapeDtypeStruct(vals.shape,...]
  transfers between devices with their start and end apart: 32 -> 32, of which waited for: 15 -> 18; matrix products, arithmetic and copies ran while one was open for 2% -> 2% of each run, Pallas kernels for 5% -> 7%
where the time goes in v4:
time: 102 us
  starting transfers between devices  63 us (62%)
  waiting for transfers between devices  23 us (23%)
  Pallas kernels  10.3 us (10%)
  local copies, waits for them, and re-layouts  2.33 us (2%)
  between operations  2.1 us (2%)
    ppermute x29, starting transfers between devices, shift(): return lax.ppermute(value, axes, [(i, (i + step) % n) for i in range(n)])  59.5 us
    ppermute x29, waiting for transfers between devices, shift(): return lax.ppermute(value, axes, [(i, (i + step) % n) for i in range(n)])  20.2 us
    pallas_call x2, Pallas kernels, aggregate(): pl.pallas_call(kernel, out_shape=out, in_specs=[pl.BlockSpec(memory_space...  4.09 us
    ppermute x3, starting transfers between devices, shift_z(): lax.ppermute(value, ('zl', 'zh'), [(at(z), at((z + step) % n)) for z in r...  3.48 us
    pallas_call x1, Pallas kernels, fetch(): pl.pallas_call(fetch_kernel, out_shape=(jax.ShapeDtypeStruct(vals.shape,...  3.43 us
    ppermute x3, waiting for transfers between devices, shift_z(): lax.ppermute(value, ('zl', 'zh'), [(at(z), at((z + step) % n)) for z in r...  2.8 us
  transfers between devices with their start and end apart: 32, of which 18 were waited for; matrix products, arithmetic and copies ran while one was open for 2% of the time, Pallas kernels for 7%

profile of v4, /device:TPU:1, one launch (start us, length us, event | category | flops | bytes accessed | tf_op | source)
XLA Modules:
  0.0 101.5 jit_solution(17437184050611429915)
XLA Ops:
  0.6 5.3 %collective-permute-start = (bf16[512,128]{1,0:T(8,128)(2,1)}, bf16[512,128]{1,0:T(8,128)(2,1)S(1)}, u32[]{:S(2)}, u32[]{:S(2)}) collective-permute-start(bf16[512,128]{1,0:T(8,128)(2,1)} %param.7), channel_id=1, source_target_pairs={{0,48},{16,0},{32,16},{48,32},{1,49},{17,1},{33,17},{49,33},{2,50}... | collective-permute-start | bytes 393224 | tf_op jit(solution)/shard_map/ppermute | solution.py:21
  5.9 2.9 %collective-permute-start.4 = (bf16[512,128]{1,0:T(8,128)(2,1)}, bf16[512,128]{1,0:T(8,128)(2,1)S(1)}, u32[]{:S(2)}, u32[]{:S(2)}) collective-permute-start(bf16[512,128]{1,0:T(8,128)(2,1)} %param.7), channel_id=1, source_target_pairs={{0,128},{64,192},{128,0},{192,64},{1,129},{65,193},{129,1},{193,65... | collective-permute-start | bytes 393224 | tf_op jit(solution)/shard_map/ppermute | solution.py:21
  11.4 1.6 %plan.1.plan_ref = s32[8,256]{1,0:T(8,128)} custom-call(s32[6]{0:T(128)} %stack.20.refs_0_, s32[1,256]{1,0:T(1,128)} %bitcast.19, s32[1,256]{1,0:T(1,128)} %bitcast.20), custom_call_target="tpu_custom_call" | custom-call | tf_op jit(solution)/shard_map/plan/pallas_call | solution.py:66
  13.7 3.4 %fetch.1 = (bf16[256,128,128]{2,1,0:T(8,128)(2,1)S(1)}, s32[1]{0:T(128)}) custom-call(s32[8,256]{1,0:T(8,128)S(1)} %copy-done, bf16[256,128,128]{2,1,0:T(8,128)(2,1)} %bitcast.18), custom_call_target="tpu_custom_call" | custom-call | bytes 16777216 | tf_op jit(solution)/shard_map/fetch/pallas_call | solution.py:92
  18.5 2.4 %collective-permute-start.3 = (bf16[2048,128]{1,0:T(8,128)(2,1)S(1)}, bf16[2048,128]{1,0:T(8,128)(2,1)S(1)}, u32[]{:S(2)}, u32[]{:S(2)}) collective-permute-start(bf16[2048,128]{1,0:T(8,128)(2,1)S(1)} %constant_dynamic-update-slice_fusion.refs_0_), channel_id=1, source_target_pairs={{0,192},{64,0},{128,64},{192,128},{1,193},{65,1},{129,65},{193,129... | collective-permute-start | bytes 1572872 | tf_op jit(solution)/shard_map/ppermute | solution.py:21
  21.9 2.0 %collective-permute-start.6 = (bf16[512,128]{1,0:T(8,128)(2,1)S(1)}, bf16[512,128]{1,0:T(8,128)(2,1)S(1)}, u32[]{:S(2)}, u32[]{:S(2)}) collective-permute-start(bf16[512,128]{1,0:T(8,128)(2,1)S(1)} %broadcast_select_fusion), channel_id=1, source_target_pairs={{0,32},{16,48},{32,0},{48,16},{1,33},{17,49},{33,1},{49,17},{2,34}... | collective-permute-start | bytes 393224 | tf_op jit(solution)/shard_map/ppermute | solution.py:21
  23.9 1.4 %collective-permute-start.7 = (bf16[512,128]{1,0:T(8,128)(2,1)S(1)}, bf16[512,128]{1,0:T(8,128)(2,1)S(1)}, u32[]{:S(2)}, u32[]{:S(2)}) collective-permute-start(bf16[512,128]{1,0:T(8,128)(2,1)S(1)} %broadcast_select_fusion), channel_id=1, source_target_pairs={{0,16},{16,32},{32,48},{48,0},{1,17},{17,33},{33,49},{49,1},{2,18}... | collective-permute-start | bytes 393224 | tf_op jit(solution)/shard_map/ppermute | solution.py:21
  25.2 3.5 %collective-permute-start.9 = (bf16[2048,128]{1,0:T(8,128)(2,1)S(1)}, bf16[2048,128]{1,0:T(8,128)(2,1)S(1)}, u32[]{:S(2)}, u32[]{:S(2)}) collective-permute-start(bf16[2048,128]{1,0:T(8,128)(2,1)S(1)} %constant_dynamic-update-slice_fusion.refs_0_), channel_id=1, source_target_pairs={{0,8},{8,0},{1,9},{9,1},{2,10},{10,2},{3,11},{11,3},{4,12},{12,4},... | collective-permute-start | bytes 1572872 | tf_op jit(solution)/shard_map/ppermute | solution.py:21
  29.2 4.2 %collective-permute-done.7 = bf16[512,128]{1,0:T(8,128)(2,1)S(1)} collective-permute-done((bf16[512,128]{1,0:T(8,128)(2,1)S(1)}, bf16[512,128]{1,0:T(8,128)(2,1)S(1)}, u32[]{:S(2)}, u32[]{:S(2)}) %collective-permute-start.7) | collective-permute-done | bytes 131104 | tf_op jit(solution)/shard_map/ppermute | solution.py:21
  33.4 3.3 %collective-permute-start.11 = (bf16[2048,128]{1,0:T(8,128)(2,1)S(1)}, bf16[2048,128]{1,0:T(8,128)(2,1)S(1)}, u32[]{:S(2)}, u32[]{:S(2)}) collective-permute-start(bf16[2048,128]{1,0:T(8,128)(2,1)S(1)} %pad_maximum_fusion.refs_2_), channel_id=1, source_target_pairs={{0,8},{8,0},{1,9},{9,1},{2,10},{10,2},{3,11},{11,3},{4,12},{12,4},... | collective-permute-start | bytes 1572872 | tf_op jit(solution)/shard_map/ppermute | solution.py:21
  37.3 1.0 collective-permute-done.11.refs_6_
  39.8 2.1 %far_rows.1 = (bf16[16384,128]{1,0:T(8,128)(2,1)S(1)}, f32[512,128]{1,0:T(8,128)S(1)}, bf16[512,128]{1,0:T(8,128)(2,1)S(1)}, bf16[512,128]{1,0:T(8,128)(2,1)S(1)}, bf16[512,128]{1,0:T(8,128)(2,1)S(1)}) custom-call(s32[8,256]{1,0:T(8,128)S(1)} %copy-done.1, bf16[256,128,128]{2,1,0:T(8,128)(2,1)S(1)} %get-tuple-element.16.vals_ref, ...), custom_call_target="tpu_custom_call" | custom-call | flops 536870912 | bytes 8388608 | tf_op jit(solution)/shard_map/far_rows/pallas_call | solution.py:164
  42.0 2.8 %collective-permute-start.13 = (bf16[512,128]{1,0:T(8,128)(2,1)S(1)}, bf16[512,128]{1,0:T(8,128)(2,1)S(1)}, u32[]{:S(2)}, u32[]{:S(2)}) collective-permute-start(bf16[512,128]{1,0:T(8,128)(2,1)S(1)} %get-tuple-element.21), channel_id=1, source_target_pairs={{0,4},{2,6},{4,0},{6,2},{1,5},{3,7},{5,1},{7,3},{8,12},{10,14},{12... | collective-permute-start | bytes 393224 | tf_op jit(solution)/shard_map/ppermute | solution.py:21
  44.8 2.7 %collective-permute-start.15 = (bf16[512,128]{1,0:T(8,128)(2,1)S(1)}, bf16[512,128]{1,0:T(8,128)(2,1)S(1)}, u32[]{:S(2)}, u32[]{:S(2)}) collective-permute-start(bf16[512,128]{1,0:T(8,128)(2,1)S(1)} %get-tuple-element.23), channel_id=1, source_target_pairs={{0,6},{2,0},{4,2},{6,4},{1,7},{3,1},{5,3},{7,5},{8,14},{10,8},{12,... | collective-permute-start | bytes 393224 | tf_op jit(solution)/shard_map/ppermute | solution.py:21
  47.5 2.0 %near_rows.1 = (f32[512,128]{1,0:T(8,128)S(1)}, bf16[512,128]{1,0:T(8,128)(2,1)S(1)}, bf16[512,128]{1,0:T(8,128)(2,1)S(1)}, bf16[512,128]{1,0:T(8,128)(2,1)S(1)}) custom-call(s32[8,256]{1,0:T(8,128)S(1)} %copy-done.1, bf16[256,128,128]{2,1,0:T(8,128)(2,1)S(1)} %get-tuple-element.16.vals_ref, bf16[16384,128]{1,0:T(8,128)(2,1)S(1)} %get-tuple-element.18.table_ref), custom_call_target="tpu_custom_call" | custom-call | flops 536870912 | bytes 8388608 | tf_op jit(solution)/shard_map/near_rows/pallas_call | solution.py:164
  49.7 2.7 %collective-permute-start.19 = (bf16[512,128]{1,0:T(8,128)(2,1)S(1)}, bf16[512,128]{1,0:T(8,128)(2,1)S(1)}, u32[]{:S(2)}, u32[]{:S(2)}) collective-permute-start(bf16[512,128]{1,0:T(8,128)(2,1)S(1)} %get-tuple-element.26), channel_id=1, source_target_pairs={{0,6},{2,0},{4,2},{6,4},{1,7},{3,1},{5,3},{7,5},{8,14},{10,8},{12,... | collective-permute-start | bytes 393224 | tf_op jit(solution)/shard_map/ppermute | solution.py:21
  52.4 4.3 %collective-permute-start.16 = (bf16[512,128]{1,0:T(8,128)(2,1)S(1)}, bf16[512,128]{1,0:T(8,128)(2,1)S(1)}, u32[]{:S(2)}, u32[]{:S(2)}) collective-permute-start(bf16[512,128]{1,0:T(8,128)(2,1)S(1)} %add_convert_fusion), channel_id=1, source_target_pairs={{0,1},{1,0},{2,3},{3,2},{4,5},{5,4},{6,7},{7,6},{8,9},{9,8},{10,11... | collective-permute-start | bytes 393224 | tf_op jit(solution)/shard_map/ppermute | solution.py:21
  56.7 2.2 %collective-permute-done.18.refs_4_ = bf16[512,128]{1,0:T(8,128)(2,1)S(1)} collective-permute-done((bf16[512,128]{1,0:T(8,128)(2,1)S(1)}, bf16[512,128]{1,0:T(8,128)(2,1)S(1)}, u32[]{:S(2)}, u32[]{:S(2)}) %collective-permute-start.18) | collective-permute-done | bytes 131104 | tf_op jit(solution)/shard_map/ppermute | solution.py:21
  58.9 1.4 %collective-permute-done.16.refs_2_ = bf16[512,128]{1,0:T(8,128)(2,1)S(1)} collective-permute-done((bf16[512,128]{1,0:T(8,128)(2,1)S(1)}, bf16[512,128]{1,0:T(8,128)(2,1)S(1)}, u32[]{:S(2)}, u32[]{:S(2)}) %collective-permute-start.16) | collective-permute-done | bytes 131104 | tf_op jit(solution)/shard_map/ppermute | solution.py:21
  60.3 1.1 %head.1 = (f32[172,512]{1,0:T(8,128)}, f32[88,128]{1,0:T(8,128)S(1)}, f32[88,128]{1,0:T(8,128)S(1)}) custom-call(s32[1]{0:T(128)} %bitcast.refs_0_, f32[512,128]{1,0:T(8,128)S(1)} %get-tuple-element.19.refs_1_, bf16[512,128]{1,0:T(8,128)(2,1)S(1)} %collective-permute-done.16.refs_2_, bf16[512,128]{1,0:T(8,128)(2,1)S(1)} %collective-permute-done.17.refs_3_, ...), custom_call_target="tpu_custom_call" | custom-call | tf_op jit(solution)/shard_map/head/pallas_call | solution.py:209
  61.4 4.4 %collective-permute-start.20 = (f32[88,128]{1,0:T(8,128)S(1)}, f32[88,128]{1,0:T(8,128)S(1)}, u32[]{:S(2)}, u32[]{:S(2)}) collective-permute-start(f32[88,128]{1,0:T(8,128)S(1)} %get-tuple-element.29), channel_id=1, source_target_pairs={{0,8},{8,0},{1,9},{9,1},{2,10},{10,2},{3,11},{11,3},{4,12},{12,4},... | collective-permute-start | bytes 135176 | tf_op jit(solution)/shard_map/ppermute | solution.py:21
  66.7 1.8 %collective-permute-start.21 = (f32[88,128]{1,0:T(8,128)S(1)}, f32[88,128]{1,0:T(8,128)S(1)}, u32[]{:S(2)}, u32[]{:S(2)}) collective-permute-start(f32[88,128]{1,0:T(8,128)S(1)} %add.45), channel_id=1, source_target_pairs={{0,128},{64,192},{128,0},{192,64},{1,129},{65,193},{129,1},{193,65... | collective-permute-start | bytes 135176 | tf_op jit(solution)/shard_map/ppermute | solution.py:21
  68.4 1.7 %collective-permute-start.22 = (f32[88,128]{1,0:T(8,128)S(1)}, f32[88,128]{1,0:T(8,128)S(1)}, u32[]{:S(2)}, u32[]{:S(2)}) collective-permute-start(f32[88,128]{1,0:T(8,128)S(1)} %add.45), channel_id=1, source_target_pairs={{0,64},{64,128},{128,192},{192,0},{1,65},{65,129},{129,193},{193,1... | collective-permute-start | bytes 135176 | tf_op jit(solution)/shard_map/ppermute | solution.py:21
  71.1 1.4 %collective-permute-done.22 = f32[88,128]{1,0:T(8,128)S(1)} collective-permute-done((f32[88,128]{1,0:T(8,128)S(1)}, f32[88,128]{1,0:T(8,128)S(1)}, u32[]{:S(2)}, u32[]{:S(2)}) %collective-permute-start.22) | collective-permute-done | bytes 45088 | tf_op jit(solution)/shard_map/ppermute | solution.py:21
  73.0 1.9 %collective-permute-start.24 = (f32[88,128]{1,0:T(8,128)S(1)}, f32[88,128]{1,0:T(8,128)S(1)}, u32[]{:S(2)}, u32[]{:S(2)}) collective-permute-start(f32[88,128]{1,0:T(8,128)S(1)} %add_add_fusion.2), channel_id=1, source_target_pairs={{0,4},{2,6},{4,0},{6,2},{1,5},{3,7},{5,1},{7,3},{8,12},{10,14},{12... | collective-permute-start | bytes 135176 | tf_op jit(solution)/shard_map/ppermute | solution.py:21
  74.9 1.8 %collective-permute-start.25 = (f32[88,128]{1,0:T(8,128)S(1)}, f32[88,128]{1,0:T(8,128)S(1)}, u32[]{:S(2)}, u32[]{:S(2)}) collective-permute-start(f32[88,128]{1,0:T(8,128)S(1)} %add_add_fusion.2), channel_id=1, source_target_pairs={{0,2},{2,4},{4,6},{6,0},{1,3},{3,5},{5,7},{7,1},{8,10},{10,12},{12... | collective-permute-start | bytes 135176 | tf_op jit(solution)/shard_map/ppermute | solution.py:21
  77.6 1.4 %collective-permute-done.25 = f32[88,128]{1,0:T(8,128)S(1)} collective-permute-done((f32[88,128]{1,0:T(8,128)S(1)}, f32[88,128]{1,0:T(8,128)S(1)}, u32[]{:S(2)}, u32[]{:S(2)}) %collective-permute-start.25) | collective-permute-done | bytes 45088 | tf_op jit(solution)/shard_map/ppermute | solution.py:21
  80.0 4.1 %collective-permute-start.27 = (f32[88,128]{1,0:T(8,128)S(1)}, f32[88,128]{1,0:T(8,128)S(1)}, u32[]{:S(2)}, u32[]{:S(2)}) collective-permute-start(f32[88,128]{1,0:T(8,128)S(1)} %add_add_fusion.1), channel_id=1, source_target_pairs={{0,1},{1,0},{2,3},{3,2},{4,5},{5,4},{6,7},{7,6},{8,9},{9,8},{10,11... | collective-permute-start | bytes 135176 | tf_op jit(solution)/shard_map/ppermute | solution.py:21
  84.1 2.8 %collective-permute-done.27 = f32[88,128]{1,0:T(8,128)S(1)} collective-permute-done((f32[88,128]{1,0:T(8,128)S(1)}, f32[88,128]{1,0:T(8,128)S(1)}, u32[]{:S(2)}, u32[]{:S(2)}) %collective-permute-start.27) | collective-permute-done | bytes 45088 | tf_op jit(solution)/shard_map/ppermute | solution.py:21
  87.7 2.7 %collective-permute-start.30 = (f32[88,128]{1,0:T(8,128)S(1)}, f32[88,128]{1,0:T(8,128)S(1)}, u32[]{:S(2)}, u32[]{:S(2)}) collective-permute-start(f32[88,128]{1,0:T(8,128)S(1)} %add.52), channel_id=1, source_target_pairs={{0,49},{16,0},{32,16},{48,32},{1,48},{17,1},{33,17},{49,33},{2,51}... | collective-permute-start | bytes 135176 | tf_op jit(solution)/shard_map/ppermute | solution.py:28
  90.3 1.7 %collective-permute-done.28 = f32[88,128]{1,0:T(8,128)S(1)} collective-permute-done((f32[88,128]{1,0:T(8,128)S(1)}, f32[88,128]{1,0:T(8,128)S(1)}, u32[]{:S(2)}, u32[]{:S(2)}) %collective-permute-start.28) | collective-permute-done | bytes 45088 | tf_op jit(solution)/shard_map/ppermute | solution.py:28
  93.1 6.9 %collective-permute-start.31 = (f32[88,128]{1,0:T(8,128)S(1)}, f32[88,128]{1,0:T(8,128)S(1)}, u32[]{:S(2)}, u32[]{:S(2)}) collective-permute-start(f32[88,128]{1,0:T(8,128)S(1)} %add_add_fusion), channel_id=1, source_target_pairs={{0,8},{8,0},{1,9},{9,1},{2,10},{10,2},{3,11},{11,3},{4,12},{12,4},... | collective-permute-start | bytes 135176 | tf_op jit(solution)/shard_map/ppermute | solution.py:21
  (60 shorter events, 14.8 us)
Async XLA Ops:
  0.6 17.2 %collective-permute-start = (bf16[512,128]{1,0:T(8,128)(2,1)}, bf16[512,128]{1,0:T(8,128)(2,1)S(1)}, u32[]{:S(2)}, u32[]{:S(2)}) collective-permute-start(bf16[512,128]{1,0:T(8,128)(2,1)} %param.7), channel_id=1, source_target_pairs={{0,48},{16,0},{32,16},{48,32},{1,49},{17,1},{33,17},{49,33},{2,50}... | collective-permute-start | bytes 393224 | tf_op jit(solution)/shard_map/ppermute | solution.py:21
  5.9 15.0 %collective-permute-start.4 = (bf16[512,128]{1,0:T(8,128)(2,1)}, bf16[512,128]{1,0:T(8,128)(2,1)S(1)}, u32[]{:S(2)}, u32[]{:S(2)}) collective-permute-start(bf16[512,128]{1,0:T(8,128)(2,1)} %param.7), channel_id=1, source_target_pairs={{0,128},{64,192},{128,0},{192,64},{1,129},{65,193},{129,1},{193,65... | collective-permute-start | bytes 393224 | tf_op jit(solution)/shard_map/ppermute | solution.py:21
  8.8 9.7 %collective-permute-start.1 = (bf16[512,128]{1,0:T(8,128)(2,1)}, bf16[512,128]{1,0:T(8,128)(2,1)S(1)}, u32[]{:S(2)}, u32[]{:S(2)}) collective-permute-start(bf16[512,128]{1,0:T(8,128)(2,1)} %param.7), channel_id=1, source_target_pairs={{0,32},{16,48},{32,0},{48,16},{1,33},{17,49},{33,1},{49,17},{2,34}... | collective-permute-start | bytes 393224 | tf_op jit(solution)/shard_map/ppermute | solution.py:21
  8.8 9.7 %collective-permute-start.2 = (bf16[512,128]{1,0:T(8,128)(2,1)}, bf16[512,128]{1,0:T(8,128)(2,1)S(1)}, u32[]{:S(2)}, u32[]{:S(2)}) collective-permute-start(bf16[512,128]{1,0:T(8,128)(2,1)} %param.7), channel_id=1, source_target_pairs={{0,16},{16,32},{32,48},{48,0},{1,17},{17,33},{33,49},{49,1},{2,18}... | collective-permute-start | bytes 393224 | tf_op jit(solution)/shard_map/ppermute | solution.py:21
  18.5 18.2 %collective-permute-start.3 = (bf16[2048,128]{1,0:T(8,128)(2,1)S(1)}, bf16[2048,128]{1,0:T(8,128)(2,1)S(1)}, u32[]{:S(2)}, u32[]{:S(2)}) collective-permute-start(bf16[2048,128]{1,0:T(8,128)(2,1)S(1)} %constant_dynamic-update-slice_fusion.refs_0_), channel_id=1, source_target_pairs={{0,192},{64,0},{128,64},{192,128},{1,193},{65,1},{129,65},{193,129... | collective-permute-start | bytes 1572872 | tf_op jit(solution)/shard_map/ppermute | solution.py:21
  20.9 16.0 %collective-permute-start.8 = (bf16[2048,128]{1,0:T(8,128)(2,1)S(1)}, bf16[2048,128]{1,0:T(8,128)(2,1)S(1)}, u32[]{:S(2)}, u32[]{:S(2)}) collective-permute-start(bf16[2048,128]{1,0:T(8,128)(2,1)S(1)} %constant_dynamic-update-slice_fusion.refs_0_), channel_id=1, source_target_pairs={{0,64},{64,128},{128,192},{192,0},{1,65},{65,129},{129,193},{193,1... | collective-permute-start | bytes 1572872 | tf_op jit(solution)/shard_map/ppermute | solution.py:21
  20.9 4.3 %collective-permute-start.5 = (bf16[512,128]{1,0:T(8,128)(2,1)S(1)}, bf16[512,128]{1,0:T(8,128)(2,1)S(1)}, u32[]{:S(2)}, u32[]{:S(2)}) collective-permute-start(bf16[512,128]{1,0:T(8,128)(2,1)S(1)} %broadcast_select_fusion), channel_id=1, source_target_pairs={{0,48},{16,0},{32,16},{48,32},{1,49},{17,1},{33,17},{49,33},{2,50}... | collective-permute-start | bytes 393224 | tf_op jit(solution)/shard_map/ppermute | solution.py:21
  21.9 7.4 %collective-permute-start.6 = (bf16[512,128]{1,0:T(8,128)(2,1)S(1)}, bf16[512,128]{1,0:T(8,128)(2,1)S(1)}, u32[]{:S(2)}, u32[]{:S(2)}) collective-permute-start(bf16[512,128]{1,0:T(8,128)(2,1)S(1)} %broadcast_select_fusion), channel_id=1, source_target_pairs={{0,32},{16,48},{32,0},{48,16},{1,33},{17,49},{33,1},{49,17},{2,34}... | collective-permute-start | bytes 393224 | tf_op jit(solution)/shard_map/ppermute | solution.py:21
  23.9 9.5 %collective-permute-start.7 = (bf16[512,128]{1,0:T(8,128)(2,1)S(1)}, bf16[512,128]{1,0:T(8,128)(2,1)S(1)}, u32[]{:S(2)}, u32[]{:S(2)}) collective-permute-start(bf16[512,128]{1,0:T(8,128)(2,1)S(1)} %broadcast_select_fusion), channel_id=1, source_target_pairs={{0,16},{16,32},{32,48},{48,0},{1,17},{17,33},{33,49},{49,1},{2,18}... | collective-permute-start | bytes 393224 | tf_op jit(solution)/shard_map/ppermute | solution.py:21
  25.2 12.1 %collective-permute-start.9 = (bf16[2048,128]{1,0:T(8,128)(2,1)S(1)}, bf16[2048,128]{1,0:T(8,128)(2,1)S(1)}, u32[]{:S(2)}, u32[]{:S(2)}) collective-permute-start(bf16[2048,128]{1,0:T(8,128)(2,1)S(1)} %constant_dynamic-update-slice_fusion.refs_0_), channel_id=1, source_target_pairs={{0,8},{8,0},{1,9},{9,1},{2,10},{10,2},{3,11},{11,3},{4,12},{12,4},... | collective-permute-start | bytes 1572872 | tf_op jit(solution)/shard_map/ppermute | solution.py:21
  33.4 4.9 %collective-permute-start.11 = (bf16[2048,128]{1,0:T(8,128)(2,1)S(1)}, bf16[2048,128]{1,0:T(8,128)(2,1)S(1)}, u32[]{:S(2)}, u32[]{:S(2)}) collective-permute-start(bf16[2048,128]{1,0:T(8,128)(2,1)S(1)} %pad_maximum_fusion.refs_2_), channel_id=1, source_target_pairs={{0,8},{8,0},{1,9},{9,1},{2,10},{10,2},{3,11},{11,3},{4,12},{12,4},... | collective-permute-start | bytes 1572872 | tf_op jit(solution)/shard_map/ppermute | solution.py:21
  36.8 2.3 %collective-permute-start.10 = (bf16[2048,128]{1,0:T(8,128)(2,1)S(1)}, bf16[2048,128]{1,0:T(8,128)(2,1)S(1)}, u32[]{:S(2)}, u32[]{:S(2)}) collective-permute-start(bf16[2048,128]{1,0:T(8,128)(2,1)S(1)} %collective-permute-done.3.refs_1_), channel_id=1, source_target_pairs={{0,8},{8,0},{1,9},{9,1},{2,10},{10,2},{3,11},{11,3},{4,12},{12,4},... | collective-permute-start | bytes 1572872 | tf_op jit(solution)/shard_map/ppermute | solution.py:21
  36.9 2.9 %collective-permute-start.12 = (bf16[2048,128]{1,0:T(8,128)(2,1)S(1)}, bf16[2048,128]{1,0:T(8,128)(2,1)S(1)}, u32[]{:S(2)}, u32[]{:S(2)}) collective-permute-start(bf16[2048,128]{1,0:T(8,128)(2,1)S(1)} %collective-permute-done.8.refs_3_), channel_id=1, source_target_pairs={{0,8},{8,0},{1,9},{9,1},{2,10},{10,2},{3,11},{11,3},{4,12},{12,4},... | collective-permute-start | bytes 1572872 | tf_op jit(solution)/shard_map/ppermute | solution.py:21
  42.0 7.7 %collective-permute-start.13 = (bf16[512,128]{1,0:T(8,128)(2,1)S(1)}, bf16[512,128]{1,0:T(8,128)(2,1)S(1)}, u32[]{:S(2)}, u32[]{:S(2)}) collective-permute-start(bf16[512,128]{1,0:T(8,128)(2,1)S(1)} %get-tuple-element.21), channel_id=1, source_target_pairs={{0,4},{2,6},{4,0},{6,2},{1,5},{3,7},{5,1},{7,3},{8,12},{10,14},{12... | collective-permute-start | bytes 393224 | tf_op jit(solution)/shard_map/ppermute | solution.py:21
  44.8 7.5 %collective-permute-start.14 = (bf16[512,128]{1,0:T(8,128)(2,1)S(1)}, bf16[512,128]{1,0:T(8,128)(2,1)S(1)}, u32[]{:S(2)}, u32[]{:S(2)}) collective-permute-start(bf16[512,128]{1,0:T(8,128)(2,1)S(1)} %get-tuple-element.22), channel_id=1, source_target_pairs={{0,2},{2,4},{4,6},{6,0},{1,3},{3,5},{5,7},{7,1},{8,10},{10,12},{12... | collective-permute-start | bytes 393224 | tf_op jit(solution)/shard_map/ppermute | solution.py:21
  44.8 7.5 %collective-permute-start.15 = (bf16[512,128]{1,0:T(8,128)(2,1)S(1)}, bf16[512,128]{1,0:T(8,128)(2,1)S(1)}, u32[]{:S(2)}, u32[]{:S(2)}) collective-permute-start(bf16[512,128]{1,0:T(8,128)(2,1)S(1)} %get-tuple-element.23), channel_id=1, source_target_pairs={{0,6},{2,0},{4,2},{6,4},{1,7},{3,1},{5,3},{7,5},{8,14},{10,8},{12,... | collective-permute-start | bytes 393224 | tf_op jit(solution)/shard_map/ppermute | solution.py:21
  49.5 7.2 %collective-permute-start.17 = (bf16[512,128]{1,0:T(8,128)(2,1)S(1)}, bf16[512,128]{1,0:T(8,128)(2,1)S(1)}, u32[]{:S(2)}, u32[]{:S(2)}) collective-permute-start(bf16[512,128]{1,0:T(8,128)(2,1)S(1)} %get-tuple-element.24), channel_id=1, source_target_pairs={{0,4},{2,6},{4,0},{6,2},{1,5},{3,7},{5,1},{7,3},{8,12},{10,14},{12... | collective-permute-start | bytes 393224 | tf_op jit(solution)/shard_map/ppermute | solution.py:21
  49.6 9.3 %collective-permute-start.18 = (bf16[512,128]{1,0:T(8,128)(2,1)S(1)}, bf16[512,128]{1,0:T(8,128)(2,1)S(1)}, u32[]{:S(2)}, u32[]{:S(2)}) collective-permute-start(bf16[512,128]{1,0:T(8,128)(2,1)S(1)} %get-tuple-element.25), channel_id=1, source_target_pairs={{0,2},{2,4},{4,6},{6,0},{1,3},{3,5},{5,7},{7,1},{8,10},{10,12},{12... | collective-permute-start | bytes 393224 | tf_op jit(solution)/shard_map/ppermute | solution.py:21
  49.7 9.2 %collective-permute-start.19 = (bf16[512,128]{1,0:T(8,128)(2,1)S(1)}, bf16[512,128]{1,0:T(8,128)(2,1)S(1)}, u32[]{:S(2)}, u32[]{:S(2)}) collective-permute-start(bf16[512,128]{1,0:T(8,128)(2,1)S(1)} %get-tuple-element.26), channel_id=1, source_target_pairs={{0,6},{2,0},{4,2},{6,4},{1,7},{3,1},{5,3},{7,5},{8,14},{10,8},{12,... | collective-permute-start | bytes 393224 | tf_op jit(solution)/shard_map/ppermute | solution.py:21
  52.4 7.9 %collective-permute-start.16 = (bf16[512,128]{1,0:T(8,128)(2,1)S(1)}, bf16[512,128]{1,0:T(8,128)(2,1)S(1)}, u32[]{:S(2)}, u32[]{:S(2)}) collective-permute-start(bf16[512,128]{1,0:T(8,128)(2,1)S(1)} %add_convert_fusion), channel_id=1, source_target_pairs={{0,1},{1,0},{2,3},{3,2},{4,5},{5,4},{6,7},{7,6},{8,9},{9,8},{10,11... | collective-permute-start | bytes 393224 | tf_op jit(solution)/shard_map/ppermute | solution.py:21
  61.4 5.2 %collective-permute-start.20 = (f32[88,128]{1,0:T(8,128)S(1)}, f32[88,128]{1,0:T(8,128)S(1)}, u32[]{:S(2)}, u32[]{:S(2)}) collective-permute-start(f32[88,128]{1,0:T(8,128)S(1)} %get-tuple-element.29), channel_id=1, source_target_pairs={{0,8},{8,0},{1,9},{9,1},{2,10},{10,2},{3,11},{11,3},{4,12},{12,4},... | collective-permute-start | bytes 135176 | tf_op jit(solution)/shard_map/ppermute | solution.py:21
  66.7 4.5 %collective-permute-start.21 = (f32[88,128]{1,0:T(8,128)S(1)}, f32[88,128]{1,0:T(8,128)S(1)}, u32[]{:S(2)}, u32[]{:S(2)}) collective-permute-start(f32[88,128]{1,0:T(8,128)S(1)} %add.45), channel_id=1, source_target_pairs={{0,128},{64,192},{128,0},{192,64},{1,129},{65,193},{129,1},{193,65... | collective-permute-start | bytes 135176 | tf_op jit(solution)/shard_map/ppermute | solution.py:21
  68.4 4.1 %collective-permute-start.22 = (f32[88,128]{1,0:T(8,128)S(1)}, f32[88,128]{1,0:T(8,128)S(1)}, u32[]{:S(2)}, u32[]{:S(2)}) collective-permute-start(f32[88,128]{1,0:T(8,128)S(1)} %add.45), channel_id=1, source_target_pairs={{0,64},{64,128},{128,192},{192,0},{1,65},{65,129},{129,193},{193,1... | collective-permute-start | bytes 135176 | tf_op jit(solution)/shard_map/ppermute | solution.py:21
  70.1 2.9 %collective-permute-start.23 = (f32[88,128]{1,0:T(8,128)S(1)}, f32[88,128]{1,0:T(8,128)S(1)}, u32[]{:S(2)}, u32[]{:S(2)}) collective-permute-start(f32[88,128]{1,0:T(8,128)S(1)} %add.45), channel_id=1, source_target_pairs={{0,192},{64,0},{128,64},{192,128},{1,193},{65,1},{129,65},{193,129... | collective-permute-start | bytes 135176 | tf_op jit(solution)/shard_map/ppermute | solution.py:21
  73.0 4.6 %collective-permute-start.24 = (f32[88,128]{1,0:T(8,128)S(1)}, f32[88,128]{1,0:T(8,128)S(1)}, u32[]{:S(2)}, u32[]{:S(2)}) collective-permute-start(f32[88,128]{1,0:T(8,128)S(1)} %add_add_fusion.2), channel_id=1, source_target_pairs={{0,4},{2,6},{4,0},{6,2},{1,5},{3,7},{5,1},{7,3},{8,12},{10,14},{12... | collective-permute-start | bytes 135176 | tf_op jit(solution)/shard_map/ppermute | solution.py:21
  74.9 4.1 %collective-permute-start.25 = (f32[88,128]{1,0:T(8,128)S(1)}, f32[88,128]{1,0:T(8,128)S(1)}, u32[]{:S(2)}, u32[]{:S(2)}) collective-permute-start(f32[88,128]{1,0:T(8,128)S(1)} %add_add_fusion.2), channel_id=1, source_target_pairs={{0,2},{2,4},{4,6},{6,0},{1,3},{3,5},{5,7},{7,1},{8,10},{10,12},{12... | collective-permute-start | bytes 135176 | tf_op jit(solution)/shard_map/ppermute | solution.py:21
  76.7 3.2 %collective-permute-start.26 = (f32[88,128]{1,0:T(8,128)S(1)}, f32[88,128]{1,0:T(8,128)S(1)}, u32[]{:S(2)}, u32[]{:S(2)}) collective-permute-start(f32[88,128]{1,0:T(8,128)S(1)} %add_add_fusion.2), channel_id=1, source_target_pairs={{0,6},{2,0},{4,2},{6,4},{1,7},{3,1},{5,3},{7,5},{8,14},{10,8},{12,... | collective-permute-start | bytes 135176 | tf_op jit(solution)/shard_map/ppermute | solution.py:21
  80.0 6.9 %collective-permute-start.27 = (f32[88,128]{1,0:T(8,128)S(1)}, f32[88,128]{1,0:T(8,128)S(1)}, u32[]{:S(2)}, u32[]{:S(2)}) collective-permute-start(f32[88,128]{1,0:T(8,128)S(1)} %add_add_fusion.1), channel_id=1, source_target_pairs={{0,1},{1,0},{2,3},{3,2},{4,5},{5,4},{6,7},{7,6},{8,9},{9,8},{10,11... | collective-permute-start | bytes 135176 | tf_op jit(solution)/shard_map/ppermute | solution.py:21
  86.9 5.1 %collective-permute-start.28 = (f32[88,128]{1,0:T(8,128)S(1)}, f32[88,128]{1,0:T(8,128)S(1)}, u32[]{:S(2)}, u32[]{:S(2)}) collective-permute-start(f32[88,128]{1,0:T(8,128)S(1)} %add.52), channel_id=1, source_target_pairs={{0,32},{16,48},{32,1},{48,17},{1,33},{17,49},{33,0},{49,16},{2,34}... | collective-permute-start | bytes 135176 | tf_op jit(solution)/shard_map/ppermute | solution.py:28
  87.7 4.6 %collective-permute-start.29 = (f32[88,128]{1,0:T(8,128)S(1)}, f32[88,128]{1,0:T(8,128)S(1)}, u32[]{:S(2)}, u32[]{:S(2)}) collective-permute-start(f32[88,128]{1,0:T(8,128)S(1)} %add.52), channel_id=1, source_target_pairs={{0,16},{16,32},{32,48},{48,1},{1,17},{17,33},{33,49},{49,0},{2,18}... | collective-permute-start | bytes 135176 | tf_op jit(solution)/shard_map/ppermute | solution.py:28
  87.7 5.5 %collective-permute-start.30 = (f32[88,128]{1,0:T(8,128)S(1)}, f32[88,128]{1,0:T(8,128)S(1)}, u32[]{:S(2)}, u32[]{:S(2)}) collective-permute-start(f32[88,128]{1,0:T(8,128)S(1)} %add.52), channel_id=1, source_target_pairs={{0,49},{16,0},{32,16},{48,32},{1,48},{17,1},{33,17},{49,33},{2,51}... | collective-permute-start | bytes 135176 | tf_op jit(solution)/shard_map/ppermute | solution.py:28
  93.1 7.7 %collective-permute-start.31 = (f32[88,128]{1,0:T(8,128)S(1)}, f32[88,128]{1,0:T(8,128)S(1)}, u32[]{:S(2)}, u32[]{:S(2)}) collective-permute-start(f32[88,128]{1,0:T(8,128)S(1)} %add_add_fusion), channel_id=1, source_target_pairs={{0,8},{8,0},{1,9},{9,1},{2,10},{10,2},{3,11},{11,3},{4,12},{12,4},... | collective-permute-start | bytes 135176 | tf_op jit(solution)/shard_map/ppermute | solution.py:21
  (4 other events, 63.5 us)

commit v5 on v4

--- a/solution.py
+++ b/solution.py
@@ -28,8 +28,9 @@
     return lax.ppermute(value, ("zl", "zh"), [(at(z), at((z + step) % n)) for z in range(n)])
 
 
-def plan_kernel(per_device, tile, place_ref, rows_ref, cols_ref, plan_ref):
-    y0, z0, core0, x0, zh0, count = (place_ref[i] for i in range(6))
+def plan_kernel(per_device, tile, count_ref, rows_ref, cols_ref, plan_ref):
+    y0, z0, core0, x0, zh0 = (lax.axis_index(axis) for axis in AXES)
+    count = count_ref[0]
     slots = rows_ref.shape[1]
     slot = lax.broadcasted_iota(jnp.int32, (1, slots), 1)
     device, part = rows_ref[...] // per_device, rows_ref[...] % per_device
@@ -62,14 +63,13 @@
 def plan(tile_rows, tile_cols, count, per_device, tile):
     slots = tile_rows.shape[1]
     vmem = pl.BlockSpec(memory_space=pltpu.VMEM)
-    place = jnp.stack([lax.axis_index(axis) for axis in AXES] + [count]).astype(jnp.int32)
     return pl.pallas_call(
         lambda *refs: plan_kernel(per_device, tile, *refs),
         out_shape=jax.ShapeDtypeStruct((8, slots), jnp.int32),
         in_specs=[pl.BlockSpec(memory_space=pltpu.SMEM), vmem, vmem],
         out_specs=vmem,
         name="plan",
-    )(place, tile_rows, tile_cols)
+    )(count, tile_rows, tile_cols)
 
 
 def fetch_kernel(plan_ref, vals_ref, out_ref, token_ref, sems):
@@ -224,12 +224,12 @@
     return jnp.where(token[0] < 0, jnp.zeros_like(value), value)
 
 
-def gather_features(features, token):
+def gather_features(features, planned, fetched):
     by_z = jnp.concatenate([features] + [shift(features, "zl", -k) for k in (1, 2, 3)], 0)
-    opposite = after(shift(features, "y", 2), token)
+    opposite = after(shift(features, "y", 2), planned)
     opposite = jnp.concatenate([opposite] + [shift(opposite, "zl", -k) for k in (1, 2, 3)], 0)
     mine = [by_z, shift(by_z, "y", -1), opposite, shift(by_z, "y", 1)]
-    return mine + [shift(piece, "core", 1) for piece in mine]
+    return mine + [shift(piece, "core", 1) for piece in [after(by_z, fetched)] + mine[1:]]
 
 
 def sum_everywhere(keep, give, core, classes):
@@ -252,11 +252,11 @@
     out_rows = nodes * lax.axis_size("x")
     core = lax.axis_index("core").astype(jnp.int32)
     lists = plan(
-        tile_rows.reshape(1, slots), tile_cols.reshape(1, slots), tile_count.reshape(()), nodes // tile, tile
+        tile_rows.reshape(1, slots), tile_cols.reshape(1, slots), tile_count.reshape(1), nodes // tile, tile
     )
 
-    vals, token = fetch(lists, vals)
-    pieces = gather_features(features, token)
+    vals, fetched = fetch(lists, vals)
+    pieces = gather_features(features, lists[3], fetched)
     table, own, *away = aggregate(functools.partial(far_kernel, len(pieces)), lists, vals, pieces, out_rows, True)
     give = own + sum(shift(away[k], "x", k + 1).astype(jnp.float32) for k in (1, 0, 2))
     own, *away = aggregate(near_kernel, lists, vals, [table], out_rows, False)

time: 102 us -> 100 us (0.980)
  starting transfers between devices: 63 us -> 59.2 us
  waiting for transfers between devices: 23 us -> 25.2 us
    ppermute x29, starting transfers between devices: 59.5 us -> 55.1 us  [shift(): return lax.ppermute(value, axes, [(i, (i + step) % n) for i in range(n)])]
    ppermute x29, waiting for transfers between devices: 20.2 us -> 23.2 us  [shift(): return lax.ppermute(value, axes, [(i, (i + step) % n) for i in range(n)])]
    slice x0 -> x1, local copies, waits for them, and re-layouts: none -> 1.21 us  [after(): return jnp.where(token[0] < 0, jnp.zeros_like(value), value)]
  transfers between devices with their start and end apart: 32 -> 32, of which waited for: 18 -> 15; matrix products, arithmetic and copies ran while one was open for 2% -> 1% of each run, Pallas kernels for 7% -> 7%
where the time goes in v5:
time: 100 us
  starting transfers between devices  59.2 us (59%)
  waiting for transfers between devices  25.2 us (25%)
  Pallas kernels  10.2 us (10%)
  between operations  2.69 us (3%)
  local copies, waits for them, and re-layouts  1.99 us (2%)
    ppermute x29, starting transfers between devices, shift(): return lax.ppermute(value, axes, [(i, (i + step) % n) for i in range(n)])  55.1 us
    ppermute x29, waiting for transfers between devices, shift(): return lax.ppermute(value, axes, [(i, (i + step) % n) for i in range(n)])  23.2 us
    ppermute x3, starting transfers between devices, shift_z(): lax.ppermute(value, ('zl', 'zh'), [(at(z), at((z + step) % n)) for z in r...  4.12 us
    pallas_call x2, Pallas kernels, aggregate(): pl.pallas_call(kernel, out_shape=out, in_specs=[pl.BlockSpec(memory_space...  4.05 us
    pallas_call x1, Pallas kernels, fetch(): pl.pallas_call(fetch_kernel, out_shape=(jax.ShapeDtypeStruct(vals.shape,...  3.43 us
    ppermute x3, waiting for transfers between devices, shift_z(): lax.ppermute(value, ('zl', 'zh'), [(at(z), at((z + step) % n)) for z in r...  2.04 us
  transfers between devices with their start and end apart: 32, of which 15 were waited for; matrix products, arithmetic and copies ran while one was open for 1% of the time, Pallas kernels for 7%

profile of v5, /device:TPU:1, one launch (start us, length us, event | category | flops | bytes accessed | tf_op | source)
XLA Modules:
  0.0 100.2 jit_solution(6209813640388475183)
XLA Ops:
  0.6 3.8 %collective-permute-start.4 = (bf16[512,128]{1,0:T(8,128)(2,1)}, bf16[512,128]{1,0:T(8,128)(2,1)S(1)}, u32[]{:S(2)}, u32[]{:S(2)}) collective-permute-start(bf16[512,128]{1,0:T(8,128)(2,1)} %param.7), channel_id=1, source_target_pairs={{0,128},{64,192},{128,0},{192,64},{1,129},{65,193},{129,1},{193,65... | collective-permute-start | bytes 393224 | tf_op jit(solution)/shard_map/ppermute | solution.py:21
  4.5 4.3 %collective-permute-start = (bf16[512,128]{1,0:T(8,128)(2,1)}, bf16[512,128]{1,0:T(8,128)(2,1)S(1)}, u32[]{:S(2)}, u32[]{:S(2)}) collective-permute-start(bf16[512,128]{1,0:T(8,128)(2,1)} %param.7), channel_id=1, source_target_pairs={{0,48},{16,0},{32,16},{48,32},{1,49},{17,1},{33,17},{49,33},{2,50}... | collective-permute-start | bytes 393224 | tf_op jit(solution)/shard_map/ppermute | solution.py:21
  9.7 1.6 %plan.1.plan_ref = s32[8,256]{1,0:T(8,128)} custom-call(s32[1]{0:T(128)} %bitcast.12.refs_0_, s32[1,256]{1,0:T(1,128)} %bitcast.16, s32[1,256]{1,0:T(1,128)} %bitcast.17), custom_call_target="tpu_custom_call" | custom-call | tf_op jit(solution)/shard_map/plan/pallas_call | solution.py:66
  11.4 1.2 %slice.11 = s32[1,1]{1,0:T(1,128)} slice(s32[8,256]{1,0:T(8,128)} %plan.1.plan_ref), slice={[3:4], [0:1]} | slice | bytes 8 | tf_op jit(solution)/shard_map/slice | solution.py:224
  13.3 3.4 %fetch.1 = (bf16[256,128,128]{2,1,0:T(8,128)(2,1)S(1)}, s32[1]{0:T(128)}) custom-call(s32[8,256]{1,0:T(8,128)S(1)} %copy-done, bf16[256,128,128]{2,1,0:T(8,128)(2,1)} %bitcast.15), custom_call_target="tpu_custom_call" | custom-call | bytes 16777216 | tf_op jit(solution)/shard_map/fetch/pallas_call | solution.py:92
  18.0 2.4 %collective-permute-start.5 = (bf16[512,128]{1,0:T(8,128)(2,1)S(1)}, bf16[512,128]{1,0:T(8,128)(2,1)S(1)}, u32[]{:S(2)}, u32[]{:S(2)}) collective-permute-start(bf16[512,128]{1,0:T(8,128)(2,1)S(1)} %broadcast_select_fusion.1), channel_id=1, source_target_pairs={{0,48},{16,0},{32,16},{48,32},{1,49},{17,1},{33,17},{49,33},{2,50}... | collective-permute-start | bytes 393224 | tf_op jit(solution)/shard_map/ppermute | solution.py:21
  21.1 1.5 %collective-permute-start.3 = (bf16[2048,128]{1,0:T(8,128)(2,1)S(1)}, bf16[2048,128]{1,0:T(8,128)(2,1)S(1)}, u32[]{:S(2)}, u32[]{:S(2)}) collective-permute-start(bf16[2048,128]{1,0:T(8,128)(2,1)S(1)} %constant_dynamic-update-slice_fusion.refs_0_), channel_id=1, source_target_pairs={{0,192},{64,0},{128,64},{192,128},{1,193},{65,1},{129,65},{193,129... | collective-permute-start | bytes 1572872 | tf_op jit(solution)/shard_map/ppermute | solution.py:21
  22.7 3.5 %collective-permute-start.9 = (bf16[2048,128]{1,0:T(8,128)(2,1)S(1)}, bf16[2048,128]{1,0:T(8,128)(2,1)S(1)}, u32[]{:S(2)}, u32[]{:S(2)}) collective-permute-start(bf16[2048,128]{1,0:T(8,128)(2,1)S(1)} %broadcast_select_fusion), channel_id=1, source_target_pairs={{0,8},{8,0},{1,9},{9,1},{2,10},{10,2},{3,11},{11,3},{4,12},{12,4},... | collective-permute-start | bytes 1572872 | tf_op jit(solution)/shard_map/ppermute | solution.py:21
  26.2 5.8 %collective-permute-done.6 = bf16[512,128]{1,0:T(8,128)(2,1)S(1)} collective-permute-done((bf16[512,128]{1,0:T(8,128)(2,1)S(1)}, bf16[512,128]{1,0:T(8,128)(2,1)S(1)}, u32[]{:S(2)}, u32[]{:S(2)}) %collective-permute-start.6) | collective-permute-done | bytes 131104 | tf_op jit(solution)/shard_map/ppermute | solution.py:21
  32.1 1.9 %collective-permute-start.11 = (bf16[2048,128]{1,0:T(8,128)(2,1)S(1)}, bf16[2048,128]{1,0:T(8,128)(2,1)S(1)}, u32[]{:S(2)}, u32[]{:S(2)}) collective-permute-start(bf16[2048,128]{1,0:T(8,128)(2,1)S(1)} %pad_maximum_fusion.refs_2_), channel_id=1, source_target_pairs={{0,8},{8,0},{1,9},{9,1},{2,10},{10,2},{3,11},{11,3},{4,12},{12,4},... | collective-permute-start | bytes 1572872 | tf_op jit(solution)/shard_map/ppermute | solution.py:21
  34.0 1.5 %collective-permute-start.10 = (bf16[2048,128]{1,0:T(8,128)(2,1)S(1)}, bf16[2048,128]{1,0:T(8,128)(2,1)S(1)}, u32[]{:S(2)}, u32[]{:S(2)}) collective-permute-start(bf16[2048,128]{1,0:T(8,128)(2,1)S(1)} %collective-permute-done.3.refs_1_), channel_id=1, source_target_pairs={{0,8},{8,0},{1,9},{9,1},{2,10},{10,2},{3,11},{11,3},{4,12},{12,4},... | collective-permute-start | bytes 1572872 | tf_op jit(solution)/shard_map/ppermute | solution.py:21
  35.5 2.6 %collective-permute-start.12 = (bf16[2048,128]{1,0:T(8,128)(2,1)S(1)}, bf16[2048,128]{1,0:T(8,128)(2,1)S(1)}, u32[]{:S(2)}, u32[]{:S(2)}) collective-permute-start(bf16[2048,128]{1,0:T(8,128)(2,1)S(1)} %collective-permute-done.8.refs_3_), channel_id=1, source_target_pairs={{0,8},{8,0},{1,9},{9,1},{2,10},{10,2},{3,11},{11,3},{4,12},{12,4},... | collective-permute-start | bytes 1572872 | tf_op jit(solution)/shard_map/ppermute | solution.py:21
  38.2 1.5 %collective-permute-done.12.refs_7_ = bf16[2048,128]{1,0:T(8,128)(2,1)S(1)} collective-permute-done((bf16[2048,128]{1,0:T(8,128)(2,1)S(1)}, bf16[2048,128]{1,0:T(8,128)(2,1)S(1)}, u32[]{:S(2)}, u32[]{:S(2)}) %collective-permute-start.12) | collective-permute-done | bytes 524320 | tf_op jit(solution)/shard_map/ppermute | solution.py:21
  39.7 2.1 %far_rows.1 = (bf16[16384,128]{1,0:T(8,128)(2,1)S(1)}, f32[512,128]{1,0:T(8,128)S(1)}, bf16[512,128]{1,0:T(8,128)(2,1)S(1)}, bf16[512,128]{1,0:T(8,128)(2,1)S(1)}, bf16[512,128]{1,0:T(8,128)(2,1)S(1)}) custom-call(s32[8,256]{1,0:T(8,128)S(1)} %copy-done.1, bf16[256,128,128]{2,1,0:T(8,128)(2,1)S(1)} %get-tuple-element.16.vals_ref, ...), custom_call_target="tpu_custom_call" | custom-call | flops 536870912 | bytes 8388608 | tf_op jit(solution)/shard_map/far_rows/pallas_call | solution.py:164
  41.8 2.5 %collective-permute-start.13 = (bf16[512,128]{1,0:T(8,128)(2,1)S(1)}, bf16[512,128]{1,0:T(8,128)(2,1)S(1)}, u32[]{:S(2)}, u32[]{:S(2)}) collective-permute-start(bf16[512,128]{1,0:T(8,128)(2,1)S(1)} %get-tuple-element.21), channel_id=1, source_target_pairs={{0,4},{2,6},{4,0},{6,2},{1,5},{3,7},{5,1},{7,3},{8,12},{10,14},{12... | collective-permute-start | bytes 393224 | tf_op jit(solution)/shard_map/ppermute | solution.py:21
  44.5 2.5 %collective-permute-start.15 = (bf16[512,128]{1,0:T(8,128)(2,1)S(1)}, bf16[512,128]{1,0:T(8,128)(2,1)S(1)}, u32[]{:S(2)}, u32[]{:S(2)}) collective-permute-start(bf16[512,128]{1,0:T(8,128)(2,1)S(1)} %get-tuple-element.23), channel_id=1, source_target_pairs={{0,6},{2,0},{4,2},{6,4},{1,7},{3,1},{5,3},{7,5},{8,14},{10,8},{12,... | collective-permute-start | bytes 393224 | tf_op jit(solution)/shard_map/ppermute | solution.py:21
  47.0 1.9 %near_rows.1 = (f32[512,128]{1,0:T(8,128)S(1)}, bf16[512,128]{1,0:T(8,128)(2,1)S(1)}, bf16[512,128]{1,0:T(8,128)(2,1)S(1)}, bf16[512,128]{1,0:T(8,128)(2,1)S(1)}) custom-call(s32[8,256]{1,0:T(8,128)S(1)} %copy-done.1, bf16[256,128,128]{2,1,0:T(8,128)(2,1)S(1)} %get-tuple-element.16.vals_ref, bf16[16384,128]{1,0:T(8,128)(2,1)S(1)} %get-tuple-element.18.table_ref), custom_call_target="tpu_custom_call" | custom-call | flops 536870912 | bytes 8388608 | tf_op jit(solution)/shard_map/near_rows/pallas_call | solution.py:164
  49.2 2.7 %collective-permute-start.19 = (bf16[512,128]{1,0:T(8,128)(2,1)S(1)}, bf16[512,128]{1,0:T(8,128)(2,1)S(1)}, u32[]{:S(2)}, u32[]{:S(2)}) collective-permute-start(bf16[512,128]{1,0:T(8,128)(2,1)S(1)} %get-tuple-element.26), channel_id=1, source_target_pairs={{0,6},{2,0},{4,2},{6,4},{1,7},{3,1},{5,3},{7,5},{8,14},{10,8},{12,... | collective-permute-start | bytes 393224 | tf_op jit(solution)/shard_map/ppermute | solution.py:21
  51.9 4.4 %collective-permute-start.16 = (bf16[512,128]{1,0:T(8,128)(2,1)S(1)}, bf16[512,128]{1,0:T(8,128)(2,1)S(1)}, u32[]{:S(2)}, u32[]{:S(2)}) collective-permute-start(bf16[512,128]{1,0:T(8,128)(2,1)S(1)} %add_convert_fusion), channel_id=1, source_target_pairs={{0,1},{1,0},{2,3},{3,2},{4,5},{5,4},{6,7},{7,6},{8,9},{9,8},{10,11... | collective-permute-start | bytes 393224 | tf_op jit(solution)/shard_map/ppermute | solution.py:21
  56.3 2.1 %collective-permute-done.18.refs_4_ = bf16[512,128]{1,0:T(8,128)(2,1)S(1)} collective-permute-done((bf16[512,128]{1,0:T(8,128)(2,1)S(1)}, bf16[512,128]{1,0:T(8,128)(2,1)S(1)}, u32[]{:S(2)}, u32[]{:S(2)}) %collective-permute-start.18) | collective-permute-done | bytes 131104 | tf_op jit(solution)/shard_map/ppermute | solution.py:21
  58.4 1.4 %collective-permute-done.16.refs_2_ = bf16[512,128]{1,0:T(8,128)(2,1)S(1)} collective-permute-done((bf16[512,128]{1,0:T(8,128)(2,1)S(1)}, bf16[512,128]{1,0:T(8,128)(2,1)S(1)}, u32[]{:S(2)}, u32[]{:S(2)}) %collective-permute-start.16) | collective-permute-done | bytes 131104 | tf_op jit(solution)/shard_map/ppermute | solution.py:21
  60.9 3.2 %collective-permute-start.20 = (f32[88,128]{1,0:T(8,128)S(1)}, f32[88,128]{1,0:T(8,128)S(1)}, u32[]{:S(2)}, u32[]{:S(2)}) collective-permute-start(f32[88,128]{1,0:T(8,128)S(1)} %get-tuple-element.29), channel_id=1, source_target_pairs={{0,8},{8,0},{1,9},{9,1},{2,10},{10,2},{3,11},{11,3},{4,12},{12,4},... | collective-permute-start | bytes 135176 | tf_op jit(solution)/shard_map/ppermute | solution.py:21
  65.4 2.4 %collective-permute-start.22 = (f32[88,128]{1,0:T(8,128)S(1)}, f32[88,128]{1,0:T(8,128)S(1)}, u32[]{:S(2)}, u32[]{:S(2)}) collective-permute-start(f32[88,128]{1,0:T(8,128)S(1)} %add.45), channel_id=1, source_target_pairs={{0,64},{64,128},{128,192},{192,0},{1,65},{65,129},{129,193},{193,1... | collective-permute-start | bytes 135176 | tf_op jit(solution)/shard_map/ppermute | solution.py:21
  68.1 1.3 %collective-permute-done.21 = f32[88,128]{1,0:T(8,128)S(1)} collective-permute-done((f32[88,128]{1,0:T(8,128)S(1)}, f32[88,128]{1,0:T(8,128)S(1)}, u32[]{:S(2)}, u32[]{:S(2)}) %collective-permute-start.21) | collective-permute-done | bytes 45088 | tf_op jit(solution)/shard_map/ppermute | solution.py:21
  71.0 1.6 %collective-permute-start.24 = (f32[88,128]{1,0:T(8,128)S(1)}, f32[88,128]{1,0:T(8,128)S(1)}, u32[]{:S(2)}, u32[]{:S(2)}) collective-permute-start(f32[88,128]{1,0:T(8,128)S(1)} %add_add_fusion.2), channel_id=1, source_target_pairs={{0,4},{2,6},{4,0},{6,2},{1,5},{3,7},{5,1},{7,3},{8,12},{10,14},{12... | collective-permute-start | bytes 135176 | tf_op jit(solution)/shard_map/ppermute | solution.py:21
  72.6 3.2 %collective-permute-start.25 = (f32[88,128]{1,0:T(8,128)S(1)}, f32[88,128]{1,0:T(8,128)S(1)}, u32[]{:S(2)}, u32[]{:S(2)}) collective-permute-start(f32[88,128]{1,0:T(8,128)S(1)} %add_add_fusion.2), channel_id=1, source_target_pairs={{0,2},{2,4},{4,6},{6,0},{1,3},{3,5},{5,7},{7,1},{8,10},{10,12},{12... | collective-permute-start | bytes 135176 | tf_op jit(solution)/shard_map/ppermute | solution.py:21
  77.0 2.1 %collective-permute-done.26 = f32[88,128]{1,0:T(8,128)S(1)} collective-permute-done((f32[88,128]{1,0:T(8,128)S(1)}, f32[88,128]{1,0:T(8,128)S(1)}, u32[]{:S(2)}, u32[]{:S(2)}) %collective-permute-start.26) | collective-permute-done | bytes 45088 | tf_op jit(solution)/shard_map/ppermute | solution.py:21
  79.0 2.5 %collective-permute-start.27 = (f32[88,128]{1,0:T(8,128)S(1)}, f32[88,128]{1,0:T(8,128)S(1)}, u32[]{:S(2)}, u32[]{:S(2)}) collective-permute-start(f32[88,128]{1,0:T(8,128)S(1)} %add_add_fusion.1), channel_id=1, source_target_pairs={{0,1},{1,0},{2,3},{3,2},{4,5},{5,4},{6,7},{7,6},{8,9},{9,8},{10,11... | collective-permute-start | bytes 135176 | tf_op jit(solution)/shard_map/ppermute | solution.py:21
  81.5 4.4 %collective-permute-done.27 = f32[88,128]{1,0:T(8,128)S(1)} collective-permute-done((f32[88,128]{1,0:T(8,128)S(1)}, f32[88,128]{1,0:T(8,128)S(1)}, u32[]{:S(2)}, u32[]{:S(2)}) %collective-permute-start.27) | collective-permute-done | bytes 45088 | tf_op jit(solution)/shard_map/ppermute | solution.py:21
  85.9 1.4 %collective-permute-start.28 = (f32[88,128]{1,0:T(8,128)S(1)}, f32[88,128]{1,0:T(8,128)S(1)}, u32[]{:S(2)}, u32[]{:S(2)}) collective-permute-start(f32[88,128]{1,0:T(8,128)S(1)} %add.52), channel_id=1, source_target_pairs={{0,32},{16,48},{32,1},{48,17},{1,33},{17,49},{33,0},{49,16},{2,34}... | collective-permute-start | bytes 135176 | tf_op jit(solution)/shard_map/ppermute | solution.py:28
  87.3 1.9 %collective-permute-start.29 = (f32[88,128]{1,0:T(8,128)S(1)}, f32[88,128]{1,0:T(8,128)S(1)}, u32[]{:S(2)}, u32[]{:S(2)}) collective-permute-start(f32[88,128]{1,0:T(8,128)S(1)} %add.52), channel_id=1, source_target_pairs={{0,16},{16,32},{32,48},{48,1},{1,17},{17,33},{33,49},{49,0},{2,18}... | collective-permute-start | bytes 135176 | tf_op jit(solution)/shard_map/ppermute | solution.py:28
  92.1 6.5 %collective-permute-start.31 = (f32[88,128]{1,0:T(8,128)S(1)}, f32[88,128]{1,0:T(8,128)S(1)}, u32[]{:S(2)}, u32[]{:S(2)}) collective-permute-start(f32[88,128]{1,0:T(8,128)S(1)} %add_add_fusion), channel_id=1, source_target_pairs={{0,8},{8,0},{1,9},{9,1},{2,10},{10,2},{3,11},{11,3},{4,12},{12,4},... | collective-permute-start | bytes 135176 | tf_op jit(solution)/shard_map/ppermute | solution.py:21
  (63 shorter events, 12.2 us)
Async XLA Ops:
  0.6 17.4 %collective-permute-start.4 = (bf16[512,128]{1,0:T(8,128)(2,1)}, bf16[512,128]{1,0:T(8,128)(2,1)S(1)}, u32[]{:S(2)}, u32[]{:S(2)}) collective-permute-start(bf16[512,128]{1,0:T(8,128)(2,1)} %param.7), channel_id=1, source_target_pairs={{0,128},{64,192},{128,0},{192,64},{1,129},{65,193},{129,1},{193,65... | collective-permute-start | bytes 393224 | tf_op jit(solution)/shard_map/ppermute | solution.py:21
  4.5 16.6 %collective-permute-start = (bf16[512,128]{1,0:T(8,128)(2,1)}, bf16[512,128]{1,0:T(8,128)(2,1)S(1)}, u32[]{:S(2)}, u32[]{:S(2)}) collective-permute-start(bf16[512,128]{1,0:T(8,128)(2,1)} %param.7), channel_id=1, source_target_pairs={{0,48},{16,0},{32,16},{48,32},{1,49},{17,1},{33,17},{49,33},{2,50}... | collective-permute-start | bytes 393224 | tf_op jit(solution)/shard_map/ppermute | solution.py:21
  8.8 12.2 %collective-permute-start.1 = (bf16[512,128]{1,0:T(8,128)(2,1)}, bf16[512,128]{1,0:T(8,128)(2,1)S(1)}, u32[]{:S(2)}, u32[]{:S(2)}) collective-permute-start(bf16[512,128]{1,0:T(8,128)(2,1)} %param.7), channel_id=1, source_target_pairs={{0,32},{16,48},{32,0},{48,16},{1,33},{17,49},{33,1},{49,17},{2,34}... | collective-permute-start | bytes 393224 | tf_op jit(solution)/shard_map/ppermute | solution.py:21
  8.8 12.3 %collective-permute-start.2 = (bf16[512,128]{1,0:T(8,128)(2,1)}, bf16[512,128]{1,0:T(8,128)(2,1)S(1)}, u32[]{:S(2)}, u32[]{:S(2)}) collective-permute-start(bf16[512,128]{1,0:T(8,128)(2,1)} %param.7), channel_id=1, source_target_pairs={{0,16},{16,32},{32,48},{48,0},{1,17},{17,33},{33,49},{49,1},{2,18}... | collective-permute-start | bytes 393224 | tf_op jit(solution)/shard_map/ppermute | solution.py:21
  18.0 4.7 %collective-permute-start.5 = (bf16[512,128]{1,0:T(8,128)(2,1)S(1)}, bf16[512,128]{1,0:T(8,128)(2,1)S(1)}, u32[]{:S(2)}, u32[]{:S(2)}) collective-permute-start(bf16[512,128]{1,0:T(8,128)(2,1)S(1)} %broadcast_select_fusion.1), channel_id=1, source_target_pairs={{0,48},{16,0},{32,16},{48,32},{1,49},{17,1},{33,17},{49,33},{2,50}... | collective-permute-start | bytes 393224 | tf_op jit(solution)/shard_map/ppermute | solution.py:21
  20.4 11.6 %collective-permute-start.6 = (bf16[512,128]{1,0:T(8,128)(2,1)S(1)}, bf16[512,128]{1,0:T(8,128)(2,1)S(1)}, u32[]{:S(2)}, u32[]{:S(2)}) collective-permute-start(bf16[512,128]{1,0:T(8,128)(2,1)S(1)} %broadcast_select_fusion.1), channel_id=1, source_target_pairs={{0,32},{16,48},{32,0},{48,16},{1,33},{17,49},{33,1},{49,17},{2,34}... | collective-permute-start | bytes 393224 | tf_op jit(solution)/shard_map/ppermute | solution.py:21
  21.0 11.0 %collective-permute-start.7 = (bf16[512,128]{1,0:T(8,128)(2,1)S(1)}, bf16[512,128]{1,0:T(8,128)(2,1)S(1)}, u32[]{:S(2)}, u32[]{:S(2)}) collective-permute-start(bf16[512,128]{1,0:T(8,128)(2,1)S(1)} %broadcast_select_fusion.1), channel_id=1, source_target_pairs={{0,16},{16,32},{32,48},{48,0},{1,17},{17,33},{33,49},{49,1},{2,18}... | collective-permute-start | bytes 393224 | tf_op jit(solution)/shard_map/ppermute | solution.py:21
  21.1 12.9 %collective-permute-start.3 = (bf16[2048,128]{1,0:T(8,128)(2,1)S(1)}, bf16[2048,128]{1,0:T(8,128)(2,1)S(1)}, u32[]{:S(2)}, u32[]{:S(2)}) collective-permute-start(bf16[2048,128]{1,0:T(8,128)(2,1)S(1)} %constant_dynamic-update-slice_fusion.refs_0_), channel_id=1, source_target_pairs={{0,192},{64,0},{128,64},{192,128},{1,193},{65,1},{129,65},{193,129... | collective-permute-start | bytes 1572872 | tf_op jit(solution)/shard_map/ppermute | solution.py:21
  22.6 12.9 %collective-permute-start.8 = (bf16[2048,128]{1,0:T(8,128)(2,1)S(1)}, bf16[2048,128]{1,0:T(8,128)(2,1)S(1)}, u32[]{:S(2)}, u32[]{:S(2)}) collective-permute-start(bf16[2048,128]{1,0:T(8,128)(2,1)S(1)} %constant_dynamic-update-slice_fusion.refs_0_), channel_id=1, source_target_pairs={{0,64},{64,128},{128,192},{192,0},{1,65},{65,129},{129,193},{193,1... | collective-permute-start | bytes 1572872 | tf_op jit(solution)/shard_map/ppermute | solution.py:21
  22.7 15.4 %collective-permute-start.9 = (bf16[2048,128]{1,0:T(8,128)(2,1)S(1)}, bf16[2048,128]{1,0:T(8,128)(2,1)S(1)}, u32[]{:S(2)}, u32[]{:S(2)}) collective-permute-start(bf16[2048,128]{1,0:T(8,128)(2,1)S(1)} %broadcast_select_fusion), channel_id=1, source_target_pairs={{0,8},{8,0},{1,9},{9,1},{2,10},{10,2},{3,11},{11,3},{4,12},{12,4},... | collective-permute-start | bytes 1572872 | tf_op jit(solution)/shard_map/ppermute | solution.py:21
  32.1 6.1 %collective-permute-start.11 = (bf16[2048,128]{1,0:T(8,128)(2,1)S(1)}, bf16[2048,128]{1,0:T(8,128)(2,1)S(1)}, u32[]{:S(2)}, u32[]{:S(2)}) collective-permute-start(bf16[2048,128]{1,0:T(8,128)(2,1)S(1)} %pad_maximum_fusion.refs_2_), channel_id=1, source_target_pairs={{0,8},{8,0},{1,9},{9,1},{2,10},{10,2},{3,11},{11,3},{4,12},{12,4},... | collective-permute-start | bytes 1572872 | tf_op jit(solution)/shard_map/ppermute | solution.py:21
  34.0 4.1 %collective-permute-start.10 = (bf16[2048,128]{1,0:T(8,128)(2,1)S(1)}, bf16[2048,128]{1,0:T(8,128)(2,1)S(1)}, u32[]{:S(2)}, u32[]{:S(2)}) collective-permute-start(bf16[2048,128]{1,0:T(8,128)(2,1)S(1)} %collective-permute-done.3.refs_1_), channel_id=1, source_target_pairs={{0,8},{8,0},{1,9},{9,1},{2,10},{10,2},{3,11},{11,3},{4,12},{12,4},... | collective-permute-start | bytes 1572872 | tf_op jit(solution)/shard_map/ppermute | solution.py:21
  35.5 4.2 %collective-permute-start.12 = (bf16[2048,128]{1,0:T(8,128)(2,1)S(1)}, bf16[2048,128]{1,0:T(8,128)(2,1)S(1)}, u32[]{:S(2)}, u32[]{:S(2)}) collective-permute-start(bf16[2048,128]{1,0:T(8,128)(2,1)S(1)} %collective-permute-done.8.refs_3_), channel_id=1, source_target_pairs={{0,8},{8,0},{1,9},{9,1},{2,10},{10,2},{3,11},{11,3},{4,12},{12,4},... | collective-permute-start | bytes 1572872 | tf_op jit(solution)/shard_map/ppermute | solution.py:21
  41.8 7.3 %collective-permute-start.13 = (bf16[512,128]{1,0:T(8,128)(2,1)S(1)}, bf16[512,128]{1,0:T(8,128)(2,1)S(1)}, u32[]{:S(2)}, u32[]{:S(2)}) collective-permute-start(bf16[512,128]{1,0:T(8,128)(2,1)S(1)} %get-tuple-element.21), channel_id=1, source_target_pairs={{0,4},{2,6},{4,0},{6,2},{1,5},{3,7},{5,1},{7,3},{8,12},{10,14},{12... | collective-permute-start | bytes 393224 | tf_op jit(solution)/shard_map/ppermute | solution.py:21
  44.4 7.5 %collective-permute-start.14 = (bf16[512,128]{1,0:T(8,128)(2,1)S(1)}, bf16[512,128]{1,0:T(8,128)(2,1)S(1)}, u32[]{:S(2)}, u32[]{:S(2)}) collective-permute-start(bf16[512,128]{1,0:T(8,128)(2,1)S(1)} %get-tuple-element.22), channel_id=1, source_target_pairs={{0,2},{2,4},{4,6},{6,0},{1,3},{3,5},{5,7},{7,1},{8,10},{10,12},{12... | collective-permute-start | bytes 393224 | tf_op jit(solution)/shard_map/ppermute | solution.py:21
  44.5 7.3 %collective-permute-start.15 = (bf16[512,128]{1,0:T(8,128)(2,1)S(1)}, bf16[512,128]{1,0:T(8,128)(2,1)S(1)}, u32[]{:S(2)}, u32[]{:S(2)}) collective-permute-start(bf16[512,128]{1,0:T(8,128)(2,1)S(1)} %get-tuple-element.23), channel_id=1, source_target_pairs={{0,6},{2,0},{4,2},{6,4},{1,7},{3,1},{5,3},{7,5},{8,14},{10,8},{12,... | collective-permute-start | bytes 393224 | tf_op jit(solution)/shard_map/ppermute | solution.py:21
  49.0 7.3 %collective-permute-start.17 = (bf16[512,128]{1,0:T(8,128)(2,1)S(1)}, bf16[512,128]{1,0:T(8,128)(2,1)S(1)}, u32[]{:S(2)}, u32[]{:S(2)}) collective-permute-start(bf16[512,128]{1,0:T(8,128)(2,1)S(1)} %get-tuple-element.24), channel_id=1, source_target_pairs={{0,4},{2,6},{4,0},{6,2},{1,5},{3,7},{5,1},{7,3},{8,12},{10,14},{12... | collective-permute-start | bytes 393224 | tf_op jit(solution)/shard_map/ppermute | solution.py:21
  49.1 9.3 %collective-permute-start.18 = (bf16[512,128]{1,0:T(8,128)(2,1)S(1)}, bf16[512,128]{1,0:T(8,128)(2,1)S(1)}, u32[]{:S(2)}, u32[]{:S(2)}) collective-permute-start(bf16[512,128]{1,0:T(8,128)(2,1)S(1)} %get-tuple-element.25), channel_id=1, source_target_pairs={{0,2},{2,4},{4,6},{6,0},{1,3},{3,5},{5,7},{7,1},{8,10},{10,12},{12... | collective-permute-start | bytes 393224 | tf_op jit(solution)/shard_map/ppermute | solution.py:21
  49.2 9.2 %collective-permute-start.19 = (bf16[512,128]{1,0:T(8,128)(2,1)S(1)}, bf16[512,128]{1,0:T(8,128)(2,1)S(1)}, u32[]{:S(2)}, u32[]{:S(2)}) collective-permute-start(bf16[512,128]{1,0:T(8,128)(2,1)S(1)} %get-tuple-element.26), channel_id=1, source_target_pairs={{0,6},{2,0},{4,2},{6,4},{1,7},{3,1},{5,3},{7,5},{8,14},{10,8},{12,... | collective-permute-start | bytes 393224 | tf_op jit(solution)/shard_map/ppermute | solution.py:21
  51.9 7.9 %collective-permute-start.16 = (bf16[512,128]{1,0:T(8,128)(2,1)S(1)}, bf16[512,128]{1,0:T(8,128)(2,1)S(1)}, u32[]{:S(2)}, u32[]{:S(2)}) collective-permute-start(bf16[512,128]{1,0:T(8,128)(2,1)S(1)} %add_convert_fusion), channel_id=1, source_target_pairs={{0,1},{1,0},{2,3},{3,2},{4,5},{5,4},{6,7},{7,6},{8,9},{9,8},{10,11... | collective-permute-start | bytes 393224 | tf_op jit(solution)/shard_map/ppermute | solution.py:21
  60.9 4.0 %collective-permute-start.20 = (f32[88,128]{1,0:T(8,128)S(1)}, f32[88,128]{1,0:T(8,128)S(1)}, u32[]{:S(2)}, u32[]{:S(2)}) collective-permute-start(f32[88,128]{1,0:T(8,128)S(1)} %get-tuple-element.29), channel_id=1, source_target_pairs={{0,8},{8,0},{1,9},{9,1},{2,10},{10,2},{3,11},{11,3},{4,12},{12,4},... | collective-permute-start | bytes 135176 | tf_op jit(solution)/shard_map/ppermute | solution.py:21
  64.9 4.4 %collective-permute-start.21 = (f32[88,128]{1,0:T(8,128)S(1)}, f32[88,128]{1,0:T(8,128)S(1)}, u32[]{:S(2)}, u32[]{:S(2)}) collective-permute-start(f32[88,128]{1,0:T(8,128)S(1)} %add.45), channel_id=1, source_target_pairs={{0,128},{64,192},{128,0},{192,64},{1,129},{65,193},{129,1},{193,65... | collective-permute-start | bytes 135176 | tf_op jit(solution)/shard_map/ppermute | solution.py:21
  65.4 5.0 %collective-permute-start.22 = (f32[88,128]{1,0:T(8,128)S(1)}, f32[88,128]{1,0:T(8,128)S(1)}, u32[]{:S(2)}, u32[]{:S(2)}) collective-permute-start(f32[88,128]{1,0:T(8,128)S(1)} %add.45), channel_id=1, source_target_pairs={{0,64},{64,128},{128,192},{192,0},{1,65},{65,129},{129,193},{193,1... | collective-permute-start | bytes 135176 | tf_op jit(solution)/shard_map/ppermute | solution.py:21
  67.8 3.2 %collective-permute-start.23 = (f32[88,128]{1,0:T(8,128)S(1)}, f32[88,128]{1,0:T(8,128)S(1)}, u32[]{:S(2)}, u32[]{:S(2)}) collective-permute-start(f32[88,128]{1,0:T(8,128)S(1)} %add.45), channel_id=1, source_target_pairs={{0,192},{64,0},{128,64},{192,128},{1,193},{65,1},{129,65},{193,129... | collective-permute-start | bytes 135176 | tf_op jit(solution)/shard_map/ppermute | solution.py:21
  71.0 4.8 %collective-permute-start.24 = (f32[88,128]{1,0:T(8,128)S(1)}, f32[88,128]{1,0:T(8,128)S(1)}, u32[]{:S(2)}, u32[]{:S(2)}) collective-permute-start(f32[88,128]{1,0:T(8,128)S(1)} %add_add_fusion.2), channel_id=1, source_target_pairs={{0,4},{2,6},{4,0},{6,2},{1,5},{3,7},{5,1},{7,3},{8,12},{10,14},{12... | collective-permute-start | bytes 135176 | tf_op jit(solution)/shard_map/ppermute | solution.py:21
  72.6 4.4 %collective-permute-start.25 = (f32[88,128]{1,0:T(8,128)S(1)}, f32[88,128]{1,0:T(8,128)S(1)}, u32[]{:S(2)}, u32[]{:S(2)}) collective-permute-start(f32[88,128]{1,0:T(8,128)S(1)} %add_add_fusion.2), channel_id=1, source_target_pairs={{0,2},{2,4},{4,6},{6,0},{1,3},{3,5},{5,7},{7,1},{8,10},{10,12},{12... | collective-permute-start | bytes 135176 | tf_op jit(solution)/shard_map/ppermute | solution.py:21
  75.8 3.2 %collective-permute-start.26 = (f32[88,128]{1,0:T(8,128)S(1)}, f32[88,128]{1,0:T(8,128)S(1)}, u32[]{:S(2)}, u32[]{:S(2)}) collective-permute-start(f32[88,128]{1,0:T(8,128)S(1)} %add_add_fusion.2), channel_id=1, source_target_pairs={{0,6},{2,0},{4,2},{6,4},{1,7},{3,1},{5,3},{7,5},{8,14},{10,8},{12,... | collective-permute-start | bytes 135176 | tf_op jit(solution)/shard_map/ppermute | solution.py:21
  79.0 6.9 %collective-permute-start.27 = (f32[88,128]{1,0:T(8,128)S(1)}, f32[88,128]{1,0:T(8,128)S(1)}, u32[]{:S(2)}, u32[]{:S(2)}) collective-permute-start(f32[88,128]{1,0:T(8,128)S(1)} %add_add_fusion.1), channel_id=1, source_target_pairs={{0,1},{1,0},{2,3},{3,2},{4,5},{5,4},{6,7},{7,6},{8,9},{9,8},{10,11... | collective-permute-start | bytes 135176 | tf_op jit(solution)/shard_map/ppermute | solution.py:21
  85.9 5.1 %collective-permute-start.28 = (f32[88,128]{1,0:T(8,128)S(1)}, f32[88,128]{1,0:T(8,128)S(1)}, u32[]{:S(2)}, u32[]{:S(2)}) collective-permute-start(f32[88,128]{1,0:T(8,128)S(1)} %add.52), channel_id=1, source_target_pairs={{0,32},{16,48},{32,1},{48,17},{1,33},{17,49},{33,0},{49,16},{2,34}... | collective-permute-start | bytes 135176 | tf_op jit(solution)/shard_map/ppermute | solution.py:28
  87.3 4.6 %collective-permute-start.29 = (f32[88,128]{1,0:T(8,128)S(1)}, f32[88,128]{1,0:T(8,128)S(1)}, u32[]{:S(2)}, u32[]{:S(2)}) collective-permute-start(f32[88,128]{1,0:T(8,128)S(1)} %add.52), channel_id=1, source_target_pairs={{0,16},{16,32},{32,48},{48,1},{1,17},{17,33},{33,49},{49,0},{2,18}... | collective-permute-start | bytes 135176 | tf_op jit(solution)/shard_map/ppermute | solution.py:28
  89.2 2.9 %collective-permute-start.30 = (f32[88,128]{1,0:T(8,128)S(1)}, f32[88,128]{1,0:T(8,128)S(1)}, u32[]{:S(2)}, u32[]{:S(2)}) collective-permute-start(f32[88,128]{1,0:T(8,128)S(1)} %add.52), channel_id=1, source_target_pairs={{0,49},{16,0},{32,16},{48,32},{1,48},{17,1},{33,17},{49,33},{2,51}... | collective-permute-start | bytes 135176 | tf_op jit(solution)/shard_map/ppermute | solution.py:28
  92.1 7.4 %collective-permute-start.31 = (f32[88,128]{1,0:T(8,128)S(1)}, f32[88,128]{1,0:T(8,128)S(1)}, u32[]{:S(2)}, u32[]{:S(2)}) collective-permute-start(f32[88,128]{1,0:T(8,128)S(1)} %add_add_fusion), channel_id=1, source_target_pairs={{0,8},{8,0},{1,9},{9,1},{2,10},{10,2},{3,11},{11,3},{4,12},{12,4},... | collective-permute-start | bytes 135176 | tf_op jit(solution)/shard_map/ppermute | solution.py:21
  (5 other events, 67.7 us)

commit v6 on v5

--- a/solution.py
+++ b/solution.py
@@ -28,10 +28,11 @@
     return lax.ppermute(value, ("zl", "zh"), [(at(z), at((z + step) % n)) for z in range(n)])
 
 
-def plan_kernel(per_device, tile, count_ref, rows_ref, cols_ref, plan_ref):
+def plan_kernel(per_device, tile, count_ref, rows_ref, cols_ref, plan_ref, token_ref):
     y0, z0, core0, x0, zh0 = (lax.axis_index(axis) for axis in AXES)
     count = count_ref[0]
     slots = rows_ref.shape[1]
+    token_ref[0] = count
     slot = lax.broadcasted_iota(jnp.int32, (1, slots), 1)
     device, part = rows_ref[...] // per_device, rows_ref[...] % per_device
     row = (device // 2 - x0) % 4 * per_device + part
@@ -65,14 +66,14 @@
     vmem = pl.BlockSpec(memory_space=pltpu.VMEM)
     return pl.pallas_call(
         lambda *refs: plan_kernel(per_device, tile, *refs),
-        out_shape=jax.ShapeDtypeStruct((8, slots), jnp.int32),
+        out_shape=(jax.ShapeDtypeStruct((8, slots), jnp.int32), jax.ShapeDtypeStruct((1,), jnp.int32)),
         in_specs=[pl.BlockSpec(memory_space=pltpu.SMEM), vmem, vmem],
-        out_specs=vmem,
+        out_specs=(vmem, pl.BlockSpec(memory_space=pltpu.SMEM)),
         name="plan",
     )(count, tile_rows, tile_cols)
 
 
-def fetch_kernel(plan_ref, vals_ref, out_ref, token_ref, sems):
+def fetch_kernel(plan_ref, vals_ref, _, out_ref, token_ref, sems):
     count = plan_ref[3, 0] + plan_ref[7, 0]
 
     def each(act):
@@ -87,18 +88,18 @@
     token_ref[0] = count
 
 
-def fetch(plan, vals):
+def fetch(plan, vals, ready):
     smem = pl.BlockSpec(memory_space=pltpu.SMEM)
     return pl.pallas_call(
         fetch_kernel,
         out_shape=(jax.ShapeDtypeStruct(vals.shape, vals.dtype), jax.ShapeDtypeStruct((1,), jnp.int32)),
-        in_specs=[smem, pl.BlockSpec(memory_space=pltpu.HBM)],
+        in_specs=[smem, pl.BlockSpec(memory_space=pltpu.HBM), pl.BlockSpec(memory_space=pl.ANY)],
         out_specs=(pl.BlockSpec(memory_space=pltpu.VMEM), smem),
         scratch_shapes=[pltpu.SemaphoreType.DMA((vals.shape[0] // CHUNK,))],
         compiler_params=pltpu.CompilerParams(vmem_limit_bytes=12 * 2**20),
         cost_estimate=pl.CostEstimate(flops=0, bytes_accessed=16 * 2**20, transcendentals=0),
         name="fetch",
-    )(plan, vals)
+    )(plan, vals, ready)
 
 
 def sum_tiles(part, plan_ref, vals_ref, table_ref, own_ref, away_refs, acc, prods):
@@ -224,12 +225,14 @@
     return jnp.where(token[0] < 0, jnp.zeros_like(value), value)
 
 
-def gather_features(features, planned, fetched):
+def gather_features(features, lists, planned, vals):
     by_z = jnp.concatenate([features] + [shift(features, "zl", -k) for k in (1, 2, 3)], 0)
     opposite = after(shift(features, "y", 2), planned)
-    opposite = jnp.concatenate([opposite] + [shift(opposite, "zl", -k) for k in (1, 2, 3)], 0)
+    late = jnp.where(by_z[-1, 0] + by_z[features.shape[0], 0] > 1e30, jnp.zeros_like(opposite), opposite)
+    opposite = jnp.concatenate([opposite] + [shift(late, "zl", -k) for k in (1, 2, 3)], 0)
     mine = [by_z, shift(by_z, "y", -1), opposite, shift(by_z, "y", 1)]
-    return mine + [shift(piece, "core", 1) for piece in [after(by_z, fetched)] + mine[1:]]
+    vals, fetched = fetch(lists, vals, by_z)
+    return vals, mine + [shift(piece, "core", 1) for piece in [after(by_z, fetched)] + mine[1:]]
 
 
 def sum_everywhere(keep, give, core, classes):
@@ -251,12 +254,11 @@
     vals = pltpu.with_memory_space_constraint(tile_vals.reshape(slots, tile, tile), pltpu.HBM)
     out_rows = nodes * lax.axis_size("x")
     core = lax.axis_index("core").astype(jnp.int32)
-    lists = plan(
+    lists, planned = plan(
         tile_rows.reshape(1, slots), tile_cols.reshape(1, slots), tile_count.reshape(1), nodes // tile, tile
     )
 
-    vals, fetched = fetch(lists, vals)
-    pieces = gather_features(features, lists[3], fetched)
+    vals, pieces = gather_features(features, lists, planned, vals)
     table, own, *away = aggregate(functools.partial(far_kernel, len(pieces)), lists, vals, pieces, out_rows, True)
     give = own + sum(shift(away[k], "x", k + 1).astype(jnp.float32) for k in (1, 0, 2))
     own, *away = aggregate(near_kernel, lists, vals, [table], out_rows, False)

time: 100 us -> 98.4 us (0.984)
  waiting for transfers between devices: 25.2 us -> 19.3 us
  starting transfers between devices: 59.2 us -> 60.5 us
  between operations: 2.69 us -> 3.96 us
    ppermute x29, waiting for transfers between devices: 23.2 us -> 16.2 us  [shift(): return lax.ppermute(value, axes, [(i, (i + step) % n) for i in range(n)])]
    ppermute x29, starting transfers between devices: 55.1 us -> 57.7 us  [shift(): return lax.ppermute(value, axes, [(i, (i + step) % n) for i in range(n)])]
    ppermute x3, starting transfers between devices: 4.12 us -> 2.83 us  [shift_z(): lax.ppermute(value, ('zl', 'zh'), [(at(z), at((z + step) % n)) for z in r...]
    ppermute x3, waiting for transfers between devices: 2.04 us -> 3.08 us  [shift_z(): lax.ppermute(value, ('zl', 'zh'), [(at(z), at((z + step) % n)) for z in r...]
  transfers between devices with their start and end apart: 32 -> 32, of which waited for: 15 -> 13; matrix products, arithmetic and copies ran while one was open for 1% -> 2% of each run, Pallas kernels for 7% -> 7%
where the time goes in v6:
time: 98.4 us; the launch traced here: 97.6 us
  starting transfers between devices  60.5 us (61%)
  waiting for transfers between devices  19.3 us (20%)
  Pallas kernels  10.3 us (10%)
  between operations  3.96 us (4%)
  local copies, waits for them, and re-layouts  2.72 us (3%)
    ppermute x29, starting transfers between devices, shift(): return lax.ppermute(value, axes, [(i, (i + step) % n) for i in range(n)])  57.7 us
    ppermute x29, waiting for transfers between devices, shift(): return lax.ppermute(value, axes, [(i, (i + step) % n) for i in range(n)])  16.2 us
    pallas_call x2, Pallas kernels, aggregate(): pl.pallas_call(kernel, out_shape=out, in_specs=[pl.BlockSpec(memory_space...  4.13 us
    pallas_call x1, Pallas kernels, fetch(): pl.pallas_call(fetch_kernel, out_shape=(jax.ShapeDtypeStruct(vals.shape,...  3.43 us
    ppermute x3, waiting for transfers between devices, shift_z(): lax.ppermute(value, ('zl', 'zh'), [(at(z), at((z + step) % n)) for z in r...  3.08 us
    ppermute x3, starting transfers between devices, shift_z(): lax.ppermute(value, ('zl', 'zh'), [(at(z), at((z + step) % n)) for z in r...  2.83 us
  transfers between devices with their start and end apart: 32, of which 13 were waited for; matrix products, arithmetic and copies ran while one was open for 2% of the time, Pallas kernels for 7%

profile of v6, /device:TPU:1, one launch (start us, length us, event | category | flops | bytes accessed | tf_op | source)
XLA Modules:
  0.0 97.6 jit_solution(2253871736838249310)
XLA Ops:
  0.6 2.5 %collective-permute-start.2 = (bf16[512,128]{1,0:T(8,128)(2,1)}, bf16[512,128]{1,0:T(8,128)(2,1)S(1)}, u32[]{:S(2)}, u32[]{:S(2)}) collective-permute-start(bf16[512,128]{1,0:T(8,128)(2,1)} %param.7), channel_id=1, source_target_pairs={{0,16},{16,32},{32,48},{48,0},{1,17},{17,33},{33,49},{49,1},{2,18}... | collective-permute-start | bytes 393224 | tf_op jit(solution)/shard_map/ppermute | solution.py:21
  3.2 2.8 %collective-permute-start = (bf16[512,128]{1,0:T(8,128)(2,1)}, bf16[512,128]{1,0:T(8,128)(2,1)S(1)}, u32[]{:S(2)}, u32[]{:S(2)}) collective-permute-start(bf16[512,128]{1,0:T(8,128)(2,1)} %param.7), channel_id=1, source_target_pairs={{0,48},{16,0},{32,16},{48,32},{1,49},{17,1},{33,17},{49,33},{2,50}... | collective-permute-start | bytes 393224 | tf_op jit(solution)/shard_map/ppermute | solution.py:21
  6.0 2.9 %collective-permute-start.4 = (bf16[512,128]{1,0:T(8,128)(2,1)}, bf16[512,128]{1,0:T(8,128)(2,1)S(1)}, u32[]{:S(2)}, u32[]{:S(2)}) collective-permute-start(bf16[512,128]{1,0:T(8,128)(2,1)} %param.7), channel_id=1, source_target_pairs={{0,128},{64,192},{128,0},{192,64},{1,129},{65,193},{129,1},{193,65... | collective-permute-start | bytes 393224 | tf_op jit(solution)/shard_map/ppermute | solution.py:21
  9.7 1.6 %plan.1 = (s32[8,256]{1,0:T(8,128)}, s32[1]{0:T(128)}) custom-call(s32[1]{0:T(128)} %bitcast.13.refs_0_, s32[1,256]{1,0:T(1,128)} %bitcast.17, s32[1,256]{1,0:T(1,128)} %bitcast.18), custom_call_target="tpu_custom_call" | custom-call | tf_op jit(solution)/shard_map/plan/pallas_call | solution.py:67
  15.2 1.3 %collective-permute-start.5 = (bf16[512,128]{1,0:T(8,128)(2,1)S(1)}, bf16[512,128]{1,0:T(8,128)(2,1)S(1)}, u32[]{:S(2)}, u32[]{:S(2)}) collective-permute-start(bf16[512,128]{1,0:T(8,128)(2,1)S(1)} %get-tuple-element.34), channel_id=1, source_target_pairs={{0,48},{16,0},{32,16},{48,32},{1,49},{17,1},{33,17},{49,33},{2,50}... | collective-permute-start | bytes 393224 | tf_op jit(solution)/shard_map/ppermute | solution.py:21
  16.5 1.5 %collective-permute-start.6 = (bf16[512,128]{1,0:T(8,128)(2,1)S(1)}, bf16[512,128]{1,0:T(8,128)(2,1)S(1)}, u32[]{:S(2)}, u32[]{:S(2)}) collective-permute-start(bf16[512,128]{1,0:T(8,128)(2,1)S(1)} %get-tuple-element.34), channel_id=1, source_target_pairs={{0,32},{16,48},{32,0},{48,16},{1,33},{17,49},{33,1},{49,17},{2,34}... | collective-permute-start | bytes 393224 | tf_op jit(solution)/shard_map/ppermute | solution.py:21
  19.0 2.3 %collective-permute-start.3 = (bf16[2048,128]{1,0:T(8,128)(2,1)S(1)}, bf16[2048,128]{1,0:T(8,128)(2,1)S(1)}, u32[]{:S(2)}, u32[]{:S(2)}) collective-permute-start(bf16[2048,128]{1,0:T(8,128)(2,1)S(1)} %constant_dynamic-update-slice_fusion._.refs_0_), channel_id=1, source_target_pairs={{0,192},{64,0},{128,64},{192,128},{1,193},{65,1},{129,65},{193,129... | collective-permute-start | bytes 1572872 | tf_op jit(solution)/shard_map/ppermute | solution.py:21
  22.0 3.4 %fetch.1 = (bf16[256,128,128]{2,1,0:T(8,128)(2,1)S(1)}, s32[1]{0:T(128)}) custom-call(s32[8,256]{1,0:T(8,128)S(1)} %copy-done, bf16[256,128,128]{2,1,0:T(8,128)(2,1)} %bitcast.16, bf16[2048,128]{1,0:T(8,128)(2,1)S(1)} %constant_dynamic-update-slice_fusion._.refs_0_), custom_call_target="tpu_custom_call" | custom-call | bytes 16777216 | tf_op jit(solution)/shard_map/fetch/pallas_call | solution.py:93
  26.2 2.6 %collective-permute-start.9 = (bf16[2048,128]{1,0:T(8,128)(2,1)S(1)}, bf16[2048,128]{1,0:T(8,128)(2,1)S(1)}, u32[]{:S(2)}, u32[]{:S(2)}) collective-permute-start(bf16[2048,128]{1,0:T(8,128)(2,1)S(1)} %broadcast_select_fusion), channel_id=1, source_target_pairs={{0,8},{8,0},{1,9},{9,1},{2,10},{10,2},{3,11},{11,3},{4,12},{12,4},... | collective-permute-start | bytes 1572872 | tf_op jit(solution)/shard_map/ppermute | solution.py:21
  28.8 2.2 %collective-permute-start.11 = (bf16[2048,128]{1,0:T(8,128)(2,1)S(1)}, bf16[2048,128]{1,0:T(8,128)(2,1)S(1)}, u32[]{:S(2)}, u32[]{:S(2)}) collective-permute-start(bf16[2048,128]{1,0:T(8,128)(2,1)S(1)} %pad_maximum_fusion.refs_2_), channel_id=1, source_target_pairs={{0,8},{8,0},{1,9},{9,1},{2,10},{10,2},{3,11},{11,3},{4,12},{12,4},... | collective-permute-start | bytes 1572872 | tf_op jit(solution)/shard_map/ppermute | solution.py:21
  30.9 2.5 %collective-permute-start.10 = (bf16[2048,128]{1,0:T(8,128)(2,1)S(1)}, bf16[2048,128]{1,0:T(8,128)(2,1)S(1)}, u32[]{:S(2)}, u32[]{:S(2)}) collective-permute-start(bf16[2048,128]{1,0:T(8,128)(2,1)S(1)} %collective-permute-done.3.refs_1_), channel_id=1, source_target_pairs={{0,8},{8,0},{1,9},{9,1},{2,10},{10,2},{3,11},{11,3},{4,12},{12,4},... | collective-permute-start | bytes 1572872 | tf_op jit(solution)/shard_map/ppermute | solution.py:21
  33.5 3.4 %collective-permute-start.12 = (bf16[2048,128]{1,0:T(8,128)(2,1)S(1)}, bf16[2048,128]{1,0:T(8,128)(2,1)S(1)}, u32[]{:S(2)}, u32[]{:S(2)}) collective-permute-start(bf16[2048,128]{1,0:T(8,128)(2,1)S(1)} %collective-permute-done.8.refs_3_), channel_id=1, source_target_pairs={{0,8},{8,0},{1,9},{9,1},{2,10},{10,2},{3,11},{11,3},{4,12},{12,4},... | collective-permute-start | bytes 1572872 | tf_op jit(solution)/shard_map/ppermute | solution.py:21
  36.9 1.5 %collective-permute-done.12.refs_7_ = bf16[2048,128]{1,0:T(8,128)(2,1)S(1)} collective-permute-done((bf16[2048,128]{1,0:T(8,128)(2,1)S(1)}, bf16[2048,128]{1,0:T(8,128)(2,1)S(1)}, u32[]{:S(2)}, u32[]{:S(2)}) %collective-permute-start.12) | collective-permute-done | bytes 524320 | tf_op jit(solution)/shard_map/ppermute | solution.py:21
  38.4 2.2 %far_rows.1 = (bf16[16384,128]{1,0:T(8,128)(2,1)S(1)}, f32[512,128]{1,0:T(8,128)S(1)}, bf16[512,128]{1,0:T(8,128)(2,1)S(1)}, bf16[512,128]{1,0:T(8,128)(2,1)S(1)}, bf16[512,128]{1,0:T(8,128)(2,1)S(1)}) custom-call(s32[8,256]{1,0:T(8,128)S(1)} %copy-done, bf16[256,128,128]{2,1,0:T(8,128)(2,1)S(1)} %get-tuple-element.19.vals_ref, ...), custom_call_target="tpu_custom_call" | custom-call | flops 536870912 | bytes 8388608 | tf_op jit(solution)/shard_map/far_rows/pallas_call | solution.py:165
  40.6 2.8 %collective-permute-start.13 = (bf16[512,128]{1,0:T(8,128)(2,1)S(1)}, bf16[512,128]{1,0:T(8,128)(2,1)S(1)}, u32[]{:S(2)}, u32[]{:S(2)}) collective-permute-start(bf16[512,128]{1,0:T(8,128)(2,1)S(1)} %get-tuple-element.25), channel_id=1, source_target_pairs={{0,4},{2,6},{4,0},{6,2},{1,5},{3,7},{5,1},{7,3},{8,12},{10,14},{12... | collective-permute-start | bytes 393224 | tf_op jit(solution)/shard_map/ppermute | solution.py:21
  43.4 2.7 %collective-permute-start.15 = (bf16[512,128]{1,0:T(8,128)(2,1)S(1)}, bf16[512,128]{1,0:T(8,128)(2,1)S(1)}, u32[]{:S(2)}, u32[]{:S(2)}) collective-permute-start(bf16[512,128]{1,0:T(8,128)(2,1)S(1)} %get-tuple-element.27), channel_id=1, source_target_pairs={{0,6},{2,0},{4,2},{6,4},{1,7},{3,1},{5,3},{7,5},{8,14},{10,8},{12,... | collective-permute-start | bytes 393224 | tf_op jit(solution)/shard_map/ppermute | solution.py:21
  46.1 2.0 %near_rows.1 = (f32[512,128]{1,0:T(8,128)S(1)}, bf16[512,128]{1,0:T(8,128)(2,1)S(1)}, bf16[512,128]{1,0:T(8,128)(2,1)S(1)}, bf16[512,128]{1,0:T(8,128)(2,1)S(1)}) custom-call(s32[8,256]{1,0:T(8,128)S(1)} %copy-done, bf16[256,128,128]{2,1,0:T(8,128)(2,1)S(1)} %get-tuple-element.19.vals_ref, bf16[16384,128]{1,0:T(8,128)(2,1)S(1)} %get-tuple-element.22.table_ref), custom_call_target="tpu_custom_call" | custom-call | flops 536870912 | bytes 8388608 | tf_op jit(solution)/shard_map/near_rows/pallas_call | solution.py:165
  48.3 2.7 %collective-permute-start.19 = (bf16[512,128]{1,0:T(8,128)(2,1)S(1)}, bf16[512,128]{1,0:T(8,128)(2,1)S(1)}, u32[]{:S(2)}, u32[]{:S(2)}) collective-permute-start(bf16[512,128]{1,0:T(8,128)(2,1)S(1)} %get-tuple-element.30), channel_id=1, source_target_pairs={{0,6},{2,0},{4,2},{6,4},{1,7},{3,1},{5,3},{7,5},{8,14},{10,8},{12,... | collective-permute-start | bytes 393224 | tf_op jit(solution)/shard_map/ppermute | solution.py:21
  51.0 4.7 %collective-permute-start.16 = (bf16[512,128]{1,0:T(8,128)(2,1)S(1)}, bf16[512,128]{1,0:T(8,128)(2,1)S(1)}, u32[]{:S(2)}, u32[]{:S(2)}) collective-permute-start(bf16[512,128]{1,0:T(8,128)(2,1)S(1)} %add_convert_fusion), channel_id=1, source_target_pairs={{0,1},{1,0},{2,3},{3,2},{4,5},{5,4},{6,7},{7,6},{8,9},{9,8},{10,11... | collective-permute-start | bytes 393224 | tf_op jit(solution)/shard_map/ppermute | solution.py:21
  55.7 1.8 %collective-permute-done.18.refs_4_ = bf16[512,128]{1,0:T(8,128)(2,1)S(1)} collective-permute-done((bf16[512,128]{1,0:T(8,128)(2,1)S(1)}, bf16[512,128]{1,0:T(8,128)(2,1)S(1)}, u32[]{:S(2)}, u32[]{:S(2)}) %collective-permute-start.18) | collective-permute-done | bytes 131104 | tf_op jit(solution)/shard_map/ppermute | solution.py:21
  57.5 3.1 %collective-permute-done.16.refs_2_ = bf16[512,128]{1,0:T(8,128)(2,1)S(1)} collective-permute-done((bf16[512,128]{1,0:T(8,128)(2,1)S(1)}, bf16[512,128]{1,0:T(8,128)(2,1)S(1)}, u32[]{:S(2)}, u32[]{:S(2)}) %collective-permute-start.16) | collective-permute-done | bytes 131104 | tf_op jit(solution)/shard_map/ppermute | solution.py:21
  61.7 2.7 %collective-permute-start.20 = (f32[88,128]{1,0:T(8,128)S(1)}, f32[88,128]{1,0:T(8,128)S(1)}, u32[]{:S(2)}, u32[]{:S(2)}) collective-permute-start(f32[88,128]{1,0:T(8,128)S(1)} %get-tuple-element.33), channel_id=1, source_target_pairs={{0,8},{8,0},{1,9},{9,1},{2,10},{10,2},{3,11},{11,3},{4,12},{12,4},... | collective-permute-start | bytes 135176 | tf_op jit(solution)/shard_map/ppermute | solution.py:21
  65.9 2.2 %collective-permute-start.23 = (f32[88,128]{1,0:T(8,128)S(1)}, f32[88,128]{1,0:T(8,128)S(1)}, u32[]{:S(2)}, u32[]{:S(2)}) collective-permute-start(f32[88,128]{1,0:T(8,128)S(1)} %add.50), channel_id=1, source_target_pairs={{0,192},{64,0},{128,64},{192,128},{1,193},{65,1},{129,65},{193,129... | collective-permute-start | bytes 135176 | tf_op jit(solution)/shard_map/ppermute | solution.py:21
  68.1 1.7 %collective-permute-done.21 = f32[88,128]{1,0:T(8,128)S(1)} collective-permute-done((f32[88,128]{1,0:T(8,128)S(1)}, f32[88,128]{1,0:T(8,128)S(1)}, u32[]{:S(2)}, u32[]{:S(2)}) %collective-permute-start.21) | collective-permute-done | bytes 45088 | tf_op jit(solution)/shard_map/ppermute | solution.py:21
  70.5 1.7 %collective-permute-start.24 = (f32[88,128]{1,0:T(8,128)S(1)}, f32[88,128]{1,0:T(8,128)S(1)}, u32[]{:S(2)}, u32[]{:S(2)}) collective-permute-start(f32[88,128]{1,0:T(8,128)S(1)} %add_add_fusion.2), channel_id=1, source_target_pairs={{0,4},{2,6},{4,0},{6,2},{1,5},{3,7},{5,1},{7,3},{8,12},{10,14},{12... | collective-permute-start | bytes 135176 | tf_op jit(solution)/shard_map/ppermute | solution.py:21
  72.1 2.2 %collective-permute-start.25 = (f32[88,128]{1,0:T(8,128)S(1)}, f32[88,128]{1,0:T(8,128)S(1)}, u32[]{:S(2)}, u32[]{:S(2)}) collective-permute-start(f32[88,128]{1,0:T(8,128)S(1)} %add_add_fusion.2), channel_id=1, source_target_pairs={{0,2},{2,4},{4,6},{6,0},{1,3},{3,5},{5,7},{7,1},{8,10},{10,12},{12... | collective-permute-start | bytes 135176 | tf_op jit(solution)/shard_map/ppermute | solution.py:21
  74.9 1.6 %collective-permute-done.25 = f32[88,128]{1,0:T(8,128)S(1)} collective-permute-done((f32[88,128]{1,0:T(8,128)S(1)}, f32[88,128]{1,0:T(8,128)S(1)}, u32[]{:S(2)}, u32[]{:S(2)}) %collective-permute-start.25) | collective-permute-done | bytes 45088 | tf_op jit(solution)/shard_map/ppermute | solution.py:21
  77.5 3.9 %collective-permute-start.27 = (f32[88,128]{1,0:T(8,128)S(1)}, f32[88,128]{1,0:T(8,128)S(1)}, u32[]{:S(2)}, u32[]{:S(2)}) collective-permute-start(f32[88,128]{1,0:T(8,128)S(1)} %add_add_fusion.1), channel_id=1, source_target_pairs={{0,1},{1,0},{2,3},{3,2},{4,5},{5,4},{6,7},{7,6},{8,9},{9,8},{10,11... | collective-permute-start | bytes 135176 | tf_op jit(solution)/shard_map/ppermute | solution.py:21
  81.5 3.0 %collective-permute-done.27 = f32[88,128]{1,0:T(8,128)S(1)} collective-permute-done((f32[88,128]{1,0:T(8,128)S(1)}, f32[88,128]{1,0:T(8,128)S(1)}, u32[]{:S(2)}, u32[]{:S(2)}) %collective-permute-start.27) | collective-permute-done | bytes 45088 | tf_op jit(solution)/shard_map/ppermute | solution.py:21
  84.5 2.1 %collective-permute-start.29 = (f32[88,128]{1,0:T(8,128)S(1)}, f32[88,128]{1,0:T(8,128)S(1)}, u32[]{:S(2)}, u32[]{:S(2)}) collective-permute-start(f32[88,128]{1,0:T(8,128)S(1)} %add.57), channel_id=1, source_target_pairs={{0,16},{16,32},{32,48},{48,1},{1,17},{17,33},{33,49},{49,0},{2,18}... | collective-permute-start | bytes 135176 | tf_op jit(solution)/shard_map/ppermute | solution.py:28
  87.3 2.7 %collective-permute-done.28 = f32[88,128]{1,0:T(8,128)S(1)} collective-permute-done((f32[88,128]{1,0:T(8,128)S(1)}, f32[88,128]{1,0:T(8,128)S(1)}, u32[]{:S(2)}, u32[]{:S(2)}) %collective-permute-start.28) | collective-permute-done | bytes 45088 | tf_op jit(solution)/shard_map/ppermute | solution.py:28
  90.4 5.7 %collective-permute-start.31 = (f32[88,128]{1,0:T(8,128)S(1)}, f32[88,128]{1,0:T(8,128)S(1)}, u32[]{:S(2)}, u32[]{:S(2)}) collective-permute-start(f32[88,128]{1,0:T(8,128)S(1)} %add_add_fusion), channel_id=1, source_target_pairs={{0,8},{8,0},{1,9},{9,1},{2,10},{10,2},{3,11},{11,3},{4,12},{12,4},... | collective-permute-start | bytes 135176 | tf_op jit(solution)/shard_map/ppermute | solution.py:21
  (60 shorter events, 11.5 us)
Async XLA Ops:
  0.6 12.3 %collective-permute-start.2 = (bf16[512,128]{1,0:T(8,128)(2,1)}, bf16[512,128]{1,0:T(8,128)(2,1)S(1)}, u32[]{:S(2)}, u32[]{:S(2)}) collective-permute-start(bf16[512,128]{1,0:T(8,128)(2,1)} %param.7), channel_id=1, source_target_pairs={{0,16},{16,32},{32,48},{48,0},{1,17},{17,33},{33,49},{49,1},{2,18}... | collective-permute-start | bytes 393224 | tf_op jit(solution)/shard_map/ppermute | solution.py:21
  3.2 10.2 %collective-permute-start = (bf16[512,128]{1,0:T(8,128)(2,1)}, bf16[512,128]{1,0:T(8,128)(2,1)S(1)}, u32[]{:S(2)}, u32[]{:S(2)}) collective-permute-start(bf16[512,128]{1,0:T(8,128)(2,1)} %param.7), channel_id=1, source_target_pairs={{0,48},{16,0},{32,16},{48,32},{1,49},{17,1},{33,17},{49,33},{2,50}... | collective-permute-start | bytes 393224 | tf_op jit(solution)/shard_map/ppermute | solution.py:21
  6.0 9.2 %collective-permute-start.4 = (bf16[512,128]{1,0:T(8,128)(2,1)}, bf16[512,128]{1,0:T(8,128)(2,1)S(1)}, u32[]{:S(2)}, u32[]{:S(2)}) collective-permute-start(bf16[512,128]{1,0:T(8,128)(2,1)} %param.7), channel_id=1, source_target_pairs={{0,128},{64,192},{128,0},{192,64},{1,129},{65,193},{129,1},{193,65... | collective-permute-start | bytes 393224 | tf_op jit(solution)/shard_map/ppermute | solution.py:21
  8.9 10.1 %collective-permute-start.1 = (bf16[512,128]{1,0:T(8,128)(2,1)}, bf16[512,128]{1,0:T(8,128)(2,1)S(1)}, u32[]{:S(2)}, u32[]{:S(2)}) collective-permute-start(bf16[512,128]{1,0:T(8,128)(2,1)} %param.7), channel_id=1, source_target_pairs={{0,32},{16,48},{32,0},{48,16},{1,33},{17,49},{33,1},{49,17},{2,34}... | collective-permute-start | bytes 393224 | tf_op jit(solution)/shard_map/ppermute | solution.py:21
  15.2 11.0 %collective-permute-start.5 = (bf16[512,128]{1,0:T(8,128)(2,1)S(1)}, bf16[512,128]{1,0:T(8,128)(2,1)S(1)}, u32[]{:S(2)}, u32[]{:S(2)}) collective-permute-start(bf16[512,128]{1,0:T(8,128)(2,1)S(1)} %get-tuple-element.34), channel_id=1, source_target_pairs={{0,48},{16,0},{32,16},{48,32},{1,49},{17,1},{33,17},{49,33},{2,50}... | collective-permute-start | bytes 393224 | tf_op jit(solution)/shard_map/ppermute | solution.py:21
  16.5 12.3 %collective-permute-start.6 = (bf16[512,128]{1,0:T(8,128)(2,1)S(1)}, bf16[512,128]{1,0:T(8,128)(2,1)S(1)}, u32[]{:S(2)}, u32[]{:S(2)}) collective-permute-start(bf16[512,128]{1,0:T(8,128)(2,1)S(1)} %get-tuple-element.34), channel_id=1, source_target_pairs={{0,32},{16,48},{32,0},{48,16},{1,33},{17,49},{33,1},{49,17},{2,34}... | collective-permute-start | bytes 393224 | tf_op jit(solution)/shard_map/ppermute | solution.py:21
  17.9 10.8 %collective-permute-start.7 = (bf16[512,128]{1,0:T(8,128)(2,1)S(1)}, bf16[512,128]{1,0:T(8,128)(2,1)S(1)}, u32[]{:S(2)}, u32[]{:S(2)}) collective-permute-start(bf16[512,128]{1,0:T(8,128)(2,1)S(1)} %get-tuple-element.34), channel_id=1, source_target_pairs={{0,16},{16,32},{32,48},{48,0},{1,17},{17,33},{33,49},{49,1},{2,18}... | collective-permute-start | bytes 393224 | tf_op jit(solution)/shard_map/ppermute | solution.py:21
  19.0 11.9 %collective-permute-start.3 = (bf16[2048,128]{1,0:T(8,128)(2,1)S(1)}, bf16[2048,128]{1,0:T(8,128)(2,1)S(1)}, u32[]{:S(2)}, u32[]{:S(2)}) collective-permute-start(bf16[2048,128]{1,0:T(8,128)(2,1)S(1)} %constant_dynamic-update-slice_fusion._.refs_0_), channel_id=1, source_target_pairs={{0,192},{64,0},{128,64},{192,128},{1,193},{65,1},{129,65},{193,129... | collective-permute-start | bytes 1572872 | tf_op jit(solution)/shard_map/ppermute | solution.py:21
  21.3 12.1 %collective-permute-start.8 = (bf16[2048,128]{1,0:T(8,128)(2,1)S(1)}, bf16[2048,128]{1,0:T(8,128)(2,1)S(1)}, u32[]{:S(2)}, u32[]{:S(2)}) collective-permute-start(bf16[2048,128]{1,0:T(8,128)(2,1)S(1)} %constant_dynamic-update-slice_fusion._.refs_0_), channel_id=1, source_target_pairs={{0,64},{64,128},{128,192},{192,0},{1,65},{65,129},{129,193},{193,1... | collective-permute-start | bytes 1572872 | tf_op jit(solution)/shard_map/ppermute | solution.py:21
  26.2 10.7 %collective-permute-start.9 = (bf16[2048,128]{1,0:T(8,128)(2,1)S(1)}, bf16[2048,128]{1,0:T(8,128)(2,1)S(1)}, u32[]{:S(2)}, u32[]{:S(2)}) collective-permute-start(bf16[2048,128]{1,0:T(8,128)(2,1)S(1)} %broadcast_select_fusion), channel_id=1, source_target_pairs={{0,8},{8,0},{1,9},{9,1},{2,10},{10,2},{3,11},{11,3},{4,12},{12,4},... | collective-permute-start | bytes 1572872 | tf_op jit(solution)/shard_map/ppermute | solution.py:21
  28.8 8.1 %collective-permute-start.11 = (bf16[2048,128]{1,0:T(8,128)(2,1)S(1)}, bf16[2048,128]{1,0:T(8,128)(2,1)S(1)}, u32[]{:S(2)}, u32[]{:S(2)}) collective-permute-start(bf16[2048,128]{1,0:T(8,128)(2,1)S(1)} %pad_maximum_fusion.refs_2_), channel_id=1, source_target_pairs={{0,8},{8,0},{1,9},{9,1},{2,10},{10,2},{3,11},{11,3},{4,12},{12,4},... | collective-permute-start | bytes 1572872 | tf_op jit(solution)/shard_map/ppermute | solution.py:21
  30.9 6.0 %collective-permute-start.10 = (bf16[2048,128]{1,0:T(8,128)(2,1)S(1)}, bf16[2048,128]{1,0:T(8,128)(2,1)S(1)}, u32[]{:S(2)}, u32[]{:S(2)}) collective-permute-start(bf16[2048,128]{1,0:T(8,128)(2,1)S(1)} %collective-permute-done.3.refs_1_), channel_id=1, source_target_pairs={{0,8},{8,0},{1,9},{9,1},{2,10},{10,2},{3,11},{11,3},{4,12},{12,4},... | collective-permute-start | bytes 1572872 | tf_op jit(solution)/shard_map/ppermute | solution.py:21
  33.5 4.9 %collective-permute-start.12 = (bf16[2048,128]{1,0:T(8,128)(2,1)S(1)}, bf16[2048,128]{1,0:T(8,128)(2,1)S(1)}, u32[]{:S(2)}, u32[]{:S(2)}) collective-permute-start(bf16[2048,128]{1,0:T(8,128)(2,1)S(1)} %collective-permute-done.8.refs_3_), channel_id=1, source_target_pairs={{0,8},{8,0},{1,9},{9,1},{2,10},{10,2},{3,11},{11,3},{4,12},{12,4},... | collective-permute-start | bytes 1572872 | tf_op jit(solution)/shard_map/ppermute | solution.py:21
  40.6 7.7 %collective-permute-start.13 = (bf16[512,128]{1,0:T(8,128)(2,1)S(1)}, bf16[512,128]{1,0:T(8,128)(2,1)S(1)}, u32[]{:S(2)}, u32[]{:S(2)}) collective-permute-start(bf16[512,128]{1,0:T(8,128)(2,1)S(1)} %get-tuple-element.25), channel_id=1, source_target_pairs={{0,4},{2,6},{4,0},{6,2},{1,5},{3,7},{5,1},{7,3},{8,12},{10,14},{12... | collective-permute-start | bytes 393224 | tf_op jit(solution)/shard_map/ppermute | solution.py:21
  43.4 7.5 %collective-permute-start.14 = (bf16[512,128]{1,0:T(8,128)(2,1)S(1)}, bf16[512,128]{1,0:T(8,128)(2,1)S(1)}, u32[]{:S(2)}, u32[]{:S(2)}) collective-permute-start(bf16[512,128]{1,0:T(8,128)(2,1)S(1)} %get-tuple-element.26), channel_id=1, source_target_pairs={{0,2},{2,4},{4,6},{6,0},{1,3},{3,5},{5,7},{7,1},{8,10},{10,12},{12... | collective-permute-start | bytes 393224 | tf_op jit(solution)/shard_map/ppermute | solution.py:21
  43.4 7.5 %collective-permute-start.15 = (bf16[512,128]{1,0:T(8,128)(2,1)S(1)}, bf16[512,128]{1,0:T(8,128)(2,1)S(1)}, u32[]{:S(2)}, u32[]{:S(2)}) collective-permute-start(bf16[512,128]{1,0:T(8,128)(2,1)S(1)} %get-tuple-element.27), channel_id=1, source_target_pairs={{0,6},{2,0},{4,2},{6,4},{1,7},{3,1},{5,3},{7,5},{8,14},{10,8},{12,... | collective-permute-start | bytes 393224 | tf_op jit(solution)/shard_map/ppermute | solution.py:21
  48.1 7.6 %collective-permute-start.17 = (bf16[512,128]{1,0:T(8,128)(2,1)S(1)}, bf16[512,128]{1,0:T(8,128)(2,1)S(1)}, u32[]{:S(2)}, u32[]{:S(2)}) collective-permute-start(bf16[512,128]{1,0:T(8,128)(2,1)S(1)} %get-tuple-element.28), channel_id=1, source_target_pairs={{0,4},{2,6},{4,0},{6,2},{1,5},{3,7},{5,1},{7,3},{8,12},{10,14},{12... | collective-permute-start | bytes 393224 | tf_op jit(solution)/shard_map/ppermute | solution.py:21
  48.2 9.3 %collective-permute-start.18 = (bf16[512,128]{1,0:T(8,128)(2,1)S(1)}, bf16[512,128]{1,0:T(8,128)(2,1)S(1)}, u32[]{:S(2)}, u32[]{:S(2)}) collective-permute-start(bf16[512,128]{1,0:T(8,128)(2,1)S(1)} %get-tuple-element.29), channel_id=1, source_target_pairs={{0,2},{2,4},{4,6},{6,0},{1,3},{3,5},{5,7},{7,1},{8,10},{10,12},{12... | collective-permute-start | bytes 393224 | tf_op jit(solution)/shard_map/ppermute | solution.py:21
  48.3 9.2 %collective-permute-start.19 = (bf16[512,128]{1,0:T(8,128)(2,1)S(1)}, bf16[512,128]{1,0:T(8,128)(2,1)S(1)}, u32[]{:S(2)}, u32[]{:S(2)}) collective-permute-start(bf16[512,128]{1,0:T(8,128)(2,1)S(1)} %get-tuple-element.30), channel_id=1, source_target_pairs={{0,6},{2,0},{4,2},{6,4},{1,7},{3,1},{5,3},{7,5},{8,14},{10,8},{12,... | collective-permute-start | bytes 393224 | tf_op jit(solution)/shard_map/ppermute | solution.py:21
  51.0 9.6 %collective-permute-start.16 = (bf16[512,128]{1,0:T(8,128)(2,1)S(1)}, bf16[512,128]{1,0:T(8,128)(2,1)S(1)}, u32[]{:S(2)}, u32[]{:S(2)}) collective-permute-start(bf16[512,128]{1,0:T(8,128)(2,1)S(1)} %add_convert_fusion), channel_id=1, source_target_pairs={{0,1},{1,0},{2,3},{3,2},{4,5},{5,4},{6,7},{7,6},{8,9},{9,8},{10,11... | collective-permute-start | bytes 393224 | tf_op jit(solution)/shard_map/ppermute | solution.py:21
  61.7 3.6 %collective-permute-start.20 = (f32[88,128]{1,0:T(8,128)S(1)}, f32[88,128]{1,0:T(8,128)S(1)}, u32[]{:S(2)}, u32[]{:S(2)}) collective-permute-start(f32[88,128]{1,0:T(8,128)S(1)} %get-tuple-element.33), channel_id=1, source_target_pairs={{0,8},{8,0},{1,9},{9,1},{2,10},{10,2},{3,11},{11,3},{4,12},{12,4},... | collective-permute-start | bytes 135176 | tf_op jit(solution)/shard_map/ppermute | solution.py:21
  65.4 4.5 %collective-permute-start.21 = (f32[88,128]{1,0:T(8,128)S(1)}, f32[88,128]{1,0:T(8,128)S(1)}, u32[]{:S(2)}, u32[]{:S(2)}) collective-permute-start(f32[88,128]{1,0:T(8,128)S(1)} %add.50), channel_id=1, source_target_pairs={{0,128},{64,192},{128,0},{192,64},{1,129},{65,193},{129,1},{193,65... | collective-permute-start | bytes 135176 | tf_op jit(solution)/shard_map/ppermute | solution.py:21
  65.4 5.0 %collective-permute-start.22 = (f32[88,128]{1,0:T(8,128)S(1)}, f32[88,128]{1,0:T(8,128)S(1)}, u32[]{:S(2)}, u32[]{:S(2)}) collective-permute-start(f32[88,128]{1,0:T(8,128)S(1)} %add.50), channel_id=1, source_target_pairs={{0,64},{64,128},{128,192},{192,0},{1,65},{65,129},{129,193},{193,1... | collective-permute-start | bytes 135176 | tf_op jit(solution)/shard_map/ppermute | solution.py:21
  65.9 4.5 %collective-permute-start.23 = (f32[88,128]{1,0:T(8,128)S(1)}, f32[88,128]{1,0:T(8,128)S(1)}, u32[]{:S(2)}, u32[]{:S(2)}) collective-permute-start(f32[88,128]{1,0:T(8,128)S(1)} %add.50), channel_id=1, source_target_pairs={{0,192},{64,0},{128,64},{192,128},{1,193},{65,1},{129,65},{193,129... | collective-permute-start | bytes 135176 | tf_op jit(solution)/shard_map/ppermute | solution.py:21
  70.5 4.5 %collective-permute-start.24 = (f32[88,128]{1,0:T(8,128)S(1)}, f32[88,128]{1,0:T(8,128)S(1)}, u32[]{:S(2)}, u32[]{:S(2)}) collective-permute-start(f32[88,128]{1,0:T(8,128)S(1)} %add_add_fusion.2), channel_id=1, source_target_pairs={{0,4},{2,6},{4,0},{6,2},{1,5},{3,7},{5,1},{7,3},{8,12},{10,14},{12... | collective-permute-start | bytes 135176 | tf_op jit(solution)/shard_map/ppermute | solution.py:21
  72.1 4.4 %collective-permute-start.25 = (f32[88,128]{1,0:T(8,128)S(1)}, f32[88,128]{1,0:T(8,128)S(1)}, u32[]{:S(2)}, u32[]{:S(2)}) collective-permute-start(f32[88,128]{1,0:T(8,128)S(1)} %add_add_fusion.2), channel_id=1, source_target_pairs={{0,2},{2,4},{4,6},{6,0},{1,3},{3,5},{5,7},{7,1},{8,10},{10,12},{12... | collective-permute-start | bytes 135176 | tf_op jit(solution)/shard_map/ppermute | solution.py:21
  74.4 3.1 %collective-permute-start.26 = (f32[88,128]{1,0:T(8,128)S(1)}, f32[88,128]{1,0:T(8,128)S(1)}, u32[]{:S(2)}, u32[]{:S(2)}) collective-permute-start(f32[88,128]{1,0:T(8,128)S(1)} %add_add_fusion.2), channel_id=1, source_target_pairs={{0,6},{2,0},{4,2},{6,4},{1,7},{3,1},{5,3},{7,5},{8,14},{10,8},{12,... | collective-permute-start | bytes 135176 | tf_op jit(solution)/shard_map/ppermute | solution.py:21
  77.5 6.9 %collective-permute-start.27 = (f32[88,128]{1,0:T(8,128)S(1)}, f32[88,128]{1,0:T(8,128)S(1)}, u32[]{:S(2)}, u32[]{:S(2)}) collective-permute-start(f32[88,128]{1,0:T(8,128)S(1)} %add_add_fusion.1), channel_id=1, source_target_pairs={{0,1},{1,0},{2,3},{3,2},{4,5},{5,4},{6,7},{7,6},{8,9},{9,8},{10,11... | collective-permute-start | bytes 135176 | tf_op jit(solution)/shard_map/ppermute | solution.py:21
  84.4 5.6 %collective-permute-start.28 = (f32[88,128]{1,0:T(8,128)S(1)}, f32[88,128]{1,0:T(8,128)S(1)}, u32[]{:S(2)}, u32[]{:S(2)}) collective-permute-start(f32[88,128]{1,0:T(8,128)S(1)} %add.57), channel_id=1, source_target_pairs={{0,32},{16,48},{32,1},{48,17},{1,33},{17,49},{33,0},{49,16},{2,34}... | collective-permute-start | bytes 135176 | tf_op jit(solution)/shard_map/ppermute | solution.py:28
  84.5 5.5 %collective-permute-start.29 = (f32[88,128]{1,0:T(8,128)S(1)}, f32[88,128]{1,0:T(8,128)S(1)}, u32[]{:S(2)}, u32[]{:S(2)}) collective-permute-start(f32[88,128]{1,0:T(8,128)S(1)} %add.57), channel_id=1, source_target_pairs={{0,16},{16,32},{32,48},{48,1},{1,17},{17,33},{33,49},{49,0},{2,18}... | collective-permute-start | bytes 135176 | tf_op jit(solution)/shard_map/ppermute | solution.py:28
  86.6 3.7 %collective-permute-start.30 = (f32[88,128]{1,0:T(8,128)S(1)}, f32[88,128]{1,0:T(8,128)S(1)}, u32[]{:S(2)}, u32[]{:S(2)}) collective-permute-start(f32[88,128]{1,0:T(8,128)S(1)} %add.57), channel_id=1, source_target_pairs={{0,49},{16,0},{32,16},{48,32},{1,48},{17,1},{33,17},{49,33},{2,51}... | collective-permute-start | bytes 135176 | tf_op jit(solution)/shard_map/ppermute | solution.py:28
  90.4 6.6 %collective-permute-start.31 = (f32[88,128]{1,0:T(8,128)S(1)}, f32[88,128]{1,0:T(8,128)S(1)}, u32[]{:S(2)}, u32[]{:S(2)}) collective-permute-start(f32[88,128]{1,0:T(8,128)S(1)} %add_add_fusion), channel_id=1, source_target_pairs={{0,8},{8,0},{1,9},{9,1},{2,10},{10,2},{3,11},{11,3},{4,12},{12,4},... | collective-permute-start | bytes 135176 | tf_op jit(solution)/shard_map/ppermute | solution.py:21
  (3 other events, 40.8 us)

commit v7 on v6

--- a/solution.py
+++ b/solution.py
@@ -38,8 +38,9 @@
     row = (device // 2 - x0) % 4 * per_device + part
     far = (device % 2 - zh0) % 2 == 1
     device, part = cols_ref[...] // per_device, cols_ref[...] % per_device
-    place = (device % 2 - core0) % 2 * 4 + (device // 8 - y0) % 4
-    place = (place * 4 + (device // 2 % 4 - z0) % 4) * per_device + part
+    y, z = (device // 8 - y0) % 4, (device // 2 % 4 - z0) % 4
+    z = jnp.where((y == 2) & (z >= 2), 5 - z, z)
+    place = (((device % 2 - core0) % 2 * 4 + y) * 4 + z) * per_device + part
     used = slot < count
     before = lax.broadcasted_iota(jnp.int32, (slots, slots), 0) <= lax.broadcasted_iota(jnp.int32, (slots, slots), 1)
     before = before.astype(jnp.bfloat16)
@@ -229,7 +230,7 @@
     by_z = jnp.concatenate([features] + [shift(features, "zl", -k) for k in (1, 2, 3)], 0)
     opposite = after(shift(features, "y", 2), planned)
     late = jnp.where(by_z[-1, 0] + by_z[features.shape[0], 0] > 1e30, jnp.zeros_like(opposite), opposite)
-    opposite = jnp.concatenate([opposite] + [shift(late, "zl", -k) for k in (1, 2, 3)], 0)
+    opposite = jnp.concatenate([opposite] + [shift(late, "zl", -k) for k in (1, 3, 2)], 0)
     mine = [by_z, shift(by_z, "y", -1), opposite, shift(by_z, "y", 1)]
     vals, fetched = fetch(lists, vals, by_z)
     return vals, mine + [shift(piece, "core", 1) for piece in [after(by_z, fetched)] + mine[1:]]

time: 98.4 us -> 97.6 us (level)
  waiting for transfers between devices: 19.3 us -> 26.5 us
  starting transfers between devices: 60.5 us -> 53.5 us
    ppermute x29, waiting for transfers between devices: 16.2 us -> 23.8 us  [shift(): return lax.ppermute(value, axes, [(i, (i + step) % n) for i in range(n)])]
    ppermute x29, starting transfers between devices: 57.7 us -> 50.7 us  [shift(): return lax.ppermute(value, axes, [(i, (i + step) % n) for i in range(n)])]
where the time goes in v7:
time: 97.6 us
  starting transfers between devices  53.5 us (55%)
  waiting for transfers between devices  26.5 us (27%)
  Pallas kernels  9.98 us (10%)
  between operations  3.95 us (4%)
  local copies, waits for them, and re-layouts  2.72 us (3%)
    ppermute x29, starting transfers between devices, shift(): return lax.ppermute(value, axes, [(i, (i + step) % n) for i in range(n)])  50.7 us
    ppermute x29, waiting for transfers between devices, shift(): return lax.ppermute(value, axes, [(i, (i + step) % n) for i in range(n)])  23.8 us
    pallas_call x2, Pallas kernels, aggregate(): pl.pallas_call(kernel, out_shape=out, in_specs=[pl.BlockSpec(memory_space...  4.13 us
    pallas_call x1, Pallas kernels, fetch(): pl.pallas_call(fetch_kernel, out_shape=(jax.ShapeDtypeStruct(vals.shape,...  3.11 us
    ppermute x3, starting transfers between devices, shift_z(): lax.ppermute(value, ('zl', 'zh'), [(at(z), at((z + step) % n)) for z in r...  2.83 us
    ppermute x3, waiting for transfers between devices, shift_z(): lax.ppermute(value, ('zl', 'zh'), [(at(z), at((z + step) % n)) for z in r...  2.73 us
  transfers between devices with their start and end apart: 32, of which 13 were waited for; matrix products, arithmetic and copies ran while one was open for 2% of the time, Pallas kernels for 7%

profile of v7, /device:TPU:1, one launch (start us, length us, event | category | flops | bytes accessed | tf_op | source)
XLA Modules:
  0.0 97.6 jit_solution(4822990377395968985)
XLA Ops:
  0.6 2.5 %collective-permute-start.2 = (bf16[512,128]{1,0:T(8,128)(2,1)}, bf16[512,128]{1,0:T(8,128)(2,1)S(1)}, u32[]{:S(2)}, u32[]{:S(2)}) collective-permute-start(bf16[512,128]{1,0:T(8,128)(2,1)} %param.7), channel_id=1, source_target_pairs={{0,16},{16,32},{32,48},{48,0},{1,17},{17,33},{33,49},{49,1},{2,18}... | collective-permute-start | bytes 393224 | tf_op jit(solution)/shard_map/ppermute | solution.py:21
  3.2 2.8 %collective-permute-start = (bf16[512,128]{1,0:T(8,128)(2,1)}, bf16[512,128]{1,0:T(8,128)(2,1)S(1)}, u32[]{:S(2)}, u32[]{:S(2)}) collective-permute-start(bf16[512,128]{1,0:T(8,128)(2,1)} %param.7), channel_id=1, source_target_pairs={{0,48},{16,0},{32,16},{48,32},{1,49},{17,1},{33,17},{49,33},{2,50}... | collective-permute-start | bytes 393224 | tf_op jit(solution)/shard_map/ppermute | solution.py:21
  6.0 2.9 %collective-permute-start.4 = (bf16[512,128]{1,0:T(8,128)(2,1)}, bf16[512,128]{1,0:T(8,128)(2,1)S(1)}, u32[]{:S(2)}, u32[]{:S(2)}) collective-permute-start(bf16[512,128]{1,0:T(8,128)(2,1)} %param.7), channel_id=1, source_target_pairs={{0,128},{64,192},{128,0},{192,64},{1,129},{65,193},{129,1},{193,65... | collective-permute-start | bytes 393224 | tf_op jit(solution)/shard_map/ppermute | solution.py:21
  9.7 1.6 %plan.1 = (s32[8,256]{1,0:T(8,128)}, s32[1]{0:T(128)}) custom-call(s32[1]{0:T(128)} %bitcast.13.refs_0_, s32[1,256]{1,0:T(1,128)} %bitcast.17, s32[1,256]{1,0:T(1,128)} %bitcast.18), custom_call_target="tpu_custom_call" | custom-call | tf_op jit(solution)/shard_map/plan/pallas_call | solution.py:68
  15.2 1.3 %collective-permute-start.5 = (bf16[512,128]{1,0:T(8,128)(2,1)S(1)}, bf16[512,128]{1,0:T(8,128)(2,1)S(1)}, u32[]{:S(2)}, u32[]{:S(2)}) collective-permute-start(bf16[512,128]{1,0:T(8,128)(2,1)S(1)} %get-tuple-element.34), channel_id=1, source_target_pairs={{0,48},{16,0},{32,16},{48,32},{1,49},{17,1},{33,17},{49,33},{2,50}... | collective-permute-start | bytes 393224 | tf_op jit(solution)/shard_map/ppermute | solution.py:21
  16.9 2.1 %collective-permute-start.7 = (bf16[512,128]{1,0:T(8,128)(2,1)S(1)}, bf16[512,128]{1,0:T(8,128)(2,1)S(1)}, u32[]{:S(2)}, u32[]{:S(2)}) collective-permute-start(bf16[512,128]{1,0:T(8,128)(2,1)S(1)} %get-tuple-element.34), channel_id=1, source_target_pairs={{0,32},{16,48},{32,0},{48,16},{1,33},{17,49},{33,1},{49,17},{2,34}... | collective-permute-start | bytes 393224 | tf_op jit(solution)/shard_map/ppermute | solution.py:21
  19.0 2.3 %collective-permute-start.3 = (bf16[2048,128]{1,0:T(8,128)(2,1)S(1)}, bf16[2048,128]{1,0:T(8,128)(2,1)S(1)}, u32[]{:S(2)}, u32[]{:S(2)}) collective-permute-start(bf16[2048,128]{1,0:T(8,128)(2,1)S(1)} %constant_dynamic-update-slice_fusion._.refs_0_), channel_id=1, source_target_pairs={{0,192},{64,0},{128,64},{192,128},{1,193},{65,1},{129,65},{193,129... | collective-permute-start | bytes 1572872 | tf_op jit(solution)/shard_map/ppermute | solution.py:21
  22.0 3.1 %fetch.1 = (bf16[256,128,128]{2,1,0:T(8,128)(2,1)S(1)}, s32[1]{0:T(128)}) custom-call(s32[8,256]{1,0:T(8,128)S(1)} %copy-done, bf16[256,128,128]{2,1,0:T(8,128)(2,1)} %bitcast.16, bf16[2048,128]{1,0:T(8,128)(2,1)S(1)} %constant_dynamic-update-slice_fusion._.refs_0_), custom_call_target="tpu_custom_call" | custom-call | bytes 16777216 | tf_op jit(solution)/shard_map/fetch/pallas_call | solution.py:94
  25.9 3.5 %collective-permute-start.9 = (bf16[2048,128]{1,0:T(8,128)(2,1)S(1)}, bf16[2048,128]{1,0:T(8,128)(2,1)S(1)}, u32[]{:S(2)}, u32[]{:S(2)}) collective-permute-start(bf16[2048,128]{1,0:T(8,128)(2,1)S(1)} %broadcast_select_fusion), channel_id=1, source_target_pairs={{0,8},{8,0},{1,9},{9,1},{2,10},{10,2},{3,11},{11,3},{4,12},{12,4},... | collective-permute-start | bytes 1572872 | tf_op jit(solution)/shard_map/ppermute | solution.py:21
  29.4 1.6 %collective-permute-start.11 = (bf16[2048,128]{1,0:T(8,128)(2,1)S(1)}, bf16[2048,128]{1,0:T(8,128)(2,1)S(1)}, u32[]{:S(2)}, u32[]{:S(2)}) collective-permute-start(bf16[2048,128]{1,0:T(8,128)(2,1)S(1)} %pad_maximum_fusion.refs_2_), channel_id=1, source_target_pairs={{0,8},{8,0},{1,9},{9,1},{2,10},{10,2},{3,11},{11,3},{4,12},{12,4},... | collective-permute-start | bytes 1572872 | tf_op jit(solution)/shard_map/ppermute | solution.py:21
  31.0 2.5 %collective-permute-start.10 = (bf16[2048,128]{1,0:T(8,128)(2,1)S(1)}, bf16[2048,128]{1,0:T(8,128)(2,1)S(1)}, u32[]{:S(2)}, u32[]{:S(2)}) collective-permute-start(bf16[2048,128]{1,0:T(8,128)(2,1)S(1)} %collective-permute-done.3.refs_1_), channel_id=1, source_target_pairs={{0,8},{8,0},{1,9},{9,1},{2,10},{10,2},{3,11},{11,3},{4,12},{12,4},... | collective-permute-start | bytes 1572872 | tf_op jit(solution)/shard_map/ppermute | solution.py:21
  33.5 3.4 %collective-permute-start.12 = (bf16[2048,128]{1,0:T(8,128)(2,1)S(1)}, bf16[2048,128]{1,0:T(8,128)(2,1)S(1)}, u32[]{:S(2)}, u32[]{:S(2)}) collective-permute-start(bf16[2048,128]{1,0:T(8,128)(2,1)S(1)} %collective-permute-done.8.refs_3_), channel_id=1, source_target_pairs={{0,8},{8,0},{1,9},{9,1},{2,10},{10,2},{3,11},{11,3},{4,12},{12,4},... | collective-permute-start | bytes 1572872 | tf_op jit(solution)/shard_map/ppermute | solution.py:21
  36.9 1.5 %collective-permute-done.12.refs_7_ = bf16[2048,128]{1,0:T(8,128)(2,1)S(1)} collective-permute-done((bf16[2048,128]{1,0:T(8,128)(2,1)S(1)}, bf16[2048,128]{1,0:T(8,128)(2,1)S(1)}, u32[]{:S(2)}, u32[]{:S(2)}) %collective-permute-start.12) | collective-permute-done | bytes 524320 | tf_op jit(solution)/shard_map/ppermute | solution.py:21
  38.4 2.2 %far_rows.1 = (bf16[16384,128]{1,0:T(8,128)(2,1)S(1)}, f32[512,128]{1,0:T(8,128)S(1)}, bf16[512,128]{1,0:T(8,128)(2,1)S(1)}, bf16[512,128]{1,0:T(8,128)(2,1)S(1)}, bf16[512,128]{1,0:T(8,128)(2,1)S(1)}) custom-call(s32[8,256]{1,0:T(8,128)S(1)} %copy-done, bf16[256,128,128]{2,1,0:T(8,128)(2,1)S(1)} %get-tuple-element.19.vals_ref, ...), custom_call_target="tpu_custom_call" | custom-call | flops 536870912 | bytes 8388608 | tf_op jit(solution)/shard_map/far_rows/pallas_call | solution.py:166
  40.6 3.8 %collective-permute-start.13 = (bf16[512,128]{1,0:T(8,128)(2,1)S(1)}, bf16[512,128]{1,0:T(8,128)(2,1)S(1)}, u32[]{:S(2)}, u32[]{:S(2)}) collective-permute-start(bf16[512,128]{1,0:T(8,128)(2,1)S(1)} %get-tuple-element.25), channel_id=1, source_target_pairs={{0,4},{2,6},{4,0},{6,2},{1,5},{3,7},{5,1},{7,3},{8,12},{10,14},{12... | collective-permute-start | bytes 393224 | tf_op jit(solution)/shard_map/ppermute | solution.py:21
  44.4 2.7 %collective-permute-start.15 = (bf16[512,128]{1,0:T(8,128)(2,1)S(1)}, bf16[512,128]{1,0:T(8,128)(2,1)S(1)}, u32[]{:S(2)}, u32[]{:S(2)}) collective-permute-start(bf16[512,128]{1,0:T(8,128)(2,1)S(1)} %get-tuple-element.27), channel_id=1, source_target_pairs={{0,6},{2,0},{4,2},{6,4},{1,7},{3,1},{5,3},{7,5},{8,14},{10,8},{12,... | collective-permute-start | bytes 393224 | tf_op jit(solution)/shard_map/ppermute | solution.py:21
  47.1 2.0 %near_rows.1 = (f32[512,128]{1,0:T(8,128)S(1)}, bf16[512,128]{1,0:T(8,128)(2,1)S(1)}, bf16[512,128]{1,0:T(8,128)(2,1)S(1)}, bf16[512,128]{1,0:T(8,128)(2,1)S(1)}) custom-call(s32[8,256]{1,0:T(8,128)S(1)} %copy-done, bf16[256,128,128]{2,1,0:T(8,128)(2,1)S(1)} %get-tuple-element.19.vals_ref, bf16[16384,128]{1,0:T(8,128)(2,1)S(1)} %get-tuple-element.22.table_ref), custom_call_target="tpu_custom_call" | custom-call | flops 536870912 | bytes 8388608 | tf_op jit(solution)/shard_map/near_rows/pallas_call | solution.py:166
  49.5 2.7 %collective-permute-start.19 = (bf16[512,128]{1,0:T(8,128)(2,1)S(1)}, bf16[512,128]{1,0:T(8,128)(2,1)S(1)}, u32[]{:S(2)}, u32[]{:S(2)}) collective-permute-start(bf16[512,128]{1,0:T(8,128)(2,1)S(1)} %get-tuple-element.30), channel_id=1, source_target_pairs={{0,6},{2,0},{4,2},{6,4},{1,7},{3,1},{5,3},{7,5},{8,14},{10,8},{12,... | collective-permute-start | bytes 393224 | tf_op jit(solution)/shard_map/ppermute | solution.py:21
  52.8 2.4 %collective-permute-start.16 = (bf16[512,128]{1,0:T(8,128)(2,1)S(1)}, bf16[512,128]{1,0:T(8,128)(2,1)S(1)}, u32[]{:S(2)}, u32[]{:S(2)}) collective-permute-start(bf16[512,128]{1,0:T(8,128)(2,1)S(1)} %add_convert_fusion), channel_id=1, source_target_pairs={{0,1},{1,0},{2,3},{3,2},{4,5},{5,4},{6,7},{7,6},{8,9},{9,8},{10,11... | collective-permute-start | bytes 393224 | tf_op jit(solution)/shard_map/ppermute | solution.py:21
  55.2 3.7 %collective-permute-done.18.refs_4_ = bf16[512,128]{1,0:T(8,128)(2,1)S(1)} collective-permute-done((bf16[512,128]{1,0:T(8,128)(2,1)S(1)}, bf16[512,128]{1,0:T(8,128)(2,1)S(1)}, u32[]{:S(2)}, u32[]{:S(2)}) %collective-permute-start.18) | collective-permute-done | bytes 131104 | tf_op jit(solution)/shard_map/ppermute | solution.py:21
  58.9 5.9 %collective-permute-done.16.refs_2_ = bf16[512,128]{1,0:T(8,128)(2,1)S(1)} collective-permute-done((bf16[512,128]{1,0:T(8,128)(2,1)S(1)}, bf16[512,128]{1,0:T(8,128)(2,1)S(1)}, u32[]{:S(2)}, u32[]{:S(2)}) %collective-permute-start.16) | collective-permute-done | bytes 131104 | tf_op jit(solution)/shard_map/ppermute | solution.py:21
  67.6 2.7 %collective-permute-start.23 = (f32[88,128]{1,0:T(8,128)S(1)}, f32[88,128]{1,0:T(8,128)S(1)}, u32[]{:S(2)}, u32[]{:S(2)}) collective-permute-start(f32[88,128]{1,0:T(8,128)S(1)} %add.50), channel_id=1, source_target_pairs={{0,192},{64,0},{128,64},{192,128},{1,193},{65,1},{129,65},{193,129... | collective-permute-start | bytes 135176 | tf_op jit(solution)/shard_map/ppermute | solution.py:21
  70.3 1.7 %collective-permute-done.21 = f32[88,128]{1,0:T(8,128)S(1)} collective-permute-done((f32[88,128]{1,0:T(8,128)S(1)}, f32[88,128]{1,0:T(8,128)S(1)}, u32[]{:S(2)}, u32[]{:S(2)}) %collective-permute-start.21) | collective-permute-done | bytes 45088 | tf_op jit(solution)/shard_map/ppermute | solution.py:21
  73.2 2.3 %collective-permute-start.25 = (f32[88,128]{1,0:T(8,128)S(1)}, f32[88,128]{1,0:T(8,128)S(1)}, u32[]{:S(2)}, u32[]{:S(2)}) collective-permute-start(f32[88,128]{1,0:T(8,128)S(1)} %add_add_fusion.2), channel_id=1, source_target_pairs={{0,2},{2,4},{4,6},{6,0},{1,3},{3,5},{5,7},{7,1},{8,10},{10,12},{12... | collective-permute-start | bytes 135176 | tf_op jit(solution)/shard_map/ppermute | solution.py:21
  75.9 1.2 %collective-permute-done.24 = f32[88,128]{1,0:T(8,128)S(1)} collective-permute-done((f32[88,128]{1,0:T(8,128)S(1)}, f32[88,128]{1,0:T(8,128)S(1)}, u32[]{:S(2)}, u32[]{:S(2)}) %collective-permute-start.24) | collective-permute-done | bytes 45088 | tf_op jit(solution)/shard_map/ppermute | solution.py:21
  77.5 1.4 %collective-permute-done.26 = f32[88,128]{1,0:T(8,128)S(1)} collective-permute-done((f32[88,128]{1,0:T(8,128)S(1)}, f32[88,128]{1,0:T(8,128)S(1)}, u32[]{:S(2)}, u32[]{:S(2)}) %collective-permute-start.26) | collective-permute-done | bytes 45088 | tf_op jit(solution)/shard_map/ppermute | solution.py:21
  78.9 1.9 %collective-permute-start.27 = (f32[88,128]{1,0:T(8,128)S(1)}, f32[88,128]{1,0:T(8,128)S(1)}, u32[]{:S(2)}, u32[]{:S(2)}) collective-permute-start(f32[88,128]{1,0:T(8,128)S(1)} %add_add_fusion.1), channel_id=1, source_target_pairs={{0,1},{1,0},{2,3},{3,2},{4,5},{5,4},{6,7},{7,6},{8,9},{9,8},{10,11... | collective-permute-start | bytes 135176 | tf_op jit(solution)/shard_map/ppermute | solution.py:21
  80.8 5.1 %collective-permute-done.27 = f32[88,128]{1,0:T(8,128)S(1)} collective-permute-done((f32[88,128]{1,0:T(8,128)S(1)}, f32[88,128]{1,0:T(8,128)S(1)}, u32[]{:S(2)}, u32[]{:S(2)}) %collective-permute-start.27) | collective-permute-done | bytes 45088 | tf_op jit(solution)/shard_map/ppermute | solution.py:21
  86.0 1.3 %collective-permute-start.29 = (f32[88,128]{1,0:T(8,128)S(1)}, f32[88,128]{1,0:T(8,128)S(1)}, u32[]{:S(2)}, u32[]{:S(2)}) collective-permute-start(f32[88,128]{1,0:T(8,128)S(1)} %add.57), channel_id=1, source_target_pairs={{0,16},{16,32},{32,48},{48,1},{1,17},{17,33},{33,49},{49,0},{2,18}... | collective-permute-start | bytes 135176 | tf_op jit(solution)/shard_map/ppermute | solution.py:28
  87.2 1.5 %collective-permute-start.30 = (f32[88,128]{1,0:T(8,128)S(1)}, f32[88,128]{1,0:T(8,128)S(1)}, u32[]{:S(2)}, u32[]{:S(2)}) collective-permute-start(f32[88,128]{1,0:T(8,128)S(1)} %add.57), channel_id=1, source_target_pairs={{0,49},{16,0},{32,16},{48,32},{1,48},{17,1},{33,17},{49,33},{2,51}... | collective-permute-start | bytes 135176 | tf_op jit(solution)/shard_map/ppermute | solution.py:28
  88.7 2.7 %collective-permute-done.28 = f32[88,128]{1,0:T(8,128)S(1)} collective-permute-done((f32[88,128]{1,0:T(8,128)S(1)}, f32[88,128]{1,0:T(8,128)S(1)}, u32[]{:S(2)}, u32[]{:S(2)}) %collective-permute-start.28) | collective-permute-done | bytes 45088 | tf_op jit(solution)/shard_map/ppermute | solution.py:28
  91.5 4.6 %collective-permute-start.31 = (f32[88,128]{1,0:T(8,128)S(1)}, f32[88,128]{1,0:T(8,128)S(1)}, u32[]{:S(2)}, u32[]{:S(2)}) collective-permute-start(f32[88,128]{1,0:T(8,128)S(1)} %add_add_fusion), channel_id=1, source_target_pairs={{0,8},{8,0},{1,9},{9,1},{2,10},{10,2},{3,11},{11,3},{4,12},{12,4},... | collective-permute-start | bytes 135176 | tf_op jit(solution)/shard_map/ppermute | solution.py:21
  (60 shorter events, 10.9 us)
Async XLA Ops:
  0.6 12.3 %collective-permute-start.2 = (bf16[512,128]{1,0:T(8,128)(2,1)}, bf16[512,128]{1,0:T(8,128)(2,1)S(1)}, u32[]{:S(2)}, u32[]{:S(2)}) collective-permute-start(bf16[512,128]{1,0:T(8,128)(2,1)} %param.7), channel_id=1, source_target_pairs={{0,16},{16,32},{32,48},{48,0},{1,17},{17,33},{33,49},{49,1},{2,18}... | collective-permute-start | bytes 393224 | tf_op jit(solution)/shard_map/ppermute | solution.py:21
  3.2 10.2 %collective-permute-start = (bf16[512,128]{1,0:T(8,128)(2,1)}, bf16[512,128]{1,0:T(8,128)(2,1)S(1)}, u32[]{:S(2)}, u32[]{:S(2)}) collective-permute-start(bf16[512,128]{1,0:T(8,128)(2,1)} %param.7), channel_id=1, source_target_pairs={{0,48},{16,0},{32,16},{48,32},{1,49},{17,1},{33,17},{49,33},{2,50}... | collective-permute-start | bytes 393224 | tf_op jit(solution)/shard_map/ppermute | solution.py:21
  6.0 9.2 %collective-permute-start.4 = (bf16[512,128]{1,0:T(8,128)(2,1)}, bf16[512,128]{1,0:T(8,128)(2,1)S(1)}, u32[]{:S(2)}, u32[]{:S(2)}) collective-permute-start(bf16[512,128]{1,0:T(8,128)(2,1)} %param.7), channel_id=1, source_target_pairs={{0,128},{64,192},{128,0},{192,64},{1,129},{65,193},{129,1},{193,65... | collective-permute-start | bytes 393224 | tf_op jit(solution)/shard_map/ppermute | solution.py:21
  8.9 10.1 %collective-permute-start.1 = (bf16[512,128]{1,0:T(8,128)(2,1)}, bf16[512,128]{1,0:T(8,128)(2,1)S(1)}, u32[]{:S(2)}, u32[]{:S(2)}) collective-permute-start(bf16[512,128]{1,0:T(8,128)(2,1)} %param.7), channel_id=1, source_target_pairs={{0,32},{16,48},{32,0},{48,16},{1,33},{17,49},{33,1},{49,17},{2,34}... | collective-permute-start | bytes 393224 | tf_op jit(solution)/shard_map/ppermute | solution.py:21
  15.2 10.6 %collective-permute-start.5 = (bf16[512,128]{1,0:T(8,128)(2,1)S(1)}, bf16[512,128]{1,0:T(8,128)(2,1)S(1)}, u32[]{:S(2)}, u32[]{:S(2)}) collective-permute-start(bf16[512,128]{1,0:T(8,128)(2,1)S(1)} %get-tuple-element.34), channel_id=1, source_target_pairs={{0,48},{16,0},{32,16},{48,32},{1,49},{17,1},{33,17},{49,33},{2,50}... | collective-permute-start | bytes 393224 | tf_op jit(solution)/shard_map/ppermute | solution.py:21
  16.5 12.9 %collective-permute-start.6 = (bf16[512,128]{1,0:T(8,128)(2,1)S(1)}, bf16[512,128]{1,0:T(8,128)(2,1)S(1)}, u32[]{:S(2)}, u32[]{:S(2)}) collective-permute-start(bf16[512,128]{1,0:T(8,128)(2,1)S(1)} %get-tuple-element.34), channel_id=1, source_target_pairs={{0,16},{16,32},{32,48},{48,0},{1,17},{17,33},{33,49},{49,1},{2,18}... | collective-permute-start | bytes 393224 | tf_op jit(solution)/shard_map/ppermute | solution.py:21
  16.9 12.5 %collective-permute-start.7 = (bf16[512,128]{1,0:T(8,128)(2,1)S(1)}, bf16[512,128]{1,0:T(8,128)(2,1)S(1)}, u32[]{:S(2)}, u32[]{:S(2)}) collective-permute-start(bf16[512,128]{1,0:T(8,128)(2,1)S(1)} %get-tuple-element.34), channel_id=1, source_target_pairs={{0,32},{16,48},{32,0},{48,16},{1,33},{17,49},{33,1},{49,17},{2,34}... | collective-permute-start | bytes 393224 | tf_op jit(solution)/shard_map/ppermute | solution.py:21
  19.0 12.0 %collective-permute-start.3 = (bf16[2048,128]{1,0:T(8,128)(2,1)S(1)}, bf16[2048,128]{1,0:T(8,128)(2,1)S(1)}, u32[]{:S(2)}, u32[]{:S(2)}) collective-permute-start(bf16[2048,128]{1,0:T(8,128)(2,1)S(1)} %constant_dynamic-update-slice_fusion._.refs_0_), channel_id=1, source_target_pairs={{0,192},{64,0},{128,64},{192,128},{1,193},{65,1},{129,65},{193,129... | collective-permute-start | bytes 1572872 | tf_op jit(solution)/shard_map/ppermute | solution.py:21
  21.3 12.1 %collective-permute-start.8 = (bf16[2048,128]{1,0:T(8,128)(2,1)S(1)}, bf16[2048,128]{1,0:T(8,128)(2,1)S(1)}, u32[]{:S(2)}, u32[]{:S(2)}) collective-permute-start(bf16[2048,128]{1,0:T(8,128)(2,1)S(1)} %constant_dynamic-update-slice_fusion._.refs_0_), channel_id=1, source_target_pairs={{0,64},{64,128},{128,192},{192,0},{1,65},{65,129},{129,193},{193,1... | collective-permute-start | bytes 1572872 | tf_op jit(solution)/shard_map/ppermute | solution.py:21
  25.9 11.0 %collective-permute-start.9 = (bf16[2048,128]{1,0:T(8,128)(2,1)S(1)}, bf16[2048,128]{1,0:T(8,128)(2,1)S(1)}, u32[]{:S(2)}, u32[]{:S(2)}) collective-permute-start(bf16[2048,128]{1,0:T(8,128)(2,1)S(1)} %broadcast_select_fusion), channel_id=1, source_target_pairs={{0,8},{8,0},{1,9},{9,1},{2,10},{10,2},{3,11},{11,3},{4,12},{12,4},... | collective-permute-start | bytes 1572872 | tf_op jit(solution)/shard_map/ppermute | solution.py:21
  29.4 7.5 %collective-permute-start.11 = (bf16[2048,128]{1,0:T(8,128)(2,1)S(1)}, bf16[2048,128]{1,0:T(8,128)(2,1)S(1)}, u32[]{:S(2)}, u32[]{:S(2)}) collective-permute-start(bf16[2048,128]{1,0:T(8,128)(2,1)S(1)} %pad_maximum_fusion.refs_2_), channel_id=1, source_target_pairs={{0,8},{8,0},{1,9},{9,1},{2,10},{10,2},{3,11},{11,3},{4,12},{12,4},... | collective-permute-start | bytes 1572872 | tf_op jit(solution)/shard_map/ppermute | solution.py:21
  31.0 5.9 %collective-permute-start.10 = (bf16[2048,128]{1,0:T(8,128)(2,1)S(1)}, bf16[2048,128]{1,0:T(8,128)(2,1)S(1)}, u32[]{:S(2)}, u32[]{:S(2)}) collective-permute-start(bf16[2048,128]{1,0:T(8,128)(2,1)S(1)} %collective-permute-done.3.refs_1_), channel_id=1, source_target_pairs={{0,8},{8,0},{1,9},{9,1},{2,10},{10,2},{3,11},{11,3},{4,12},{12,4},... | collective-permute-start | bytes 1572872 | tf_op jit(solution)/shard_map/ppermute | solution.py:21
  33.5 4.9 %collective-permute-start.12 = (bf16[2048,128]{1,0:T(8,128)(2,1)S(1)}, bf16[2048,128]{1,0:T(8,128)(2,1)S(1)}, u32[]{:S(2)}, u32[]{:S(2)}) collective-permute-start(bf16[2048,128]{1,0:T(8,128)(2,1)S(1)} %collective-permute-done.8.refs_3_), channel_id=1, source_target_pairs={{0,8},{8,0},{1,9},{9,1},{2,10},{10,2},{3,11},{11,3},{4,12},{12,4},... | collective-permute-start | bytes 1572872 | tf_op jit(solution)/shard_map/ppermute | solution.py:21
  40.6 8.9 %collective-permute-start.13 = (bf16[512,128]{1,0:T(8,128)(2,1)S(1)}, bf16[512,128]{1,0:T(8,128)(2,1)S(1)}, u32[]{:S(2)}, u32[]{:S(2)}) collective-permute-start(bf16[512,128]{1,0:T(8,128)(2,1)S(1)} %get-tuple-element.25), channel_id=1, source_target_pairs={{0,4},{2,6},{4,0},{6,2},{1,5},{3,7},{5,1},{7,3},{8,12},{10,14},{12... | collective-permute-start | bytes 393224 | tf_op jit(solution)/shard_map/ppermute | solution.py:21
  44.4 7.8 %collective-permute-start.14 = (bf16[512,128]{1,0:T(8,128)(2,1)S(1)}, bf16[512,128]{1,0:T(8,128)(2,1)S(1)}, u32[]{:S(2)}, u32[]{:S(2)}) collective-permute-start(bf16[512,128]{1,0:T(8,128)(2,1)S(1)} %get-tuple-element.26), channel_id=1, source_target_pairs={{0,2},{2,4},{4,6},{6,0},{1,3},{3,5},{5,7},{7,1},{8,10},{10,12},{12... | collective-permute-start | bytes 393224 | tf_op jit(solution)/shard_map/ppermute | solution.py:21
  44.4 8.3 %collective-permute-start.15 = (bf16[512,128]{1,0:T(8,128)(2,1)S(1)}, bf16[512,128]{1,0:T(8,128)(2,1)S(1)}, u32[]{:S(2)}, u32[]{:S(2)}) collective-permute-start(bf16[512,128]{1,0:T(8,128)(2,1)S(1)} %get-tuple-element.27), channel_id=1, source_target_pairs={{0,6},{2,0},{4,2},{6,4},{1,7},{3,1},{5,3},{7,5},{8,14},{10,8},{12,... | collective-permute-start | bytes 393224 | tf_op jit(solution)/shard_map/ppermute | solution.py:21
  49.1 6.2 %collective-permute-start.17 = (bf16[512,128]{1,0:T(8,128)(2,1)S(1)}, bf16[512,128]{1,0:T(8,128)(2,1)S(1)}, u32[]{:S(2)}, u32[]{:S(2)}) collective-permute-start(bf16[512,128]{1,0:T(8,128)(2,1)S(1)} %get-tuple-element.28), channel_id=1, source_target_pairs={{0,4},{2,6},{4,0},{6,2},{1,5},{3,7},{5,1},{7,3},{8,12},{10,14},{12... | collective-permute-start | bytes 393224 | tf_op jit(solution)/shard_map/ppermute | solution.py:21
  49.5 9.4 %collective-permute-start.18 = (bf16[512,128]{1,0:T(8,128)(2,1)S(1)}, bf16[512,128]{1,0:T(8,128)(2,1)S(1)}, u32[]{:S(2)}, u32[]{:S(2)}) collective-permute-start(bf16[512,128]{1,0:T(8,128)(2,1)S(1)} %get-tuple-element.29), channel_id=1, source_target_pairs={{0,2},{2,4},{4,6},{6,0},{1,3},{3,5},{5,7},{7,1},{8,10},{10,12},{12... | collective-permute-start | bytes 393224 | tf_op jit(solution)/shard_map/ppermute | solution.py:21
  49.5 9.4 %collective-permute-start.19 = (bf16[512,128]{1,0:T(8,128)(2,1)S(1)}, bf16[512,128]{1,0:T(8,128)(2,1)S(1)}, u32[]{:S(2)}, u32[]{:S(2)}) collective-permute-start(bf16[512,128]{1,0:T(8,128)(2,1)S(1)} %get-tuple-element.30), channel_id=1, source_target_pairs={{0,6},{2,0},{4,2},{6,4},{1,7},{3,1},{5,3},{7,5},{8,14},{10,8},{12,... | collective-permute-start | bytes 393224 | tf_op jit(solution)/shard_map/ppermute | solution.py:21
  52.8 12.1 %collective-permute-start.16 = (bf16[512,128]{1,0:T(8,128)(2,1)S(1)}, bf16[512,128]{1,0:T(8,128)(2,1)S(1)}, u32[]{:S(2)}, u32[]{:S(2)}) collective-permute-start(bf16[512,128]{1,0:T(8,128)(2,1)S(1)} %add_convert_fusion), channel_id=1, source_target_pairs={{0,1},{1,0},{2,3},{3,2},{4,5},{5,4},{6,7},{7,6},{8,9},{9,8},{10,11... | collective-permute-start | bytes 393224 | tf_op jit(solution)/shard_map/ppermute | solution.py:21
  65.9 1.5 %collective-permute-start.20 = (f32[88,128]{1,0:T(8,128)S(1)}, f32[88,128]{1,0:T(8,128)S(1)}, u32[]{:S(2)}, u32[]{:S(2)}) collective-permute-start(f32[88,128]{1,0:T(8,128)S(1)} %get-tuple-element.33), channel_id=1, source_target_pairs={{0,8},{8,0},{1,9},{9,1},{2,10},{10,2},{3,11},{11,3},{4,12},{12,4},... | collective-permute-start | bytes 135176 | tf_op jit(solution)/shard_map/ppermute | solution.py:21
  67.5 4.5 %collective-permute-start.21 = (f32[88,128]{1,0:T(8,128)S(1)}, f32[88,128]{1,0:T(8,128)S(1)}, u32[]{:S(2)}, u32[]{:S(2)}) collective-permute-start(f32[88,128]{1,0:T(8,128)S(1)} %add.50), channel_id=1, source_target_pairs={{0,128},{64,192},{128,0},{192,64},{1,129},{65,193},{129,1},{193,65... | collective-permute-start | bytes 135176 | tf_op jit(solution)/shard_map/ppermute | solution.py:21
  67.5 5.0 %collective-permute-start.22 = (f32[88,128]{1,0:T(8,128)S(1)}, f32[88,128]{1,0:T(8,128)S(1)}, u32[]{:S(2)}, u32[]{:S(2)}) collective-permute-start(f32[88,128]{1,0:T(8,128)S(1)} %add.50), channel_id=1, source_target_pairs={{0,64},{64,128},{128,192},{192,0},{1,65},{65,129},{129,193},{193,1... | collective-permute-start | bytes 135176 | tf_op jit(solution)/shard_map/ppermute | solution.py:21
  67.6 5.0 %collective-permute-start.23 = (f32[88,128]{1,0:T(8,128)S(1)}, f32[88,128]{1,0:T(8,128)S(1)}, u32[]{:S(2)}, u32[]{:S(2)}) collective-permute-start(f32[88,128]{1,0:T(8,128)S(1)} %add.50), channel_id=1, source_target_pairs={{0,192},{64,0},{128,64},{192,128},{1,193},{65,1},{129,65},{193,129... | collective-permute-start | bytes 135176 | tf_op jit(solution)/shard_map/ppermute | solution.py:21
  72.6 4.5 %collective-permute-start.24 = (f32[88,128]{1,0:T(8,128)S(1)}, f32[88,128]{1,0:T(8,128)S(1)}, u32[]{:S(2)}, u32[]{:S(2)}) collective-permute-start(f32[88,128]{1,0:T(8,128)S(1)} %add_add_fusion.2), channel_id=1, source_target_pairs={{0,4},{2,6},{4,0},{6,2},{1,5},{3,7},{5,1},{7,3},{8,12},{10,14},{12... | collective-permute-start | bytes 135176 | tf_op jit(solution)/shard_map/ppermute | solution.py:21
  73.2 4.3 %collective-permute-start.25 = (f32[88,128]{1,0:T(8,128)S(1)}, f32[88,128]{1,0:T(8,128)S(1)}, u32[]{:S(2)}, u32[]{:S(2)}) collective-permute-start(f32[88,128]{1,0:T(8,128)S(1)} %add_add_fusion.2), channel_id=1, source_target_pairs={{0,2},{2,4},{4,6},{6,0},{1,3},{3,5},{5,7},{7,1},{8,10},{10,12},{12... | collective-permute-start | bytes 135176 | tf_op jit(solution)/shard_map/ppermute | solution.py:21
  75.5 3.4 %collective-permute-start.26 = (f32[88,128]{1,0:T(8,128)S(1)}, f32[88,128]{1,0:T(8,128)S(1)}, u32[]{:S(2)}, u32[]{:S(2)}) collective-permute-start(f32[88,128]{1,0:T(8,128)S(1)} %add_add_fusion.2), channel_id=1, source_target_pairs={{0,6},{2,0},{4,2},{6,4},{1,7},{3,1},{5,3},{7,5},{8,14},{10,8},{12,... | collective-permute-start | bytes 135176 | tf_op jit(solution)/shard_map/ppermute | solution.py:21
  78.9 6.9 %collective-permute-start.27 = (f32[88,128]{1,0:T(8,128)S(1)}, f32[88,128]{1,0:T(8,128)S(1)}, u32[]{:S(2)}, u32[]{:S(2)}) collective-permute-start(f32[88,128]{1,0:T(8,128)S(1)} %add_add_fusion.1), channel_id=1, source_target_pairs={{0,1},{1,0},{2,3},{3,2},{4,5},{5,4},{6,7},{7,6},{8,9},{9,8},{10,11... | collective-permute-start | bytes 135176 | tf_op jit(solution)/shard_map/ppermute | solution.py:21
  85.9 5.6 %collective-permute-start.28 = (f32[88,128]{1,0:T(8,128)S(1)}, f32[88,128]{1,0:T(8,128)S(1)}, u32[]{:S(2)}, u32[]{:S(2)}) collective-permute-start(f32[88,128]{1,0:T(8,128)S(1)} %add.57), channel_id=1, source_target_pairs={{0,32},{16,48},{32,1},{48,17},{1,33},{17,49},{33,0},{49,16},{2,34}... | collective-permute-start | bytes 135176 | tf_op jit(solution)/shard_map/ppermute | solution.py:28
  86.0 5.5 %collective-permute-start.29 = (f32[88,128]{1,0:T(8,128)S(1)}, f32[88,128]{1,0:T(8,128)S(1)}, u32[]{:S(2)}, u32[]{:S(2)}) collective-permute-start(f32[88,128]{1,0:T(8,128)S(1)} %add.57), channel_id=1, source_target_pairs={{0,16},{16,32},{32,48},{48,1},{1,17},{17,33},{33,49},{49,0},{2,18}... | collective-permute-start | bytes 135176 | tf_op jit(solution)/shard_map/ppermute | solution.py:28
  87.2 4.2 %collective-permute-start.30 = (f32[88,128]{1,0:T(8,128)S(1)}, f32[88,128]{1,0:T(8,128)S(1)}, u32[]{:S(2)}, u32[]{:S(2)}) collective-permute-start(f32[88,128]{1,0:T(8,128)S(1)} %add.57), channel_id=1, source_target_pairs={{0,49},{16,0},{32,16},{48,32},{1,48},{17,1},{33,17},{49,33},{2,51}... | collective-permute-start | bytes 135176 | tf_op jit(solution)/shard_map/ppermute | solution.py:28
  91.5 5.5 %collective-permute-start.31 = (f32[88,128]{1,0:T(8,128)S(1)}, f32[88,128]{1,0:T(8,128)S(1)}, u32[]{:S(2)}, u32[]{:S(2)}) collective-permute-start(f32[88,128]{1,0:T(8,128)S(1)} %add_add_fusion), channel_id=1, source_target_pairs={{0,8},{8,0},{1,9},{9,1},{2,10},{10,2},{3,11},{11,3},{4,12},{12,4},... | collective-permute-start | bytes 135176 | tf_op jit(solution)/shard_map/ppermute | solution.py:21
  (3 other events, 49.2 us)
